TPU v7x, 512 devices: a whole 4x8x8 slice. The times are simulated.
512 devices in a mesh: pool: 2 (over core), dev: 64 (over y, z), rep: 4 (over x).
Axes of the slice: x: 4, y: 8, z: 8, core: 2. Of those that a mesh axis runs over, the one named last changes fastest.
Arguments:
- moe_rows: bfloat16 [4096, 4096], P(('rep', 'dev')), parts along dimension 0, may hold values from -6 to 6
- routes: int32 [4096, 8], P(('rep', 'dev')), parts along dimension 0, may hold values from 0 to 15, all different within a row; in each aligned block of 16 rows (0 to 15, 16 to 31, ...) at most 12 rows name the same one
- gate_values: float32 [4096, 8], P(('rep', 'dev')), parts along dimension 0, may hold values from 0.02 to 0.3
- gate_weight: bfloat16 [64, 4096, 256], P('dev', None, 'pool'), may hold values from -0.09375 to 0.09375
- up_weight: bfloat16 [64, 4096, 256], P('dev', None, 'pool'), may hold values from -0.09375 to 0.09375
- down_weight: bfloat16 [64, 256, 4096], P('dev', 'pool'), may hold values from -0.1875 to 0.1875
Outputs:
- expert_out: bfloat16 [4096, 4096], P(('rep', 'dev')), parts along dimension 0
There are 4 independent parts, one for each index of `rep`. A program takes and returns all parts, laid end to end along the dimension named above; an argument that names none is the same for every part. Nothing has to cross between parts.
Inputs may be any that keep to these rules, and one draw needn't show every extreme that they name: `routes`: each row names 8 different experts. Among the rows of one device no expert is named by more than 12 rows, and in every draw some device's rows name some expert exactly 12 times.
All inputs are finite; a program needn't handle non-finite values.
Results may differ from a plain program's by a relative error of at most 0.0057.
Values may be sent and summed in bfloat16 or wider, within the bound.
No kernel may reach another device: no remote copies, remote signals or barrier semaphores. Data moves between devices by JAX's collectives and lax.ppermute only.
A program may use at most 128 MiB of HBM per device.

v0:
```python
import jax
import jax.numpy as jnp
from jax import lax
from jax.sharding import PartitionSpec as P

EXPERTS = 16
TOPK = 8
CAP = 12


def body(moe_rows, routes, gate_values, gate_weight, up_weight, down_weight):
    device_count = lax.axis_size("dev")
    split_count = max(1, device_count // EXPERTS)
    per_device = gate_weight.shape[0]
    row_count = moe_rows.shape[0]
    width = moe_rows.shape[1]
    expert_ids = jnp.arange(EXPERTS, dtype=jnp.int32)
    chosen = routes[:, :, None] == expert_ids[None, None, :]
    member = jnp.sum(chosen.astype(jnp.int32), axis=1)
    earlier = jnp.cumsum(member, axis=0) - member
    slot_ids = jnp.arange(CAP, dtype=jnp.int32)
    placed = (member.T[:, None, :] == 1) & (earlier.T[:, None, :] == slot_ids[None, :, None])
    placed_pieces = jnp.repeat(placed, split_count, axis=0).reshape(
        device_count, per_device, CAP, row_count
    )
    outgoing = jnp.einsum(
        "jqcr,rd->jqcd",
        placed_pieces.astype(jnp.bfloat16),
        moe_rows,
        preferred_element_type=jnp.float32,
    ).astype(jnp.bfloat16)
    arrived = lax.all_to_all(outgoing, "dev", split_axis=0, concat_axis=0, tiled=True)
    gate_act = jnp.einsum(
        "spcd,pdh->spch", arrived, gate_weight, preferred_element_type=jnp.float32
    )
    up_act = jnp.einsum("spcd,pdh->spch", arrived, up_weight, preferred_element_type=jnp.float32)
    act = (jax.nn.silu(gate_act) * up_act).astype(jnp.bfloat16)
    partial_out = jnp.einsum("spch,phd->spcd", act, down_weight, preferred_element_type=jnp.float32)
    results = partial_out.astype(jnp.bfloat16)
    returned_rows = lax.all_to_all(results, "dev", split_axis=0, concat_axis=0, tiled=True)
    flat_rows = returned_rows.reshape(-1, width)
    slot_of = jnp.take_along_axis(earlier, routes, axis=1)
    split_ids = jnp.arange(split_count, dtype=jnp.int32)
    flat_index = (routes[:, :, None] * split_count + split_ids[None, None, :]) * CAP + slot_of[
        :, :, None
    ]
    local_total = jnp.zeros((row_count, width), jnp.float32)
    for choice_slot in range(TOPK):
        picked = jnp.take(flat_rows, flat_index[:, choice_slot, :], axis=0).astype(jnp.float32)
        local_total = local_total + gate_values[:, choice_slot, None] * jnp.sum(picked, axis=1)
    expert_out = lax.psum(local_total, "pool").astype(jnp.bfloat16)
    return expert_out


def solution(mesh):
    return jax.shard_map(
        body,
        mesh=mesh,
        in_specs=(
            P(("rep", "dev"), None),
            P(("rep", "dev"), None),
            P(("rep", "dev"), None),
            P("dev", None, "pool"),
            P("dev", None, "pool"),
            P("dev", "pool", None),
        ),
        out_specs=P(("rep", "dev"), None),
        check_vma=False,
    )
```

profile of v0, /device:TPU:243, one launch (start us, length us, event | category | flops | bytes accessed | tf_op | source)
XLA Modules:
  0.0 665.4 jit_solution(16986120736321898907)
XLA Ops:
  0.0 0.8 copy.74
  0.8 0.1 convert_reduce_fusion.8
  1.2 0.1 broadcast_in_dim.12
  1.3 2.7 fusion.4
  4.0 6.8 %copy.81 = bf16[64,1,12,4096]{3,2,1,0:T(8,128)(2,1)} copy(bf16[64,1,12,4096]{3,0,2,1:T(8,128)(2,1)S(1)} %fusion.4) | data formatting | bytes 12582912 | tf_op jit(solution)/shard_map/convert_element_type | solution.py:31
  10.7 229.1 %all_to_all.10 = bf16[64,1,12,4096]{3,2,1,0:T(8,128)(2,1)S(1)} all-to-all(bf16[64,1,12,4096]{3,2,1,0:T(8,128)(2,1)} %copy.81), channel_id=1, replica_groups=mesh['pool'=2,'dev'=64,'rep'=4] {'dev'}, dimensions={0} | all-to-all | bytes 12582912 | tf_op jit(solution)/shard_map/all_to_all | solution.py:32
  239.8 3.2 copy-done.2
  243.1 6.7 %fusion.8 = f32[64,1,12,128]{3,0,2,1:T(8,128)S(1)} fusion(bf16[64,1,12,4096]{3,2,1,0:T(8,128)(2,1)S(1)} %all_to_all.10, bf16[1,4096,128]{2,1,0:T(8,128)(2,1)S(1)} %copy-done.6), kind=kOutput, calls=%fused_computation.19 | convolution fusion | flops 805306368 | bytes 7733248 | tf_op jit(solution)/shard_map/spcd,pdh->spch/dot_general | solution.py:33
  249.8 13.0 %fusion.5 = bf16[64,1,12,4096]{3,0,2,1:T(8,128)(2,1)} fusion(bf16[1,128,4096]{2,1,0:T(8,128)(2,1)S(1)} %copy-done, bf16[64,1,12,4096]{3,2,1,0:T(8,128)(2,1)} %copy-done.2, bf16[1,4096,128]{2,1,0:T(8,128)(2,1)S(1)} %copy-done.3, f32[64,1,12,128]{3,0,2,1:T(8,128)S(1)} %fusion.8), kind=kOutput, calls=%fused_computation.16 | convolution fusion | flops 1614348288 | bytes 15073280 | tf_op jit(solution)/shard_map/spch,phd->spcd/dot_general | solution.py:38
  262.7 9.6 %copy.83 = bf16[64,1,12,4096]{3,2,1,0:T(8,128)(2,1)} copy(bf16[64,1,12,4096]{3,0,2,1:T(8,128)(2,1)} %fusion.5) | data formatting | bytes 12582912 | tf_op jit(solution)/shard_map/convert_element_type | solution.py:39
  272.3 17.9 %all-to-all-start.1 = ((bf16[64,1,12,4096]{3,2,1,0:T(8,128)(2,1)}), bf16[64,1,12,4096]{3,2,1,0:T(8,128)(2,1)}, u32[]{:S(2)}, u32[]{:S(2)}) async-start(bf16[64,1,12,4096]{3,2,1,0:T(8,128)(2,1)} %copy.83), calls=%async_computation.1 | async-start | bytes 16777216 | tf_op jit(solution)/shard_map/all_to_all | solution.py:40
  290.4 1.3 gather_fusion
  292.2 0.1 reshape.154
  292.3 0.1 copy.77
  292.4 0.1 copy.85
  292.7 0.1 reshape.162
  292.8 0.1 copy.87
  292.9 0.1 copy.89
  293.1 0.1 reshape.166
  293.4 0.1 copy.91
  293.5 0.1 copy.93
  293.7 0.1 reshape.174
  293.9 0.1 copy.95
  294.0 0.1 copy.97
  294.2 293.9 %all-to-all-done.1 = bf16[64,1,12,4096]{3,2,1,0:T(8,128)(2,1)} async-done(((bf16[64,1,12,4096]{3,2,1,0:T(8,128)(2,1)}), bf16[64,1,12,4096]{3,2,1,0:T(8,128)(2,1)}, u32[]{:S(2)}, u32[]{:S(2)}) %all-to-all-start.1) | async-done | bytes 6291488 | tf_op jit(solution)/shard_map/all_to_all | solution.py:40
  588.2 10.2 %reshape.57 = bf16[768,4096]{1,0:T(8,128)(2,1)} reshape(bf16[64,1,12,4096]{3,2,1,0:T(8,128)(2,1)} %all-to-all-done.1) | data formatting | bytes 12582912 | tf_op jit(solution)/shard_map/reshape | solution.py:41
  598.4 5.0 gather_fusion.1
  603.4 0.2 reshape.153
  603.6 5.0 gather_fusion.2
  608.6 0.2 reshape.157
  608.8 5.0 gather_fusion.3
  613.7 0.2 reshape.161
  613.9 5.0 gather_fusion.4
  618.9 1.0 reshape.165
  619.9 5.0 gather_fusion.5
  624.9 0.2 reshape.169
  625.1 5.0 gather_fusion.6
  630.1 1.0 reshape.173
  631.1 5.9 gather_fusion.7
  637.0 2.1 reshape.177
  639.1 5.8 gather_fusion.8
  644.9 2.0 reshape.181
  646.9 1.7 convert_reduce_fusion.6
  648.6 2.7 convert_reduce_fusion.4
  651.4 2.7 convert_reduce_fusion.2
  654.1 2.9 convert_reduce_fusion
  657.0 0.2 multiply_add_fusion
  657.2 7.9 %all-reduce.1 = bf16[16,4096]{1,0:T(8,128)(2,1)} all-reduce(f32[16,4096]{1,0:T(8,128)S(1)} %multiply_add_fusion), channel_id=1, replica_groups=mesh['pool'=2,'dev'=64,'rep'=4] {'pool'}, use_global_device_ids=true, to_apply=%region_10.12 | all-reduce | flops 65536 | bytes 393216 | tf_op jit(solution)/shard_map/psum | solution.py:51
  (49 shorter events, 1.7 us)
Async XLA Ops:
  0.0 249.7 %copy-start = (bf16[1,128,4096]{2,1,0:T(8,128)(2,1)S(1)}, bf16[1,128,4096]{2,1,0:T(8,128)(2,1)}, u32[]{:S(2)}) copy-start(bf16[1,128,4096]{2,1,0:T(8,128)(2,1)} %param.13) | copy-start | bytes 3145732
  10.7 232.3 %copy-start.6 = (bf16[1,4096,128]{2,1,0:T(8,128)(2,1)S(1)}, bf16[1,4096,128]{2,1,0:T(8,128)(2,1)}, u32[]{:S(2)}) copy-start(bf16[1,4096,128]{2,1,0:T(8,128)(2,1)} %param.11) | copy-start | bytes 3145732
  239.8 3.2 copy-start.2
  243.0 6.7 %copy-start.3 = (bf16[1,4096,128]{2,1,0:T(8,128)(2,1)S(1)}, bf16[1,4096,128]{2,1,0:T(8,128)(2,1)}, u32[]{:S(2)}) copy-start(bf16[1,4096,128]{2,1,0:T(8,128)(2,1)} %param.12) | copy-start | bytes 3145732
  272.3 17.9 %copy-start.4 = (s32[16,8]{0,1:T(8,128)S(1)}, s32[16,8]{0,1:T(8,128)}, u32[]{:S(2)}) copy-start(s32[16,8]{0,1:T(8,128)} %param.9) | copy-start | bytes 1540
  272.3 315.8 %all-to-all-start.1 = ((bf16[64,1,12,4096]{3,2,1,0:T(8,128)(2,1)}), bf16[64,1,12,4096]{3,2,1,0:T(8,128)(2,1)}, u32[]{:S(2)}, u32[]{:S(2)}) async-start(bf16[64,1,12,4096]{3,2,1,0:T(8,128)(2,1)} %copy.83), calls=%async_computation.1 | async-start | bytes 16777216 | tf_op jit(solution)/shard_map/all_to_all | solution.py:40
  290.2 4.0 copy-start.5
  637.0 28.2 %copy-start.1 = (bf16[1,128,4096]{2,1,0:T(8,128)(2,1)S(1)}, bf16[1,128,4096]{2,1,0:T(8,128)(2,1)}, u32[]{:S(2)}) copy-start(bf16[1,128,4096]{2,1,0:T(8,128)(2,1)} %param.13) | copy-start | bytes 3145732
where the time goes:
time: 671 us; the launch traced here: 665 us
  waiting for transfers between devices  294 us (44%)
  blocking collectives  237 us (35%)
  local copies, waits for them, and re-layouts  83.2 us (12%)
  matrix products  22.3 us (3%)
  starting transfers between devices  17.9 us (3%)
  other arithmetic  10.5 us (2%)
    all_to_all x1, waiting for transfers between devices, body(): lax.all_to_all(results, 'dev', split_axis=0, concat_axis=0, tiled=True)  294 us
    all_to_all x1, blocking collectives, body(): lax.all_to_all(outgoing, 'dev', split_axis=0, concat_axis=0, tiled=True)  229 us
    gather x16, local copies, waits for them, and re-layouts, body(): jnp.take(flat_rows, flat_index[:, choice_slot, :], axis=0)  48.4 us
    all_to_all x1, starting transfers between devices, body(): lax.all_to_all(results, 'dev', split_axis=0, concat_axis=0, tiled=True)  17.9 us
  transfers between devices with their start and end apart: 1, of which 1 were waited for; matrix products, arithmetic and copies ran while one was open for 1% of the time, Pallas kernels for 0%

commit v1 on v0

v1 whole, which is shorter than its diff:
```python
import jax
import jax.numpy as jnp
from jax import lax
from jax.sharding import PartitionSpec as P

EXPERTS = 16
SIDE = 8
AXES = ("pool", "dev")
PAD = 128


def line_groups(side):
    along_z = [[y * side + z for z in range(side)] for y in range(side)]
    along_y = [[y * side + z for y in range(side)] for z in range(side)]
    shift = side * side
    first = along_z + [[shift + i for i in group] for group in along_y]
    second = along_y + [[shift + i for i in group] for group in along_z]
    return first, second


def body(moe_rows, routes, gate_values, gate_weight, up_weight, down_weight):
    device_count = lax.axis_size("dev")
    first, second = line_groups(SIDE)
    pool = lax.axis_index("pool")
    expert = lax.axis_index("dev") * EXPERTS // device_count
    row_count, width = moe_rows.shape
    half = row_count // 2

    expert_ids = jnp.arange(EXPERTS, dtype=jnp.int32)
    chosen = routes[:, :, None] == expert_ids[None, None, :]
    weight = jnp.sum(jnp.where(chosen, gate_values[:, :, None], 0.0), axis=1)
    high = lax.reduce_precision(weight, 8, 7)
    middle = lax.reduce_precision(weight - high, 8, 7)
    low = weight - high - middle
    terms = jnp.concatenate([high, middle, low], axis=1).astype(jnp.bfloat16)
    packed = jnp.concatenate(
        [moe_rows, jnp.pad(terms, ((0, 0), (0, PAD - 3 * EXPERTS)))], axis=1
    )
    mine = lax.dynamic_slice_in_dim(packed, pool * half, half, 0)

    swap = [(0, 1), (1, 0)]
    gate_other = lax.ppermute(gate_weight[0], "pool", swap)
    up_other = lax.ppermute(up_weight[0], "pool", swap)
    down_other = lax.ppermute(down_weight[0], "pool", swap)

    spread = jnp.broadcast_to(mine[None], (SIDE,) + mine.shape)
    line = lax.all_to_all(
        spread, AXES, split_axis=0, concat_axis=0, tiled=True, axis_index_groups=first
    ).reshape(SIDE * half, width + PAD)
    plane = lax.all_gather(line, AXES, axis=0, tiled=True, axis_index_groups=second)

    rows = plane[:, :width]
    gathered_terms = plane[:, width : width + 3 * EXPERTS].astype(jnp.float32)
    term_ids = jnp.arange(3 * EXPERTS, dtype=jnp.int32) % EXPERTS
    column = jnp.sum(jnp.where(term_ids[None, :] == expert, gathered_terms, 0.0), axis=1)

    def act_of(gate_part, up_part):
        gate_act = jnp.dot(rows, gate_part, preferred_element_type=jnp.float32)
        up_act = jnp.dot(rows, up_part, preferred_element_type=jnp.float32)
        return (jax.nn.silu(gate_act) * up_act).astype(jnp.bfloat16)

    act = jnp.concatenate(
        [act_of(gate_weight[0], up_weight[0]), act_of(gate_other, up_other)], axis=1
    )
    down = jnp.concatenate([down_weight[0], down_other], axis=0)
    part = jnp.dot(act, down, preferred_element_type=jnp.float32)
    part = (part * column[:, None]).astype(jnp.bfloat16)

    summed = lax.psum_scatter(
        part, AXES, scatter_dimension=0, tiled=True, axis_index_groups=second
    )
    returned = lax.all_to_all(
        summed.reshape(SIDE, half, width),
        AXES,
        split_axis=0,
        concat_axis=0,
        tiled=True,
        axis_index_groups=first,
    )
    total = jnp.sum(returned.astype(jnp.float32), axis=0).astype(jnp.bfloat16)
    other = lax.ppermute(total, "pool", swap)
    lower = jnp.where(pool == 0, total, other)
    upper = jnp.where(pool == 0, other, total)
    return jnp.concatenate([lower, upper], axis=0)


def solution(mesh):
    return jax.shard_map(
        body,
        mesh=mesh,
        in_specs=(
            P(("rep", "dev"), None),
            P(("rep", "dev"), None),
            P(("rep", "dev"), None),
            P("dev", None, "pool"),
            P("dev", None, "pool"),
            P("dev", "pool", None),
        ),
        out_specs=P(("rep", "dev"), None),
        check_vma=False,
    )
```

time: 671 us -> 164 us (0.24)
  the two profiles are of different devices: /device:TPU:243 before, /device:TPU:1 now
where the time goes in v1:
time: 164 us
  waiting for transfers between devices  77.9 us (48%)
  blocking collectives  37.8 us (23%)
  starting transfers between devices  19.3 us (12%)
  between operations  13.6 us (8%)
  matrix products  12 us (7%)
  other arithmetic  1.92 us (1%)
    reduce_scatter x1, waiting for transfers between devices, body(): lax.psum_scatter(part, AXES, scatter_dimension=0, tiled=True, axis_index_...  45.7 us
    all_gather x1, waiting for transfers between devices, body(): lax.all_gather(line, AXES, axis=0, tiled=True, axis_index_groups=second)  31.2 us
    all_to_all x1, blocking collectives, body(): lax.all_to_all(spread, AXES, split_axis=0, concat_axis=0, tiled=True, axi...  19.9 us
    all_to_all x1, blocking collectives, body(): lax.all_to_all(summed.reshape(SIDE, half, width), AXES, split_axis=0, con...  17.9 us
    ppermute x1, starting transfers between devices, body(): other = lax.ppermute(total, 'pool', swap)  7.74 us
    ppermute x1, starting transfers between devices, body(): gate_other = lax.ppermute(gate_weight[0], 'pool', swap)  7.23 us
    dot_general x2, matrix products, act_of(): gate_act = jnp.dot(rows, gate_part, preferred_element_type=jnp.float32)  5.67 us
  transfers between devices with their start and end apart: 6, of which 3 were waited for; matrix products, arithmetic and copies ran while one was open for 5% of the time, Pallas kernels for 0%

profile of v1, /device:TPU:1, one launch (start us, length us, event | category | flops | bytes accessed | tf_op | source)
XLA Modules:
  0.0 164.1 jit_solution(2532473950384916043)
XLA Ops:
  6.5 0.0 all-gather.2.cloned.1.call-start
  6.5 0.8 copy.12
  7.3 0.8 copy.13
  8.1 0.1 select_reduce_fusion.1
  8.2 0.1 fusion.26
  8.3 0.8 fusion.20
  9.1 19.9 %all_to_all.10 = bf16[8,8,4224]{2,1,0:T(8,128)(2,1)} all-to-all(bf16[8,8,4224]{2,1,0:T(8,128)(2,1)S(1)} %broadcast_in_dim.37), channel_id=1, replica_groups={{0,4,8,12,16,20,24,28},{32,36,40,44,48,52,56,60},{64,68,72,76,80,84,88,..., dimensions={0} | all-to-all | bytes 1081344 | tf_op jit(solution)/shard_map/all_to_all | solution.py:47
  29.0 0.0 all-gather.2.cloned.1.call-update
  29.0 0.0 reduce-scatter.2.cloned.1.call-start
  29.1 7.2 %collective-permute-start = (bf16[4096,128]{1,0:T(8,128)(2,1)}, bf16[4096,128]{1,0:T(8,128)(2,1)S(1)}, u32[]{:S(2)}, u32[]{:S(2)}) collective-permute-start(bf16[4096,128]{1,0:T(8,128)(2,1)} %bitcast.13), channel_id=1, source_target_pairs={{0,256},{256,0},{1,257},{257,1},{2,258},{258,2},{3,259},{259,3},{4... | collective-permute-start | bytes 3145736 | tf_op jit(solution)/shard_map/ppermute | solution.py:42
  36.3 1.9 %collective-permute-start.1 = (bf16[4096,128]{1,0:T(8,128)(2,1)}, bf16[4096,128]{1,0:T(8,128)(2,1)S(1)}, u32[]{:S(2)}, u32[]{:S(2)}) collective-permute-start(bf16[4096,128]{1,0:T(8,128)(2,1)} %bitcast.14), channel_id=1, source_target_pairs={{0,256},{256,0},{1,257},{257,1},{2,258},{258,2},{3,259},{259,3},{4... | collective-permute-start | bytes 3145736 | tf_op jit(solution)/shard_map/ppermute | solution.py:43
  38.3 2.4 %collective-permute-start.2 = (bf16[128,4096]{1,0:T(8,128)(2,1)}, bf16[128,4096]{1,0:T(8,128)(2,1)S(1)}, u32[]{:S(2)}, u32[]{:S(2)}) collective-permute-start(bf16[128,4096]{1,0:T(8,128)(2,1)} %bitcast.15), channel_id=1, source_target_pairs={{0,256},{256,0},{1,257},{257,1},{2,258},{258,2},{3,259},{259,3},{4... | collective-permute-start | bytes 3145736 | tf_op jit(solution)/shard_map/ppermute | solution.py:44
  40.7 31.2 %all-gather.2.cloned.1.call-done = bf16[512,4224]{1,0:T(8,128)(2,1)} async-done(((bf16[64,4224]{1,0:T(8,128)(2,1)}), bf16[512,4224]{1,0:T(8,128)(2,1)}) %all-gather.2.cloned.1.call-update) | async-done | bytes 4325392 | tf_op jit(solution)/shard_map/all_gather | solution.py:50
  72.0 0.0 copy-start
  72.0 4.1 %fusion.6 = f32[512,128]{0,1:T(8,128)S(1)} fusion(bf16[512,4224]{1,0:T(8,128)(2,1)} %all-gather.2.cloned.1.call-done, bf16[1,4096,128]{2,1,0:T(8,128)(2,1)} %param.9), kind=kOutput, calls=%fused_computation.7 | convolution fusion | flops 536870912 | bytes 5505024 | tf_op jit(solution)/shard_map/dot_general | solution.py:58
  76.1 0.0 copy-start.1
  76.1 0.0 collective-permute-done
  76.1 0.0 copy-done
  76.1 1.5 fusion.2
  77.7 0.1 select_reduce_fusion
  77.8 0.0 copy-done.1
  77.8 1.5 fusion.14
  79.4 0.0 copy-start.2
  79.4 0.0 collective-permute-done.1
  79.4 1.5 multiply_convert_fusion.1
  80.9 0.0 collective-permute-done.2
  80.9 0.0 copy-done.2
  80.9 3.2 %multiply_convert_fusion = bf16[512,4096]{1,0:T(8,128)(2,1)} fusion(f32[512]{0:T(512)S(1)} %select_reduce_fusion, bf16[128,4096]{1,0:T(8,128)(2,1)S(1)} %collective-permute-done.2, bf16[128,4096]{1,0:T(8,128)(2,1)S(1)} %bitcast.16, bf16[512,128]{0,1:T(8,128)(2,1)S(1)} %multiply_convert_fusion.1, bf16[512,128]{0,1:T(8,128)(2,1)S(1)} %fusion.14), kind=kOutput, calls=%fused_computation | convolution fusion | flops 1082654720 | bytes 6555648 | tf_op jit(solution)/shard_map/dot_general | solution.py:66
  84.2 0.0 reduce-scatter.2.cloned.1.call-update
  84.2 45.7 %reduce-scatter.2.cloned.1.call-done = bf16[64,4096]{1,0:T(8,128)(2,1)} async-done(((bf16[512,4096]{1,0:T(8,128)(2,1)}), bf16[64,4096]{1,0:T(8,128)(2,1)}) %reduce-scatter.2.cloned.1.call-update) | async-done | bytes 524304 | tf_op jit(solution)/shard_map/reduce_scatter | solution.py:69
  129.9 17.9 %all_to_all.11 = bf16[8,8,4096]{2,1,0:T(8,128)(2,1)S(1)} all-to-all(bf16[8,8,4096]{2,1,0:T(8,128)(2,1)} %bitcast.12), channel_id=1, replica_groups={{0,4,8,12,16,20,24,28},{32,36,40,44,48,52,56,60},{64,68,72,76,80,84,88,..., dimensions={0} | all-to-all | bytes 1048576 | tf_op jit(solution)/shard_map/all_to_all | solution.py:72
  147.8 0.1 reduce_sum.32
  147.9 7.7 %collective-permute-start.3 = (bf16[8,4096]{1,0:T(8,128)(2,1)S(1)}, bf16[8,4096]{1,0:T(8,128)(2,1)S(1)}, u32[]{:S(2)}, u32[]{:S(2)}) collective-permute-start(bf16[8,4096]{1,0:T(8,128)(2,1)S(1)} %reduce_sum.32), channel_id=1, source_target_pairs={{0,256},{256,0},{1,257},{257,1},{2,258},{258,2},{3,259},{259,3},{4... | collective-permute-start | bytes 196616 | tf_op jit(solution)/shard_map/ppermute | solution.py:81
  155.7 0.9 collective-permute-done.3
  156.5 0.7 pad_maximum_fusion
  (4 shorter events, 0.1 us)
Async XLA Ops:
  6.5 65.4 %all-gather.2.cloned.1.call-start = ((), (), s32[]{:S(2)}) async-start(), calls=%async_computation.3 | async-start | bytes 4866048 | tf_op jit(solution)/shard_map/all_gather | solution.py:50
  29.0 100.8 %reduce-scatter.2.cloned.1.call-start = ((), (), s32[]{:S(2)}) async-start(), calls=%async_computation.4 | async-start | bytes 4718592 | tf_op jit(solution)/shard_map/reduce_scatter | solution.py:69
  29.1 47.0 %collective-permute-start = (bf16[4096,128]{1,0:T(8,128)(2,1)}, bf16[4096,128]{1,0:T(8,128)(2,1)S(1)}, u32[]{:S(2)}, u32[]{:S(2)}) collective-permute-start(bf16[4096,128]{1,0:T(8,128)(2,1)} %bitcast.13), channel_id=1, source_target_pairs={{0,256},{256,0},{1,257},{257,1},{2,258},{258,2},{3,259},{259,3},{4... | collective-permute-start | bytes 3145736 | tf_op jit(solution)/shard_map/ppermute | solution.py:42
  36.3 43.0 %collective-permute-start.1 = (bf16[4096,128]{1,0:T(8,128)(2,1)}, bf16[4096,128]{1,0:T(8,128)(2,1)S(1)}, u32[]{:S(2)}, u32[]{:S(2)}) collective-permute-start(bf16[4096,128]{1,0:T(8,128)(2,1)} %bitcast.14), channel_id=1, source_target_pairs={{0,256},{256,0},{1,257},{257,1},{2,258},{258,2},{3,259},{259,3},{4... | collective-permute-start | bytes 3145736 | tf_op jit(solution)/shard_map/ppermute | solution.py:43
  38.3 42.7 %collective-permute-start.2 = (bf16[128,4096]{1,0:T(8,128)(2,1)}, bf16[128,4096]{1,0:T(8,128)(2,1)S(1)}, u32[]{:S(2)}, u32[]{:S(2)}) collective-permute-start(bf16[128,4096]{1,0:T(8,128)(2,1)} %bitcast.15), channel_id=1, source_target_pairs={{0,256},{256,0},{1,257},{257,1},{2,258},{258,2},{3,259},{259,3},{4... | collective-permute-start | bytes 3145736 | tf_op jit(solution)/shard_map/ppermute | solution.py:44
  72.0 4.2 %copy-start = (bf16[512,4224]{1,0:T(8,128)(2,1)S(1)}, bf16[512,4224]{1,0:T(8,128)(2,1)}, u32[]{:S(2)}) copy-start(bf16[512,4224]{1,0:T(8,128)(2,1)} %all-gather.2.cloned.1.call-done) | copy-start | bytes 12976132
  76.1 1.7 %copy-start.1 = (bf16[1,4096,128]{2,1,0:T(8,128)(2,1)S(1)}, bf16[1,4096,128]{2,1,0:T(8,128)(2,1)}, u32[]{:S(2)}) copy-start(bf16[1,4096,128]{2,1,0:T(8,128)(2,1)} %param.10) | copy-start | bytes 3145732
  79.4 1.6 copy-start.2
  147.9 8.6 %collective-permute-start.3 = (bf16[8,4096]{1,0:T(8,128)(2,1)S(1)}, bf16[8,4096]{1,0:T(8,128)(2,1)S(1)}, u32[]{:S(2)}, u32[]{:S(2)}) collective-permute-start(bf16[8,4096]{1,0:T(8,128)(2,1)S(1)} %reduce_sum.32), channel_id=1, source_target_pairs={{0,256},{256,0},{1,257},{257,1},{2,258},{258,2},{3,259},{259,3},{4... | collective-permute-start | bytes 196616 | tf_op jit(solution)/shard_map/ppermute | solution.py:81
Sparse Core Ops, SparseCore 0:
  29.2 42.7 all-gather.1
  84.3 45.5 reduce-scatter.1

commit v2 on v1

v2 whole, which is shorter than its diff:
```python
import jax
import jax.numpy as jnp
from jax import lax
from jax.sharding import PartitionSpec as P

EXPERTS = 16
SIDE = 8
AXES = ("pool", "dev")
PAD = 128
REACH = SIDE // 2 - 1
SWAP = [(0, 1), (1, 0)]


def line_groups():
    along_z = [[y * SIDE + z for z in range(SIDE)] for y in range(SIDE)]
    along_y = [[y * SIDE + z for y in range(SIDE)] for z in range(SIDE)]
    shift = SIDE * SIDE
    return along_z + [[shift + i for i in group] for group in along_y]


def second_axis(other):
    places = [(y, z) for y in range(SIDE) for z in range(SIDE)]
    shift = SIDE * SIDE
    pairs = [(y * SIDE + z, other(y) * SIDE + z) for y, z in places]
    return pairs + [(shift + y * SIDE + z, shift + y * SIDE + other(z)) for y, z in places]


def neighbour_swap(odd):
    return second_axis(lambda c: (c + 1) % SIDE if c % 2 == odd else (c - 1) % SIDE)


def body(moe_rows, routes, gate_values, gate_weight, up_weight, down_weight):
    device_count = lax.axis_size("dev")
    groups = line_groups()
    odd_pairs, even_pairs = neighbour_swap(1), neighbour_swap(0)
    pool = lax.axis_index("pool")
    expert = lax.axis_index("dev") * EXPERTS // device_count
    row_count, width = moe_rows.shape
    half = row_count // 2

    expert_ids = jnp.arange(EXPERTS, dtype=jnp.int32)
    chosen = routes[:, :, None] == expert_ids[None, None, :]
    weight = jnp.sum(jnp.where(chosen, gate_values[:, :, None], 0.0), axis=1)
    high = lax.reduce_precision(weight, 8, 7)
    middle = lax.reduce_precision(weight - high, 8, 7)
    low = weight - high - middle
    terms = jnp.concatenate([high, middle, low], axis=1).astype(jnp.bfloat16)
    packed = jnp.concatenate(
        [moe_rows, jnp.pad(terms, ((0, 0), (0, PAD - 3 * EXPERTS)))], axis=1
    )
    mine = lax.dynamic_slice_in_dim(packed, pool * half, half, 0)

    cut = gate_weight.shape[2]
    spread = jnp.broadcast_to(mine[None], (SIDE,) + mine.shape)
    own = lax.all_to_all(
        spread, AXES, split_axis=0, concat_axis=0, tiled=True, axis_index_groups=groups
    ).reshape(SIDE * half, width + PAD)

    def swap_both(to_one, to_two, step):
        pairs = (odd_pairs, even_pairs) if step % 2 else (even_pairs, odd_pairs)
        return lax.ppermute(to_one, AXES, pairs[0]), lax.ppermute(to_two, AXES, pairs[1])

    one_in, two_in = [own], [own]
    for step in range(1, REACH + 1):
        from_one, from_two = swap_both(one_in[-1], two_in[-1], step)
        one_in.append(from_one)
        two_in.append(from_two)
    middle_column = width // 2
    to_one = one_in[-1][:, :middle_column]
    _, to_two = lax.optimization_barrier((to_one, two_in[-1][:, middle_column:]))
    far = jnp.concatenate(swap_both(to_one, to_two, REACH + 1), axis=1)

    gate_part, up_part, down, _ = lax.optimization_barrier(
        (gate_weight[0], up_weight[0], down_weight[0], own)
    )
    gate_up = jnp.concatenate([gate_part, up_part], axis=1)
    gate_up_other = lax.ppermute(gate_up, "pool", SWAP)
    down_other = lax.ppermute(down, "pool", SWAP)

    term_ids = jnp.arange(3 * EXPERTS, dtype=jnp.int32) % EXPERTS

    def act_of(rows, weights):
        hidden = jnp.dot(rows, weights, preferred_element_type=jnp.float32)
        return (jax.nn.silu(hidden[:, :cut]) * hidden[:, cut:]).astype(jnp.bfloat16)

    def part_of(block):
        rows = block[:, :width]
        act, act_other = act_of(rows, gate_up), act_of(rows, gate_up_other)
        column_terms = block[:, width : width + 3 * EXPERTS].astype(jnp.float32)
        column = jnp.sum(jnp.where(term_ids[None, :] == expert, column_terms, 0.0), axis=1)
        out = jnp.dot(act, down, preferred_element_type=jnp.float32)
        out = out + jnp.dot(act_other, down_other, preferred_element_type=jnp.float32)
        return out * column[:, None]

    size = SIDE * half
    far_part = part_of(far).astype(jnp.bfloat16)
    from_one, from_two = swap_both(
        far_part[:, :middle_column], far_part[:, middle_column:], REACH + 1
    )
    from_one = jnp.pad(from_one, ((0, 0), (0, width - middle_column)))
    from_two = jnp.pad(from_two, ((0, 0), (middle_column, 0)))
    for step in range(REACH, 0, -1):
        parts = part_of(jnp.concatenate([one_in[step], two_in[step]], axis=0))
        part_one, part_two = lax.optimization_barrier((parts[:size], parts[size:]))
        one_sum = part_one + from_one.astype(jnp.float32)
        two_sum = part_two + from_two.astype(jnp.float32)
        from_one, from_two = swap_both(
            one_sum.astype(jnp.bfloat16), two_sum.astype(jnp.bfloat16), step
        )
    summed = part_of(own) + from_one.astype(jnp.float32) + from_two.astype(jnp.float32)

    returned = lax.all_to_all(
        summed.astype(jnp.bfloat16).reshape(SIDE, half, width),
        AXES,
        split_axis=0,
        concat_axis=0,
        tiled=True,
        axis_index_groups=groups,
    )
    total = jnp.sum(returned.astype(jnp.float32), axis=0).astype(jnp.bfloat16)
    other = lax.ppermute(total, "pool", SWAP)
    lower = jnp.where(pool == 0, total, other)
    upper = jnp.where(pool == 0, other, total)
    return jnp.concatenate([lower, upper], axis=0)


def solution(mesh):
    return jax.shard_map(
        body,
        mesh=mesh,
        in_specs=(
            P(("rep", "dev"), None),
            P(("rep", "dev"), None),
            P(("rep", "dev"), None),
            P("dev", None, "pool"),
            P("dev", None, "pool"),
            P("dev", "pool", None),
        ),
        out_specs=P(("rep", "dev"), None),
        check_vma=False,
    )
```

time: 164 us -> 153 us (0.933)
  starting transfers between devices: 19.3 us -> 75.5 us
  waiting for transfers between devices: 77.9 us -> 47 us
  blocking collectives: 37.8 us -> 13.9 us
  between operations: 13.6 us -> 0.53 us
  matrix products: 12 us -> 8.61 us
  local copies, waits for them, and re-layouts: 1.57 us -> 3.86 us
    ppermute x4 -> x19, starting transfers between devices: 19.3 us -> 67.9 us  [the longest x8 32.3 us: swap_both(): lax.ppermute(to_one, AXES, pairs[0])]
    reduce_scatter x1 -> x0, waiting for transfers between devices: 45.7 us -> none  [body(): lax.psum_scatter(part, AXES, scatter_dimension=0, tiled=True, axis_index_...]
    ppermute x4 -> x19, waiting for transfers between devices: 0.88 us -> 34.6 us  [the longest x8 16.9 us: swap_both(): lax.ppermute(to_one, AXES, pairs[0])]
    all_gather x1 -> x0, waiting for transfers between devices: 31.2 us -> none  [body(): lax.all_gather(line, AXES, axis=0, tiled=True, axis_index_groups=second)]
    all_to_all x2 -> x1, blocking collectives: 37.8 us -> 13.9 us  [body(): lax.all_to_all(summed.astype(jnp.bfloat16).reshape(SIDE, half, width), AX...]
    all_to_all x0 -> x1, waiting for transfers between devices: none -> 12.3 us  [body(): lax.all_to_all(spread, AXES, split_axis=0, concat_axis=0, tiled=True, axi...]
    all_to_all x0 -> x1, starting transfers between devices: none -> 7.65 us  [body(): lax.all_to_all(spread, AXES, split_axis=0, concat_axis=0, tiled=True, axi...]
    dot_general x5 -> x20, matrix products: 12 us -> 8.61 us  [the longest x10 4.65 us: act_of(): hidden = jnp.dot(rows, weights, preferred_element_type=jnp.float32)]
  transfers between devices with their start and end apart: 6 -> 20, of which waited for: 3 -> 14; matrix products, arithmetic and copies ran while one was open for 5% -> 7% of each run, Pallas kernels for 0% -> 0%
where the time goes in v2:
time: 153 us; the launch traced here: 152 us
  starting transfers between devices  75.5 us (49%)
  waiting for transfers between devices  47 us (31%)
  blocking collectives  13.9 us (9%)
  matrix products  8.61 us (6%)
  local copies, waits for them, and re-layouts  3.86 us (3%)
  other arithmetic  2.6 us (2%)
    ppermute x8, starting transfers between devices, swap_both(): lax.ppermute(to_one, AXES, pairs[0])  32.3 us
    ppermute x8, starting transfers between devices, swap_both(): lax.ppermute(to_two, AXES, pairs[1])  18.2 us
    ppermute x8, waiting for transfers between devices, swap_both(): lax.ppermute(to_one, AXES, pairs[0])  16.9 us
    ppermute x8, waiting for transfers between devices, swap_both(): lax.ppermute(to_two, AXES, pairs[1])  16.9 us
    all_to_all x1, blocking collectives, body(): lax.all_to_all(summed.astype(jnp.bfloat16).reshape(SIDE, half, width), AX...  13.9 us
    ppermute x1, starting transfers between devices, body(): other = lax.ppermute(total, 'pool', SWAP)  13.1 us
    all_to_all x1, waiting for transfers between devices, body(): lax.all_to_all(spread, AXES, split_axis=0, concat_axis=0, tiled=True, axi...  12.3 us
    all_to_all x1, starting transfers between devices, body(): lax.all_to_all(spread, AXES, split_axis=0, concat_axis=0, tiled=True, axi...  7.65 us
  transfers between devices with their start and end apart: 20, of which 14 were waited for; matrix products, arithmetic and copies ran while one was open for 7% of the time, Pallas kernels for 0%

profile of v2, /device:TPU:1, one launch (start us, length us, event | category | flops | bytes accessed | tf_op | source)
XLA Modules:
  0.0 152.0 jit_solution(15781811684377484965)
XLA Ops:
  0.0 0.9 copy.12
  0.9 0.8 copy.13
  1.9 0.8 fusion.28
  2.7 0.8 broadcast_in_dim.69
  3.6 7.7 %all-to-all-start = ((bf16[8,8,4224]{2,1,0:T(8,128)(2,1)}), bf16[8,8,4224]{2,1,0:T(8,128)(2,1)S(1)}, u32[]{:S(2)}, u32[]{:S(2)}) async-start(bf16[8,8,4224]{2,1,0:T(8,128)(2,1)} %broadcast_in_dim.69), calls=%async_computation | async-start | bytes 1081344 | tf_op jit(solution)/shard_map/all_to_all | solution.py:55
  11.2 12.3 %all-to-all-done = bf16[8,8,4224]{2,1,0:T(8,128)(2,1)S(1)} async-done(((bf16[8,8,4224]{2,1,0:T(8,128)(2,1)}), bf16[8,8,4224]{2,1,0:T(8,128)(2,1)S(1)}, u32[]{:S(2)}, u32[]{:S(2)}) %all-to-all-start) | async-done | bytes 540704 | tf_op jit(solution)/shard_map/all_to_all | solution.py:55
  23.5 10.7 %collective-permute-start.2 = (bf16[64,4224]{1,0:T(8,128)(2,1)S(1)}, bf16[64,4224]{1,0:T(8,128)(2,1)S(1)}, u32[]{:S(2)}, u32[]{:S(2)}) collective-permute-start(bf16[64,4224]{1,0:T(8,128)(2,1)S(1)} %bitcast.32), channel_id=1, source_target_pairs={{0,224},{4,228},{8,232},{12,236},{16,240},{20,244},{24,248},{28,25... | collective-permute-start | bytes 1622024 | tf_op jit(solution)/shard_map/ppermute | solution.py:61
  34.2 1.9 %collective-permute-start.3 = (bf16[64,4224]{1,0:T(8,128)(2,1)S(1)}, bf16[64,4224]{1,0:T(8,128)(2,1)S(1)}, u32[]{:S(2)}, u32[]{:S(2)}) collective-permute-start(bf16[64,4224]{1,0:T(8,128)(2,1)S(1)} %bitcast.33), channel_id=1, source_target_pairs={{0,32},{4,36},{8,40},{12,44},{16,48},{20,52},{24,56},{28,60},{32,0... | collective-permute-start | bytes 1622024 | tf_op jit(solution)/shard_map/ppermute | solution.py:61
  36.6 1.9 %collective-permute-start = (bf16[4096,256]{1,0:T(8,128)(2,1)S(1)}, bf16[4096,256]{1,0:T(8,128)(2,1)S(1)}, u32[]{:S(2)}, u32[]{:S(2)}) collective-permute-start(bf16[4096,256]{1,0:T(8,128)(2,1)S(1)} %constant_dynamic-update-slice_fusion), channel_id=1, source_target_pairs={{0,256},{256,0},{1,257},{257,1},{2,258},{258,2},{3,259},{259,3},{4... | collective-permute-start | bytes 6291464 | tf_op jit(solution)/shard_map/ppermute | solution.py:77
  38.6 2.4 %collective-permute-start.1 = (bf16[128,4096]{1,0:T(8,128)(2,1)S(1)}, bf16[128,4096]{1,0:T(8,128)(2,1)S(1)}, u32[]{:S(2)}, u32[]{:S(2)}) collective-permute-start(bf16[128,4096]{1,0:T(8,128)(2,1)S(1)} %bitcast.26), channel_id=1, source_target_pairs={{0,256},{256,0},{1,257},{257,1},{2,258},{258,2},{3,259},{259,3},{4... | collective-permute-start | bytes 3145736 | tf_op jit(solution)/shard_map/ppermute | solution.py:78
  41.0 0.5 fusion.24
  41.5 3.4 %collective-permute-start.4 = (bf16[64,4224]{1,0:T(8,128)(2,1)S(1)}, bf16[64,4224]{1,0:T(8,128)(2,1)S(1)}, u32[]{:S(2)}, u32[]{:S(2)}) collective-permute-start(bf16[64,4224]{1,0:T(8,128)(2,1)S(1)} %collective-permute-done.2), channel_id=1, source_target_pairs={{0,32},{4,36},{8,40},{12,44},{16,48},{20,52},{24,56},{28,60},{32,0... | collective-permute-start | bytes 1622024 | tf_op jit(solution)/shard_map/ppermute | solution.py:61
  44.9 2.6 %collective-permute-start.5 = (bf16[64,4224]{1,0:T(8,128)(2,1)S(1)}, bf16[64,4224]{1,0:T(8,128)(2,1)S(1)}, u32[]{:S(2)}, u32[]{:S(2)}) collective-permute-start(bf16[64,4224]{1,0:T(8,128)(2,1)S(1)} %collective-permute-done.3), channel_id=1, source_target_pairs={{0,224},{4,228},{8,232},{12,236},{16,240},{20,244},{24,248},{28,25... | collective-permute-start | bytes 1622024 | tf_op jit(solution)/shard_map/ppermute | solution.py:61
  47.5 0.5 fusion.20
  48.5 3.4 %collective-permute-done.4 = bf16[64,4224]{1,0:T(8,128)(2,1)S(1)} collective-permute-done((bf16[64,4224]{1,0:T(8,128)(2,1)S(1)}, bf16[64,4224]{1,0:T(8,128)(2,1)S(1)}, u32[]{:S(2)}, u32[]{:S(2)}) %collective-permute-start.4) | collective-permute-done | bytes 540704 | tf_op jit(solution)/shard_map/ppermute | solution.py:61
  51.9 4.0 %collective-permute-start.6 = (bf16[64,4224]{1,0:T(8,128)(2,1)S(1)}, bf16[64,4224]{1,0:T(8,128)(2,1)S(1)}, u32[]{:S(2)}, u32[]{:S(2)}) collective-permute-start(bf16[64,4224]{1,0:T(8,128)(2,1)S(1)} %collective-permute-done.4), channel_id=1, source_target_pairs={{0,224},{4,228},{8,232},{12,236},{16,240},{20,244},{24,248},{28,25... | collective-permute-start | bytes 1622024 | tf_op jit(solution)/shard_map/ppermute | solution.py:61
  55.9 0.6 collective-permute-done.5
  56.5 1.9 %collective-permute-start.7 = (bf16[64,4224]{1,0:T(8,128)(2,1)S(1)}, bf16[64,4224]{1,0:T(8,128)(2,1)S(1)}, u32[]{:S(2)}, u32[]{:S(2)}) collective-permute-start(bf16[64,4224]{1,0:T(8,128)(2,1)S(1)} %collective-permute-done.5), channel_id=1, source_target_pairs={{0,32},{4,36},{8,40},{12,44},{16,48},{20,52},{24,56},{28,60},{32,0... | collective-permute-start | bytes 1622024 | tf_op jit(solution)/shard_map/ppermute | solution.py:61
  58.5 0.5 fusion.16
  59.4 4.1 %collective-permute-done.6 = bf16[64,4224]{1,0:T(8,128)(2,1)S(1)} collective-permute-done((bf16[64,4224]{1,0:T(8,128)(2,1)S(1)}, bf16[64,4224]{1,0:T(8,128)(2,1)S(1)}, u32[]{:S(2)}, u32[]{:S(2)}) %collective-permute-start.6) | collective-permute-done | bytes 540704 | tf_op jit(solution)/shard_map/ppermute | solution.py:61
  63.5 2.2 %collective-permute-start.8 = (bf16[64,2048]{1,0:T(8,128)(2,1)S(1)}, bf16[64,2048]{1,0:T(8,128)(2,1)S(1)}, u32[]{:S(2)}, u32[]{:S(2)}) collective-permute-start(bf16[64,2048]{1,0:T(8,128)(2,1)S(1)} %slice.190), channel_id=1, source_target_pairs={{0,32},{4,36},{8,40},{12,44},{16,48},{20,52},{24,56},{28,60},{32,0... | collective-permute-start | bytes 786440 | tf_op jit(solution)/shard_map/ppermute | solution.py:61
  65.6 1.2 collective-permute-done.7
  66.9 2.3 %collective-permute-start.9 = (bf16[64,2176]{1,0:T(8,128)(2,1)S(1)}, bf16[64,2176]{1,0:T(8,128)(2,1)S(1)}, u32[]{:S(2)}, u32[]{:S(2)}) collective-permute-start(bf16[64,2176]{1,0:T(8,128)(2,1)S(1)} %slice.191), channel_id=1, source_target_pairs={{0,224},{4,228},{8,232},{12,236},{16,240},{20,244},{24,248},{28,25... | collective-permute-start | bytes 835592 | tf_op jit(solution)/shard_map/ppermute | solution.py:61
  69.3 0.5 fusion.12
  70.3 5.4 %collective-permute-done.9 = bf16[64,2176]{1,0:T(8,128)(2,1)S(1)} collective-permute-done((bf16[64,2176]{1,0:T(8,128)(2,1)S(1)}, bf16[64,2176]{1,0:T(8,128)(2,1)S(1)}, u32[]{:S(2)}, u32[]{:S(2)}) %collective-permute-start.9) | collective-permute-done | bytes 278560 | tf_op jit(solution)/shard_map/ppermute | solution.py:61
  75.8 0.5 fusion.26
  76.6 0.5 fusion.27
  77.5 1.9 %collective-permute-start.10 = (bf16[64,2048]{1,0:T(8,128)(2,1)S(1)}, bf16[64,2048]{1,0:T(8,128)(2,1)S(1)}, u32[]{:S(2)}, u32[]{:S(2)}) collective-permute-start(bf16[64,2048]{1,0:T(8,128)(2,1)S(1)} %get-tuple-element.36), channel_id=1, source_target_pairs={{0,32},{4,36},{8,40},{12,44},{16,48},{20,52},{24,56},{28,60},{32,0... | collective-permute-start | bytes 786440 | tf_op jit(solution)/shard_map/ppermute | solution.py:61
  80.5 0.4 fusion.14
  82.7 2.5 %collective-permute-start.14 = (bf16[64,2048]{1,0:T(8,128)(2,1)S(1)}, bf16[64,2048]{1,0:T(8,128)(2,1)S(1)}, u32[]{:S(2)}, u32[]{:S(2)}) collective-permute-start(bf16[64,2048]{1,0:T(8,128)(2,1)S(1)} %get-tuple-element.37), channel_id=1, source_target_pairs={{0,224},{4,228},{8,232},{12,236},{16,240},{20,244},{24,248},{28,25... | collective-permute-start | bytes 786440 | tf_op jit(solution)/shard_map/ppermute | solution.py:61
  85.3 4.0 %collective-permute-start.11 = (bf16[64,4096]{1,0:T(8,128)(2,1)S(1)}, bf16[64,4096]{1,0:T(8,128)(2,1)S(1)}, u32[]{:S(2)}, u32[]{:S(2)}) collective-permute-start(bf16[64,4096]{1,0:T(8,128)(2,1)S(1)} %add_convert_fusion.5), channel_id=1, source_target_pairs={{0,224},{4,228},{8,232},{12,236},{16,240},{20,244},{24,248},{28,25... | collective-permute-start | bytes 1572872 | tf_op jit(solution)/shard_map/ppermute | solution.py:61
  89.3 1.7 %collective-permute-done.14 = bf16[64,2048]{1,0:T(8,128)(2,1)S(1)} collective-permute-done((bf16[64,2048]{1,0:T(8,128)(2,1)S(1)}, bf16[64,2048]{1,0:T(8,128)(2,1)S(1)}, u32[]{:S(2)}, u32[]{:S(2)}) %collective-permute-start.14) | collective-permute-done | bytes 262176 | tf_op jit(solution)/shard_map/ppermute | solution.py:61
  91.1 2.1 %collective-permute-start.15 = (bf16[64,4096]{1,0:T(8,128)(2,1)S(1)}, bf16[64,4096]{1,0:T(8,128)(2,1)S(1)}, u32[]{:S(2)}, u32[]{:S(2)}) collective-permute-start(bf16[64,4096]{1,0:T(8,128)(2,1)S(1)} %add_convert_fusion.2), channel_id=1, source_target_pairs={{0,32},{4,36},{8,40},{12,44},{16,48},{20,52},{24,56},{28,60},{32,0... | collective-permute-start | bytes 1572872 | tf_op jit(solution)/shard_map/ppermute | solution.py:61
  93.3 3.7 %collective-permute-done.11 = bf16[64,4096]{1,0:T(8,128)(2,1)S(1)} collective-permute-done((bf16[64,4096]{1,0:T(8,128)(2,1)S(1)}, bf16[64,4096]{1,0:T(8,128)(2,1)S(1)}, u32[]{:S(2)}, u32[]{:S(2)}) %collective-permute-start.11) | collective-permute-done | bytes 524320 | tf_op jit(solution)/shard_map/ppermute | solution.py:61
  97.0 2.1 %collective-permute-start.12 = (bf16[64,4096]{1,0:T(8,128)(2,1)S(1)}, bf16[64,4096]{1,0:T(8,128)(2,1)S(1)}, u32[]{:S(2)}, u32[]{:S(2)}) collective-permute-start(bf16[64,4096]{1,0:T(8,128)(2,1)S(1)} %add_convert_fusion.4), channel_id=1, source_target_pairs={{0,32},{4,36},{8,40},{12,44},{16,48},{20,52},{24,56},{28,60},{32,0... | collective-permute-start | bytes 1572872 | tf_op jit(solution)/shard_map/ppermute | solution.py:61
  99.2 2.1 %collective-permute-done.15 = bf16[64,4096]{1,0:T(8,128)(2,1)S(1)} collective-permute-done((bf16[64,4096]{1,0:T(8,128)(2,1)S(1)}, bf16[64,4096]{1,0:T(8,128)(2,1)S(1)}, u32[]{:S(2)}, u32[]{:S(2)}) %collective-permute-start.15) | collective-permute-done | bytes 524320 | tf_op jit(solution)/shard_map/ppermute | solution.py:61
  101.4 2.8 %collective-permute-start.16 = (bf16[64,4096]{1,0:T(8,128)(2,1)S(1)}, bf16[64,4096]{1,0:T(8,128)(2,1)S(1)}, u32[]{:S(2)}, u32[]{:S(2)}) collective-permute-start(bf16[64,4096]{1,0:T(8,128)(2,1)S(1)} %add_convert_fusion.1), channel_id=1, source_target_pairs={{0,224},{4,228},{8,232},{12,236},{16,240},{20,244},{24,248},{28,25... | collective-permute-start | bytes 1572872 | tf_op jit(solution)/shard_map/ppermute | solution.py:61
  104.3 2.7 %collective-permute-done.12 = bf16[64,4096]{1,0:T(8,128)(2,1)S(1)} collective-permute-done((bf16[64,4096]{1,0:T(8,128)(2,1)S(1)}, bf16[64,4096]{1,0:T(8,128)(2,1)S(1)}, u32[]{:S(2)}, u32[]{:S(2)}) %collective-permute-start.12) | collective-permute-done | bytes 524320 | tf_op jit(solution)/shard_map/ppermute | solution.py:61
  107.1 4.1 %collective-permute-start.13 = (bf16[64,4096]{1,0:T(8,128)(2,1)S(1)}, bf16[64,4096]{1,0:T(8,128)(2,1)S(1)}, u32[]{:S(2)}, u32[]{:S(2)}) collective-permute-start(bf16[64,4096]{1,0:T(8,128)(2,1)S(1)} %add_convert_fusion.3), channel_id=1, source_target_pairs={{0,224},{4,228},{8,232},{12,236},{16,240},{20,244},{24,248},{28,25... | collective-permute-start | bytes 1572872 | tf_op jit(solution)/shard_map/ppermute | solution.py:61
  111.2 1.4 collective-permute-done.16
  112.7 1.9 %collective-permute-start.17 = (bf16[64,4096]{1,0:T(8,128)(2,1)S(1)}, bf16[64,4096]{1,0:T(8,128)(2,1)S(1)}, u32[]{:S(2)}, u32[]{:S(2)}) collective-permute-start(bf16[64,4096]{1,0:T(8,128)(2,1)S(1)} %add_convert_fusion), channel_id=1, source_target_pairs={{0,32},{4,36},{8,40},{12,44},{16,48},{20,52},{24,56},{28,60},{32,0... | collective-permute-start | bytes 1572872 | tf_op jit(solution)/shard_map/ppermute | solution.py:61
  114.9 0.5 fusion.22
  115.4 3.1 %collective-permute-done.13 = bf16[64,4096]{1,0:T(8,128)(2,1)S(1)} collective-permute-done((bf16[64,4096]{1,0:T(8,128)(2,1)S(1)}, bf16[64,4096]{1,0:T(8,128)(2,1)S(1)}, u32[]{:S(2)}, u32[]{:S(2)}) %collective-permute-start.13) | collective-permute-done | bytes 524320 | tf_op jit(solution)/shard_map/ppermute | solution.py:61
  118.5 4.4 %collective-permute-done.17 = bf16[64,4096]{1,0:T(8,128)(2,1)S(1)} collective-permute-done((bf16[64,4096]{1,0:T(8,128)(2,1)S(1)}, bf16[64,4096]{1,0:T(8,128)(2,1)S(1)}, u32[]{:S(2)}, u32[]{:S(2)}) %collective-permute-start.17) | collective-permute-done | bytes 524320 | tf_op jit(solution)/shard_map/ppermute | solution.py:61
  123.4 13.9 %all_to_all.10 = bf16[8,8,4096]{2,1,0:T(8,128)(2,1)S(1)} all-to-all(bf16[8,8,4096]{2,1,0:T(8,128)(2,1)S(1)} %fusion.9), channel_id=1, replica_groups={{0,4,8,12,16,20,24,28},{32,36,40,44,48,52,56,60},{64,68,72,76,80,84,88,..., dimensions={0} | all-to-all | bytes 1048576 | tf_op jit(solution)/shard_map/all_to_all | solution.py:112
  137.3 13.1 %collective-permute-start.18 = (bf16[8,4096]{1,0:T(8,128)(2,1)S(1)}, bf16[8,4096]{1,0:T(8,128)(2,1)S(1)}, u32[]{:S(2)}, u32[]{:S(2)}) collective-permute-start(bf16[8,4096]{1,0:T(8,128)(2,1)S(1)} %reduce_sum.72), channel_id=1, source_target_pairs={{0,256},{256,0},{1,257},{257,1},{2,258},{258,2},{3,259},{259,3},{4... | collective-permute-start | bytes 196616 | tf_op jit(solution)/shard_map/ppermute | solution.py:121
  150.4 0.9 collective-permute-done.18
  151.3 0.7 pad_maximum_fusion.3
  (52 shorter events, 7.3 us)
Async XLA Ops:
  0.0 36.1 %copy-start.1 = (bf16[1,4096,128]{2,1,0:T(8,128)(2,1)S(1)}, bf16[1,4096,128]{2,1,0:T(8,128)(2,1)}, u32[]{:S(2)}) copy-start(bf16[1,4096,128]{2,1,0:T(8,128)(2,1)} %param.9) | copy-start | bytes 3145732
  0.0 36.3 %copy-start.2 = (bf16[1,4096,128]{2,1,0:T(8,128)(2,1)S(1)}, bf16[1,4096,128]{2,1,0:T(8,128)(2,1)}, u32[]{:S(2)}) copy-start(bf16[1,4096,128]{2,1,0:T(8,128)(2,1)} %param.10) | copy-start | bytes 3145732
  3.6 20.0 %all-to-all-start = ((bf16[8,8,4224]{2,1,0:T(8,128)(2,1)}), bf16[8,8,4224]{2,1,0:T(8,128)(2,1)S(1)}, u32[]{:S(2)}, u32[]{:S(2)}) async-start(bf16[8,8,4224]{2,1,0:T(8,128)(2,1)} %broadcast_in_dim.69), calls=%async_computation | async-start | bytes 1081344 | tf_op jit(solution)/shard_map/all_to_all | solution.py:55
  23.5 17.9 %collective-permute-start.2 = (bf16[64,4224]{1,0:T(8,128)(2,1)S(1)}, bf16[64,4224]{1,0:T(8,128)(2,1)S(1)}, u32[]{:S(2)}, u32[]{:S(2)}) collective-permute-start(bf16[64,4224]{1,0:T(8,128)(2,1)S(1)} %bitcast.32), channel_id=1, source_target_pairs={{0,224},{4,228},{8,232},{12,236},{16,240},{20,244},{24,248},{28,25... | collective-permute-start | bytes 1622024 | tf_op jit(solution)/shard_map/ppermute | solution.py:61
  34.2 10.7 %collective-permute-start.3 = (bf16[64,4224]{1,0:T(8,128)(2,1)S(1)}, bf16[64,4224]{1,0:T(8,128)(2,1)S(1)}, u32[]{:S(2)}, u32[]{:S(2)}) collective-permute-start(bf16[64,4224]{1,0:T(8,128)(2,1)S(1)} %bitcast.33), channel_id=1, source_target_pairs={{0,32},{4,36},{8,40},{12,44},{16,48},{20,52},{24,56},{28,60},{32,0... | collective-permute-start | bytes 1622024 | tf_op jit(solution)/shard_map/ppermute | solution.py:61
  36.1 2.4 %copy-start = (bf16[1,128,4096]{2,1,0:T(8,128)(2,1)S(1)}, bf16[1,128,4096]{2,1,0:T(8,128)(2,1)}, u32[]{:S(2)}) copy-start(bf16[1,128,4096]{2,1,0:T(8,128)(2,1)} %param.11) | copy-start | bytes 3145732
  36.6 40.0 %collective-permute-start = (bf16[4096,256]{1,0:T(8,128)(2,1)S(1)}, bf16[4096,256]{1,0:T(8,128)(2,1)S(1)}, u32[]{:S(2)}, u32[]{:S(2)}) collective-permute-start(bf16[4096,256]{1,0:T(8,128)(2,1)S(1)} %constant_dynamic-update-slice_fusion), channel_id=1, source_target_pairs={{0,256},{256,0},{1,257},{257,1},{2,258},{258,2},{3,259},{259,3},{4... | collective-permute-start | bytes 6291464 | tf_op jit(solution)/shard_map/ppermute | solution.py:77
  38.6 38.6 %collective-permute-start.1 = (bf16[128,4096]{1,0:T(8,128)(2,1)S(1)}, bf16[128,4096]{1,0:T(8,128)(2,1)S(1)}, u32[]{:S(2)}, u32[]{:S(2)}) collective-permute-start(bf16[128,4096]{1,0:T(8,128)(2,1)S(1)} %bitcast.26), channel_id=1, source_target_pairs={{0,256},{256,0},{1,257},{257,1},{2,258},{258,2},{3,259},{259,3},{4... | collective-permute-start | bytes 3145736 | tf_op jit(solution)/shard_map/ppermute | solution.py:78
  41.5 10.4 %collective-permute-start.4 = (bf16[64,4224]{1,0:T(8,128)(2,1)S(1)}, bf16[64,4224]{1,0:T(8,128)(2,1)S(1)}, u32[]{:S(2)}, u32[]{:S(2)}) collective-permute-start(bf16[64,4224]{1,0:T(8,128)(2,1)S(1)} %collective-permute-done.2), channel_id=1, source_target_pairs={{0,32},{4,36},{8,40},{12,44},{16,48},{20,52},{24,56},{28,60},{32,0... | collective-permute-start | bytes 1622024 | tf_op jit(solution)/shard_map/ppermute | solution.py:61
  44.9 11.6 %collective-permute-start.5 = (bf16[64,4224]{1,0:T(8,128)(2,1)S(1)}, bf16[64,4224]{1,0:T(8,128)(2,1)S(1)}, u32[]{:S(2)}, u32[]{:S(2)}) collective-permute-start(bf16[64,4224]{1,0:T(8,128)(2,1)S(1)} %collective-permute-done.3), channel_id=1, source_target_pairs={{0,224},{4,228},{8,232},{12,236},{16,240},{20,244},{24,248},{28,25... | collective-permute-start | bytes 1622024 | tf_op jit(solution)/shard_map/ppermute | solution.py:61
  51.9 11.6 %collective-permute-start.6 = (bf16[64,4224]{1,0:T(8,128)(2,1)S(1)}, bf16[64,4224]{1,0:T(8,128)(2,1)S(1)}, u32[]{:S(2)}, u32[]{:S(2)}) collective-permute-start(bf16[64,4224]{1,0:T(8,128)(2,1)S(1)} %collective-permute-done.4), channel_id=1, source_target_pairs={{0,224},{4,228},{8,232},{12,236},{16,240},{20,244},{24,248},{28,25... | collective-permute-start | bytes 1622024 | tf_op jit(solution)/shard_map/ppermute | solution.py:61
  56.5 10.4 %collective-permute-start.7 = (bf16[64,4224]{1,0:T(8,128)(2,1)S(1)}, bf16[64,4224]{1,0:T(8,128)(2,1)S(1)}, u32[]{:S(2)}, u32[]{:S(2)}) collective-permute-start(bf16[64,4224]{1,0:T(8,128)(2,1)S(1)} %collective-permute-done.5), channel_id=1, source_target_pairs={{0,32},{4,36},{8,40},{12,44},{16,48},{20,52},{24,56},{28,60},{32,0... | collective-permute-start | bytes 1622024 | tf_op jit(solution)/shard_map/ppermute | solution.py:61
  63.5 12.3 %collective-permute-start.8 = (bf16[64,2048]{1,0:T(8,128)(2,1)S(1)}, bf16[64,2048]{1,0:T(8,128)(2,1)S(1)}, u32[]{:S(2)}, u32[]{:S(2)}) collective-permute-start(bf16[64,2048]{1,0:T(8,128)(2,1)S(1)} %slice.190), channel_id=1, source_target_pairs={{0,32},{4,36},{8,40},{12,44},{16,48},{20,52},{24,56},{28,60},{32,0... | collective-permute-start | bytes 786440 | tf_op jit(solution)/shard_map/ppermute | solution.py:61
  66.9 8.8 %collective-permute-start.9 = (bf16[64,2176]{1,0:T(8,128)(2,1)S(1)}, bf16[64,2176]{1,0:T(8,128)(2,1)S(1)}, u32[]{:S(2)}, u32[]{:S(2)}) collective-permute-start(bf16[64,2176]{1,0:T(8,128)(2,1)S(1)} %slice.191), channel_id=1, source_target_pairs={{0,224},{4,228},{8,232},{12,236},{16,240},{20,244},{24,248},{28,25... | collective-permute-start | bytes 835592 | tf_op jit(solution)/shard_map/ppermute | solution.py:61
  77.5 7.7 %collective-permute-start.10 = (bf16[64,2048]{1,0:T(8,128)(2,1)S(1)}, bf16[64,2048]{1,0:T(8,128)(2,1)S(1)}, u32[]{:S(2)}, u32[]{:S(2)}) collective-permute-start(bf16[64,2048]{1,0:T(8,128)(2,1)S(1)} %get-tuple-element.36), channel_id=1, source_target_pairs={{0,32},{4,36},{8,40},{12,44},{16,48},{20,52},{24,56},{28,60},{32,0... | collective-permute-start | bytes 786440 | tf_op jit(solution)/shard_map/ppermute | solution.py:61
  82.7 8.3 %collective-permute-start.14 = (bf16[64,2048]{1,0:T(8,128)(2,1)S(1)}, bf16[64,2048]{1,0:T(8,128)(2,1)S(1)}, u32[]{:S(2)}, u32[]{:S(2)}) collective-permute-start(bf16[64,2048]{1,0:T(8,128)(2,1)S(1)} %get-tuple-element.37), channel_id=1, source_target_pairs={{0,224},{4,228},{8,232},{12,236},{16,240},{20,244},{24,248},{28,25... | collective-permute-start | bytes 786440 | tf_op jit(solution)/shard_map/ppermute | solution.py:61
  85.3 11.6 %collective-permute-start.11 = (bf16[64,4096]{1,0:T(8,128)(2,1)S(1)}, bf16[64,4096]{1,0:T(8,128)(2,1)S(1)}, u32[]{:S(2)}, u32[]{:S(2)}) collective-permute-start(bf16[64,4096]{1,0:T(8,128)(2,1)S(1)} %add_convert_fusion.5), channel_id=1, source_target_pairs={{0,224},{4,228},{8,232},{12,236},{16,240},{20,244},{24,248},{28,25... | collective-permute-start | bytes 1572872 | tf_op jit(solution)/shard_map/ppermute | solution.py:61
  91.1 10.2 %collective-permute-start.15 = (bf16[64,4096]{1,0:T(8,128)(2,1)S(1)}, bf16[64,4096]{1,0:T(8,128)(2,1)S(1)}, u32[]{:S(2)}, u32[]{:S(2)}) collective-permute-start(bf16[64,4096]{1,0:T(8,128)(2,1)S(1)} %add_convert_fusion.2), channel_id=1, source_target_pairs={{0,32},{4,36},{8,40},{12,44},{16,48},{20,52},{24,56},{28,60},{32,0... | collective-permute-start | bytes 1572872 | tf_op jit(solution)/shard_map/ppermute | solution.py:61
  97.0 9.9 %collective-permute-start.12 = (bf16[64,4096]{1,0:T(8,128)(2,1)S(1)}, bf16[64,4096]{1,0:T(8,128)(2,1)S(1)}, u32[]{:S(2)}, u32[]{:S(2)}) collective-permute-start(bf16[64,4096]{1,0:T(8,128)(2,1)S(1)} %add_convert_fusion.4), channel_id=1, source_target_pairs={{0,32},{4,36},{8,40},{12,44},{16,48},{20,52},{24,56},{28,60},{32,0... | collective-permute-start | bytes 1572872 | tf_op jit(solution)/shard_map/ppermute | solution.py:61
  101.4 11.1 %collective-permute-start.16 = (bf16[64,4096]{1,0:T(8,128)(2,1)S(1)}, bf16[64,4096]{1,0:T(8,128)(2,1)S(1)}, u32[]{:S(2)}, u32[]{:S(2)}) collective-permute-start(bf16[64,4096]{1,0:T(8,128)(2,1)S(1)} %add_convert_fusion.1), channel_id=1, source_target_pairs={{0,224},{4,228},{8,232},{12,236},{16,240},{20,244},{24,248},{28,25... | collective-permute-start | bytes 1572872 | tf_op jit(solution)/shard_map/ppermute | solution.py:61
  107.1 11.4 %collective-permute-start.13 = (bf16[64,4096]{1,0:T(8,128)(2,1)S(1)}, bf16[64,4096]{1,0:T(8,128)(2,1)S(1)}, u32[]{:S(2)}, u32[]{:S(2)}) collective-permute-start(bf16[64,4096]{1,0:T(8,128)(2,1)S(1)} %add_convert_fusion.3), channel_id=1, source_target_pairs={{0,224},{4,228},{8,232},{12,236},{16,240},{20,244},{24,248},{28,25... | collective-permute-start | bytes 1572872 | tf_op jit(solution)/shard_map/ppermute | solution.py:61
  112.7 10.2 %collective-permute-start.17 = (bf16[64,4096]{1,0:T(8,128)(2,1)S(1)}, bf16[64,4096]{1,0:T(8,128)(2,1)S(1)}, u32[]{:S(2)}, u32[]{:S(2)}) collective-permute-start(bf16[64,4096]{1,0:T(8,128)(2,1)S(1)} %add_convert_fusion), channel_id=1, source_target_pairs={{0,32},{4,36},{8,40},{12,44},{16,48},{20,52},{24,56},{28,60},{32,0... | collective-permute-start | bytes 1572872 | tf_op jit(solution)/shard_map/ppermute | solution.py:61
  137.3 14.0 %collective-permute-start.18 = (bf16[8,4096]{1,0:T(8,128)(2,1)S(1)}, bf16[8,4096]{1,0:T(8,128)(2,1)S(1)}, u32[]{:S(2)}, u32[]{:S(2)}) collective-permute-start(bf16[8,4096]{1,0:T(8,128)(2,1)S(1)} %reduce_sum.72), channel_id=1, source_target_pairs={{0,256},{256,0},{1,257},{257,1},{2,258},{258,2},{3,259},{259,3},{4... | collective-permute-start | bytes 196616 | tf_op jit(solution)/shard_map/ppermute | solution.py:121

commit v3 on v2

--- a/solution.py
+++ b/solution.py
@@ -33,6 +33,7 @@
     device_count = lax.axis_size("dev")
     groups = line_groups()
     odd_pairs, even_pairs = neighbour_swap(1), neighbour_swap(0)
+    opposite = second_axis(lambda c: (c + SIDE // 2) % SIDE)
     pool = lax.axis_index("pool")
     expert = lax.axis_index("dev") * EXPERTS // device_count
     row_count, width = moe_rows.shape
@@ -61,14 +62,14 @@
         return lax.ppermute(to_one, AXES, pairs[0]), lax.ppermute(to_two, AXES, pairs[1])
 
     one_in, two_in = [own], [own]
+    far = lax.ppermute(own, AXES, opposite)
     for step in range(1, REACH + 1):
-        from_one, from_two = swap_both(one_in[-1], two_in[-1], step)
+        to_one, to_two = one_in[-1], two_in[-1]
+        if step == REACH:
+            to_one, far = lax.optimization_barrier((to_one, far))
+        from_one, from_two = swap_both(to_one, to_two, step)
         one_in.append(from_one)
         two_in.append(from_two)
-    middle_column = width // 2
-    to_one = one_in[-1][:, :middle_column]
-    _, to_two = lax.optimization_barrier((to_one, two_in[-1][:, middle_column:]))
-    far = jnp.concatenate(swap_both(to_one, to_two, REACH + 1), axis=1)
 
     gate_part, up_part, down, _ = lax.optimization_barrier(
         (gate_weight[0], up_weight[0], down_weight[0], own)
@@ -93,17 +94,24 @@
         return out * column[:, None]
 
     size = SIDE * half
+    middle_column = width // 2
     far_part = part_of(far).astype(jnp.bfloat16)
     from_one, from_two = swap_both(
         far_part[:, :middle_column], far_part[:, middle_column:], REACH + 1
     )
+    parts = [None]
+    for step in range(1, REACH):
+        parts.append(part_of(jnp.concatenate([one_in[step], two_in[step]], axis=0)))
+    last_one, last_two, from_one, from_two, parts[1], parts[2] = lax.optimization_barrier(
+        (one_in[REACH], two_in[REACH], from_one, from_two, parts[1], parts[2])
+    )
+    parts.append(part_of(jnp.concatenate([last_one, last_two], axis=0)))
     from_one = jnp.pad(from_one, ((0, 0), (0, width - middle_column)))
     from_two = jnp.pad(from_two, ((0, 0), (middle_column, 0)))
     for step in range(REACH, 0, -1):
-        parts = part_of(jnp.concatenate([one_in[step], two_in[step]], axis=0))
-        part_one, part_two = lax.optimization_barrier((parts[:size], parts[size:]))
-        one_sum = part_one + from_one.astype(jnp.float32)
-        two_sum = part_two + from_two.astype(jnp.float32)
+        one_part, two_part = lax.optimization_barrier((parts[step][:size], parts[step][size:]))
+        one_sum = one_part + from_one.astype(jnp.float32)
+        two_sum = two_part + from_two.astype(jnp.float32)
         from_one, from_two = swap_both(
             one_sum.astype(jnp.bfloat16), two_sum.astype(jnp.bfloat16), step
         )

time: 153 us -> 146 us (0.954)
  starting transfers between devices: 75.5 us -> 69.4 us
    ppermute x8 -> x7, waiting for transfers between devices: 16.9 us -> 4.99 us  [swap_both(): lax.ppermute(to_two, AXES, pairs[1])]
    ppermute x8 -> x7, starting transfers between devices: 32.3 us -> 23.3 us  [swap_both(): lax.ppermute(to_one, AXES, pairs[0])]
    ppermute x8 -> x7, waiting for transfers between devices: 16.9 us -> 24.2 us  [swap_both(): lax.ppermute(to_one, AXES, pairs[0])]
    ppermute x0 -> x1, starting transfers between devices: none -> 4.25 us  [body(): far = lax.ppermute(own, AXES, opposite)]
    ppermute x0 -> x1, waiting for transfers between devices: none -> 3.83 us  [body(): far = lax.ppermute(own, AXES, opposite)]
    ppermute x1, starting transfers between devices: 13.1 us -> 10.8 us  [body(): other = lax.ppermute(total, 'pool', SWAP)]
    ppermute x8 -> x7, starting transfers between devices: 18.2 us -> 18.2 us  [swap_both(): lax.ppermute(to_two, AXES, pairs[1])]
  transfers between devices with their start and end apart: 20 -> 19, of which waited for: 14 -> 12; matrix products, arithmetic and copies ran while one was open for 7% -> 6% of each run, Pallas kernels for 0% -> 0%
where the time goes in v3:
time: 146 us
  starting transfers between devices  69.4 us (48%)
  waiting for transfers between devices  46.3 us (32%)
  blocking collectives  14.3 us (10%)
  matrix products  8.54 us (6%)
  local copies, waits for them, and re-layouts  3.87 us (3%)
  other arithmetic  2.64 us (2%)
    ppermute x7, waiting for transfers between devices, swap_both(): lax.ppermute(to_one, AXES, pairs[0])  24.2 us
    ppermute x7, starting transfers between devices, swap_both(): lax.ppermute(to_one, AXES, pairs[0])  23.3 us
    ppermute x7, starting transfers between devices, swap_both(): lax.ppermute(to_two, AXES, pairs[1])  18.2 us
    all_to_all x1, blocking collectives, body(): lax.all_to_all(summed.astype(jnp.bfloat16).reshape(SIDE, half, width), AX...  14.3 us
    all_to_all x1, waiting for transfers between devices, body(): lax.all_to_all(spread, AXES, split_axis=0, concat_axis=0, tiled=True, axi...  12.3 us
    ppermute x1, starting transfers between devices, body(): other = lax.ppermute(total, 'pool', SWAP)  10.8 us
    all_to_all x1, starting transfers between devices, body(): lax.all_to_all(spread, AXES, split_axis=0, concat_axis=0, tiled=True, axi...  7.65 us
    ppermute x7, waiting for transfers between devices, swap_both(): lax.ppermute(to_two, AXES, pairs[1])  4.99 us
  transfers between devices with their start and end apart: 19, of which 12 were waited for; matrix products, arithmetic and copies ran while one was open for 6% of the time, Pallas kernels for 0%

profile of v3, /device:TPU:1, one launch (start us, length us, event | category | flops | bytes accessed | tf_op | source)
XLA Modules:
  0.0 145.5 jit_solution(17566078382220555694)
XLA Ops:
  0.0 0.9 copy.12
  0.9 0.8 copy.13
  1.9 0.8 fusion.30
  2.7 0.8 broadcast_in_dim.69
  3.6 7.7 %all-to-all-start = ((bf16[8,8,4224]{2,1,0:T(8,128)(2,1)}), bf16[8,8,4224]{2,1,0:T(8,128)(2,1)S(1)}, u32[]{:S(2)}, u32[]{:S(2)}) async-start(bf16[8,8,4224]{2,1,0:T(8,128)(2,1)} %broadcast_in_dim.69), calls=%async_computation | async-start | bytes 1081344 | tf_op jit(solution)/shard_map/all_to_all | solution.py:56
  11.2 12.3 %all-to-all-done = bf16[8,8,4224]{2,1,0:T(8,128)(2,1)S(1)} async-done(((bf16[8,8,4224]{2,1,0:T(8,128)(2,1)}), bf16[8,8,4224]{2,1,0:T(8,128)(2,1)S(1)}, u32[]{:S(2)}, u32[]{:S(2)}) %all-to-all-start) | async-done | bytes 540704 | tf_op jit(solution)/shard_map/all_to_all | solution.py:56
  23.5 10.7 %collective-permute-start.2 = (bf16[64,4224]{1,0:T(8,128)(2,1)S(1)}, bf16[64,4224]{1,0:T(8,128)(2,1)S(1)}, u32[]{:S(2)}, u32[]{:S(2)}) collective-permute-start(bf16[64,4224]{1,0:T(8,128)(2,1)S(1)} %bitcast.32), channel_id=1, source_target_pairs={{0,224},{4,228},{8,232},{12,236},{16,240},{20,244},{24,248},{28,25... | collective-permute-start | bytes 1622024 | tf_op jit(solution)/shard_map/ppermute | solution.py:62
  34.2 1.9 %collective-permute-start.6 = (bf16[64,4224]{1,0:T(8,128)(2,1)S(1)}, bf16[64,4224]{1,0:T(8,128)(2,1)S(1)}, u32[]{:S(2)}, u32[]{:S(2)}) collective-permute-start(bf16[64,4224]{1,0:T(8,128)(2,1)S(1)} %bitcast.33), channel_id=1, source_target_pairs={{0,32},{4,36},{8,40},{12,44},{16,48},{20,52},{24,56},{28,60},{32,0... | collective-permute-start | bytes 1622024 | tf_op jit(solution)/shard_map/ppermute | solution.py:62
  36.1 4.3 %collective-permute-start.4 = (bf16[64,4224]{1,0:T(8,128)(2,1)S(1)}, bf16[64,4224]{1,0:T(8,128)(2,1)S(1)}, u32[]{:S(2)}, u32[]{:S(2)}) collective-permute-start(bf16[64,4224]{1,0:T(8,128)(2,1)S(1)} %bitcast.34), channel_id=1, source_target_pairs={{0,128},{4,132},{8,136},{12,140},{16,144},{20,148},{24,152},{28,15... | collective-permute-start | bytes 1622024 | tf_op jit(solution)/shard_map/ppermute | solution.py:65
  40.9 3.3 %collective-permute-start = (bf16[4096,256]{1,0:T(8,128)(2,1)S(1)}, bf16[4096,256]{1,0:T(8,128)(2,1)S(1)}, u32[]{:S(2)}, u32[]{:S(2)}) collective-permute-start(bf16[4096,256]{1,0:T(8,128)(2,1)S(1)} %constant_dynamic-update-slice_fusion), channel_id=1, source_target_pairs={{0,256},{256,0},{1,257},{257,1},{2,258},{258,2},{3,259},{259,3},{4... | collective-permute-start | bytes 6291464 | tf_op jit(solution)/shard_map/ppermute | solution.py:78
  44.2 1.9 %collective-permute-start.1 = (bf16[128,4096]{1,0:T(8,128)(2,1)S(1)}, bf16[128,4096]{1,0:T(8,128)(2,1)S(1)}, u32[]{:S(2)}, u32[]{:S(2)}) collective-permute-start(bf16[128,4096]{1,0:T(8,128)(2,1)S(1)} %bitcast.26), channel_id=1, source_target_pairs={{0,256},{256,0},{1,257},{257,1},{2,258},{258,2},{3,259},{259,3},{4... | collective-permute-start | bytes 3145736 | tf_op jit(solution)/shard_map/ppermute | solution.py:79
  46.1 0.5 fusion.24
  46.6 2.3 %collective-permute-start.3 = (bf16[64,4224]{1,0:T(8,128)(2,1)S(1)}, bf16[64,4224]{1,0:T(8,128)(2,1)S(1)}, u32[]{:S(2)}, u32[]{:S(2)}) collective-permute-start(bf16[64,4224]{1,0:T(8,128)(2,1)S(1)} %collective-permute-done.2), channel_id=1, source_target_pairs={{0,32},{4,36},{8,40},{12,44},{16,48},{20,52},{24,56},{28,60},{32,0... | collective-permute-start | bytes 1622024 | tf_op jit(solution)/shard_map/ppermute | solution.py:62
  48.9 1.4 collective-permute-done.6
  50.4 1.9 %collective-permute-start.7 = (bf16[64,4224]{1,0:T(8,128)(2,1)S(1)}, bf16[64,4224]{1,0:T(8,128)(2,1)S(1)}, u32[]{:S(2)}, u32[]{:S(2)}) collective-permute-start(bf16[64,4224]{1,0:T(8,128)(2,1)S(1)} %collective-permute-done.6), channel_id=1, source_target_pairs={{0,224},{4,228},{8,232},{12,236},{16,240},{20,244},{24,248},{28,25... | collective-permute-start | bytes 1622024 | tf_op jit(solution)/shard_map/ppermute | solution.py:62
  52.4 0.4 fusion.20
  53.2 3.8 %collective-permute-done.4 = bf16[64,4224]{1,0:T(8,128)(2,1)S(1)} collective-permute-done((bf16[64,4224]{1,0:T(8,128)(2,1)S(1)}, bf16[64,4224]{1,0:T(8,128)(2,1)S(1)}, u32[]{:S(2)}, u32[]{:S(2)}) %collective-permute-start.4) | collective-permute-done | bytes 540704 | tf_op jit(solution)/shard_map/ppermute | solution.py:65
  57.1 5.0 %collective-permute-done.3 = bf16[64,4224]{1,0:T(8,128)(2,1)S(1)} collective-permute-done((bf16[64,4224]{1,0:T(8,128)(2,1)S(1)}, bf16[64,4224]{1,0:T(8,128)(2,1)S(1)}, u32[]{:S(2)}, u32[]{:S(2)}) %collective-permute-start.3) | collective-permute-done | bytes 540704 | tf_op jit(solution)/shard_map/ppermute | solution.py:62
  62.1 1.9 %collective-permute-start.5 = (bf16[64,4224]{1,0:T(8,128)(2,1)S(1)}, bf16[64,4224]{1,0:T(8,128)(2,1)S(1)}, u32[]{:S(2)}, u32[]{:S(2)}) collective-permute-start(bf16[64,4224]{1,0:T(8,128)(2,1)S(1)} %collective-permute-done.3), channel_id=1, source_target_pairs={{0,224},{4,228},{8,232},{12,236},{16,240},{20,244},{24,248},{28,25... | collective-permute-start | bytes 1622024 | tf_op jit(solution)/shard_map/ppermute | solution.py:62
  64.1 0.5 fusion.28
  64.6 2.3 %collective-permute-start.8 = (bf16[64,4224]{1,0:T(8,128)(2,1)S(1)}, bf16[64,4224]{1,0:T(8,128)(2,1)S(1)}, u32[]{:S(2)}, u32[]{:S(2)}) collective-permute-start(bf16[64,4224]{1,0:T(8,128)(2,1)S(1)} %collective-permute-done.7), channel_id=1, source_target_pairs={{0,32},{4,36},{8,40},{12,44},{16,48},{20,52},{24,56},{28,60},{32,0... | collective-permute-start | bytes 1622024 | tf_op jit(solution)/shard_map/ppermute | solution.py:62
  67.4 0.5 fusion.16
  68.3 0.5 fusion.26
  69.2 4.2 %collective-permute-start.10 = (bf16[64,2048]{1,0:T(8,128)(2,1)S(1)}, bf16[64,2048]{1,0:T(8,128)(2,1)S(1)}, u32[]{:S(2)}, u32[]{:S(2)}) collective-permute-start(bf16[64,2048]{1,0:T(8,128)(2,1)S(1)} %get-tuple-element.49), channel_id=1, source_target_pairs={{0,224},{4,228},{8,232},{12,236},{16,240},{20,244},{24,248},{28,25... | collective-permute-start | bytes 786440 | tf_op jit(solution)/shard_map/ppermute | solution.py:62
  73.4 1.9 %collective-permute-start.9 = (bf16[64,2048]{1,0:T(8,128)(2,1)S(1)}, bf16[64,2048]{1,0:T(8,128)(2,1)S(1)}, u32[]{:S(2)}, u32[]{:S(2)}) collective-permute-start(bf16[64,2048]{1,0:T(8,128)(2,1)S(1)} %get-tuple-element.50), channel_id=1, source_target_pairs={{0,32},{4,36},{8,40},{12,44},{16,48},{20,52},{24,56},{28,60},{32,0... | collective-permute-start | bytes 786440 | tf_op jit(solution)/shard_map/ppermute | solution.py:62
  75.3 0.4 fusion.14
  76.2 0.4 fusion.18
  77.5 3.3 %collective-permute-done.9 = bf16[64,2048]{1,0:T(8,128)(2,1)S(1)} collective-permute-done((bf16[64,2048]{1,0:T(8,128)(2,1)S(1)}, bf16[64,2048]{1,0:T(8,128)(2,1)S(1)}, u32[]{:S(2)}, u32[]{:S(2)}) %collective-permute-start.9) | collective-permute-done | bytes 262176 | tf_op jit(solution)/shard_map/ppermute | solution.py:62
  80.9 0.4 fusion.12
  81.9 0.4 fusion.10
  82.3 0.4 fusion
  83.0 2.3 %collective-permute-start.11 = (bf16[64,4096]{1,0:T(8,128)(2,1)S(1)}, bf16[64,4096]{1,0:T(8,128)(2,1)S(1)}, u32[]{:S(2)}, u32[]{:S(2)}) collective-permute-start(bf16[64,4096]{1,0:T(8,128)(2,1)S(1)} %add_convert_fusion.5), channel_id=1, source_target_pairs={{0,224},{4,228},{8,232},{12,236},{16,240},{20,244},{24,248},{28,25... | collective-permute-start | bytes 1572872 | tf_op jit(solution)/shard_map/ppermute | solution.py:62
  85.4 0.4 fusion.84
  85.9 1.9 %collective-permute-start.14 = (bf16[64,4096]{1,0:T(8,128)(2,1)S(1)}, bf16[64,4096]{1,0:T(8,128)(2,1)S(1)}, u32[]{:S(2)}, u32[]{:S(2)}) collective-permute-start(bf16[64,4096]{1,0:T(8,128)(2,1)S(1)} %add_convert_fusion.2), channel_id=1, source_target_pairs={{0,32},{4,36},{8,40},{12,44},{16,48},{20,52},{24,56},{28,60},{32,0... | collective-permute-start | bytes 1572872 | tf_op jit(solution)/shard_map/ppermute | solution.py:62
  87.8 6.7 %collective-permute-done.11 = bf16[64,4096]{1,0:T(8,128)(2,1)S(1)} collective-permute-done((bf16[64,4096]{1,0:T(8,128)(2,1)S(1)}, bf16[64,4096]{1,0:T(8,128)(2,1)S(1)}, u32[]{:S(2)}, u32[]{:S(2)}) %collective-permute-start.11) | collective-permute-done | bytes 524320 | tf_op jit(solution)/shard_map/ppermute | solution.py:62
  94.6 1.9 %collective-permute-start.12 = (bf16[64,4096]{1,0:T(8,128)(2,1)S(1)}, bf16[64,4096]{1,0:T(8,128)(2,1)S(1)}, u32[]{:S(2)}, u32[]{:S(2)}) collective-permute-start(bf16[64,4096]{1,0:T(8,128)(2,1)S(1)} %add_convert_fusion.4), channel_id=1, source_target_pairs={{0,32},{4,36},{8,40},{12,44},{16,48},{20,52},{24,56},{28,60},{32,0... | collective-permute-start | bytes 1572872 | tf_op jit(solution)/shard_map/ppermute | solution.py:62
  96.6 3.8 %collective-permute-start.15 = (bf16[64,4096]{1,0:T(8,128)(2,1)S(1)}, bf16[64,4096]{1,0:T(8,128)(2,1)S(1)}, u32[]{:S(2)}, u32[]{:S(2)}) collective-permute-start(bf16[64,4096]{1,0:T(8,128)(2,1)S(1)} %add_convert_fusion.1), channel_id=1, source_target_pairs={{0,224},{4,228},{8,232},{12,236},{16,240},{20,244},{24,248},{28,25... | collective-permute-start | bytes 1572872 | tf_op jit(solution)/shard_map/ppermute | solution.py:62
  100.4 4.4 %collective-permute-done.12 = bf16[64,4096]{1,0:T(8,128)(2,1)S(1)} collective-permute-done((bf16[64,4096]{1,0:T(8,128)(2,1)S(1)}, bf16[64,4096]{1,0:T(8,128)(2,1)S(1)}, u32[]{:S(2)}, u32[]{:S(2)}) %collective-permute-start.12) | collective-permute-done | bytes 524320 | tf_op jit(solution)/shard_map/ppermute | solution.py:62
  104.9 2.3 %collective-permute-start.13 = (bf16[64,4096]{1,0:T(8,128)(2,1)S(1)}, bf16[64,4096]{1,0:T(8,128)(2,1)S(1)}, u32[]{:S(2)}, u32[]{:S(2)}) collective-permute-start(bf16[64,4096]{1,0:T(8,128)(2,1)S(1)} %add_convert_fusion.3), channel_id=1, source_target_pairs={{0,224},{4,228},{8,232},{12,236},{16,240},{20,244},{24,248},{28,25... | collective-permute-start | bytes 1572872 | tf_op jit(solution)/shard_map/ppermute | solution.py:62
  107.2 0.8 collective-permute-done.15
  108.1 2.2 %collective-permute-start.16 = (bf16[64,4096]{1,0:T(8,128)(2,1)S(1)}, bf16[64,4096]{1,0:T(8,128)(2,1)S(1)}, u32[]{:S(2)}, u32[]{:S(2)}) collective-permute-start(bf16[64,4096]{1,0:T(8,128)(2,1)S(1)} %add_convert_fusion), channel_id=1, source_target_pairs={{0,32},{4,36},{8,40},{12,44},{16,48},{20,52},{24,56},{28,60},{32,0... | collective-permute-start | bytes 1572872 | tf_op jit(solution)/shard_map/ppermute | solution.py:62
  110.6 0.5 fusion.22
  111.1 4.9 %collective-permute-done.13 = bf16[64,4096]{1,0:T(8,128)(2,1)S(1)} collective-permute-done((bf16[64,4096]{1,0:T(8,128)(2,1)S(1)}, bf16[64,4096]{1,0:T(8,128)(2,1)S(1)}, u32[]{:S(2)}, u32[]{:S(2)}) %collective-permute-start.13) | collective-permute-done | bytes 524320 | tf_op jit(solution)/shard_map/ppermute | solution.py:62
  116.0 2.3 %collective-permute-done.16 = bf16[64,4096]{1,0:T(8,128)(2,1)S(1)} collective-permute-done((bf16[64,4096]{1,0:T(8,128)(2,1)S(1)}, bf16[64,4096]{1,0:T(8,128)(2,1)S(1)}, u32[]{:S(2)}, u32[]{:S(2)}) %collective-permute-start.16) | collective-permute-done | bytes 524320 | tf_op jit(solution)/shard_map/ppermute | solution.py:62
  118.8 14.3 %all_to_all.10 = bf16[8,8,4096]{2,1,0:T(8,128)(2,1)S(1)} all-to-all(bf16[8,8,4096]{2,1,0:T(8,128)(2,1)S(1)} %fusion.9), channel_id=1, replica_groups={{0,4,8,12,16,20,24,28},{32,36,40,44,48,52,56,60},{64,68,72,76,80,84,88,..., dimensions={0} | all-to-all | bytes 1048576 | tf_op jit(solution)/shard_map/all_to_all | solution.py:120
  133.1 10.8 %collective-permute-start.17 = (bf16[8,4096]{1,0:T(8,128)(2,1)S(1)}, bf16[8,4096]{1,0:T(8,128)(2,1)S(1)}, u32[]{:S(2)}, u32[]{:S(2)}) collective-permute-start(bf16[8,4096]{1,0:T(8,128)(2,1)S(1)} %reduce_sum.72), channel_id=1, source_target_pairs={{0,256},{256,0},{1,257},{257,1},{2,258},{258,2},{3,259},{259,3},{4... | collective-permute-start | bytes 196616 | tf_op jit(solution)/shard_map/ppermute | solution.py:129
  144.0 0.9 collective-permute-done.17
  144.8 0.7 pad_maximum_fusion
  (48 shorter events, 6.0 us)
Async XLA Ops:
  0.0 40.4 %copy-start.1 = (bf16[1,4096,128]{2,1,0:T(8,128)(2,1)S(1)}, bf16[1,4096,128]{2,1,0:T(8,128)(2,1)}, u32[]{:S(2)}) copy-start(bf16[1,4096,128]{2,1,0:T(8,128)(2,1)} %param.9) | copy-start | bytes 3145732
  0.0 40.6 %copy-start.2 = (bf16[1,4096,128]{2,1,0:T(8,128)(2,1)S(1)}, bf16[1,4096,128]{2,1,0:T(8,128)(2,1)}, u32[]{:S(2)}) copy-start(bf16[1,4096,128]{2,1,0:T(8,128)(2,1)} %param.10) | copy-start | bytes 3145732
  3.6 20.0 %all-to-all-start = ((bf16[8,8,4224]{2,1,0:T(8,128)(2,1)}), bf16[8,8,4224]{2,1,0:T(8,128)(2,1)S(1)}, u32[]{:S(2)}, u32[]{:S(2)}) async-start(bf16[8,8,4224]{2,1,0:T(8,128)(2,1)} %broadcast_in_dim.69), calls=%async_computation | async-start | bytes 1081344 | tf_op jit(solution)/shard_map/all_to_all | solution.py:56
  23.5 23.1 %collective-permute-start.2 = (bf16[64,4224]{1,0:T(8,128)(2,1)S(1)}, bf16[64,4224]{1,0:T(8,128)(2,1)S(1)}, u32[]{:S(2)}, u32[]{:S(2)}) collective-permute-start(bf16[64,4224]{1,0:T(8,128)(2,1)S(1)} %bitcast.32), channel_id=1, source_target_pairs={{0,224},{4,228},{8,232},{12,236},{16,240},{20,244},{24,248},{28,25... | collective-permute-start | bytes 1622024 | tf_op jit(solution)/shard_map/ppermute | solution.py:62
  34.2 16.2 %collective-permute-start.6 = (bf16[64,4224]{1,0:T(8,128)(2,1)S(1)}, bf16[64,4224]{1,0:T(8,128)(2,1)S(1)}, u32[]{:S(2)}, u32[]{:S(2)}) collective-permute-start(bf16[64,4224]{1,0:T(8,128)(2,1)S(1)} %bitcast.33), channel_id=1, source_target_pairs={{0,32},{4,36},{8,40},{12,44},{16,48},{20,52},{24,56},{28,60},{32,0... | collective-permute-start | bytes 1622024 | tf_op jit(solution)/shard_map/ppermute | solution.py:62
  36.1 20.9 %collective-permute-start.4 = (bf16[64,4224]{1,0:T(8,128)(2,1)S(1)}, bf16[64,4224]{1,0:T(8,128)(2,1)S(1)}, u32[]{:S(2)}, u32[]{:S(2)}) collective-permute-start(bf16[64,4224]{1,0:T(8,128)(2,1)S(1)} %bitcast.34), channel_id=1, source_target_pairs={{0,128},{4,132},{8,136},{12,140},{16,144},{20,148},{24,152},{28,15... | collective-permute-start | bytes 1622024 | tf_op jit(solution)/shard_map/ppermute | solution.py:65
  40.4 3.8 %copy-start = (bf16[1,128,4096]{2,1,0:T(8,128)(2,1)S(1)}, bf16[1,128,4096]{2,1,0:T(8,128)(2,1)}, u32[]{:S(2)}) copy-start(bf16[1,128,4096]{2,1,0:T(8,128)(2,1)} %param.11) | copy-start | bytes 3145732
  40.9 27.4 %collective-permute-start = (bf16[4096,256]{1,0:T(8,128)(2,1)S(1)}, bf16[4096,256]{1,0:T(8,128)(2,1)S(1)}, u32[]{:S(2)}, u32[]{:S(2)}) collective-permute-start(bf16[4096,256]{1,0:T(8,128)(2,1)S(1)} %constant_dynamic-update-slice_fusion), channel_id=1, source_target_pairs={{0,256},{256,0},{1,257},{257,1},{2,258},{258,2},{3,259},{259,3},{4... | collective-permute-start | bytes 6291464 | tf_op jit(solution)/shard_map/ppermute | solution.py:78
  44.2 24.6 %collective-permute-start.1 = (bf16[128,4096]{1,0:T(8,128)(2,1)S(1)}, bf16[128,4096]{1,0:T(8,128)(2,1)S(1)}, u32[]{:S(2)}, u32[]{:S(2)}) collective-permute-start(bf16[128,4096]{1,0:T(8,128)(2,1)S(1)} %bitcast.26), channel_id=1, source_target_pairs={{0,256},{256,0},{1,257},{257,1},{2,258},{258,2},{3,259},{259,3},{4... | collective-permute-start | bytes 3145736 | tf_op jit(solution)/shard_map/ppermute | solution.py:79
  46.6 15.5 %collective-permute-start.3 = (bf16[64,4224]{1,0:T(8,128)(2,1)S(1)}, bf16[64,4224]{1,0:T(8,128)(2,1)S(1)}, u32[]{:S(2)}, u32[]{:S(2)}) collective-permute-start(bf16[64,4224]{1,0:T(8,128)(2,1)S(1)} %collective-permute-done.2), channel_id=1, source_target_pairs={{0,32},{4,36},{8,40},{12,44},{16,48},{20,52},{24,56},{28,60},{32,0... | collective-permute-start | bytes 1622024 | tf_op jit(solution)/shard_map/ppermute | solution.py:62
  50.4 14.2 %collective-permute-start.7 = (bf16[64,4224]{1,0:T(8,128)(2,1)S(1)}, bf16[64,4224]{1,0:T(8,128)(2,1)S(1)}, u32[]{:S(2)}, u32[]{:S(2)}) collective-permute-start(bf16[64,4224]{1,0:T(8,128)(2,1)S(1)} %collective-permute-done.6), channel_id=1, source_target_pairs={{0,224},{4,228},{8,232},{12,236},{16,240},{20,244},{24,248},{28,25... | collective-permute-start | bytes 1622024 | tf_op jit(solution)/shard_map/ppermute | solution.py:62
  62.1 15.0 %collective-permute-start.5 = (bf16[64,4224]{1,0:T(8,128)(2,1)S(1)}, bf16[64,4224]{1,0:T(8,128)(2,1)S(1)}, u32[]{:S(2)}, u32[]{:S(2)}) collective-permute-start(bf16[64,4224]{1,0:T(8,128)(2,1)S(1)} %collective-permute-done.3), channel_id=1, source_target_pairs={{0,224},{4,228},{8,232},{12,236},{16,240},{20,244},{24,248},{28,25... | collective-permute-start | bytes 1622024 | tf_op jit(solution)/shard_map/ppermute | solution.py:62
  64.6 12.5 %collective-permute-start.8 = (bf16[64,4224]{1,0:T(8,128)(2,1)S(1)}, bf16[64,4224]{1,0:T(8,128)(2,1)S(1)}, u32[]{:S(2)}, u32[]{:S(2)}) collective-permute-start(bf16[64,4224]{1,0:T(8,128)(2,1)S(1)} %collective-permute-done.7), channel_id=1, source_target_pairs={{0,32},{4,36},{8,40},{12,44},{16,48},{20,52},{24,56},{28,60},{32,0... | collective-permute-start | bytes 1622024 | tf_op jit(solution)/shard_map/ppermute | solution.py:62
  69.2 8.3 %collective-permute-start.10 = (bf16[64,2048]{1,0:T(8,128)(2,1)S(1)}, bf16[64,2048]{1,0:T(8,128)(2,1)S(1)}, u32[]{:S(2)}, u32[]{:S(2)}) collective-permute-start(bf16[64,2048]{1,0:T(8,128)(2,1)S(1)} %get-tuple-element.49), channel_id=1, source_target_pairs={{0,224},{4,228},{8,232},{12,236},{16,240},{20,244},{24,248},{28,25... | collective-permute-start | bytes 786440 | tf_op jit(solution)/shard_map/ppermute | solution.py:62
  73.4 7.4 %collective-permute-start.9 = (bf16[64,2048]{1,0:T(8,128)(2,1)S(1)}, bf16[64,2048]{1,0:T(8,128)(2,1)S(1)}, u32[]{:S(2)}, u32[]{:S(2)}) collective-permute-start(bf16[64,2048]{1,0:T(8,128)(2,1)S(1)} %get-tuple-element.50), channel_id=1, source_target_pairs={{0,32},{4,36},{8,40},{12,44},{16,48},{20,52},{24,56},{28,60},{32,0... | collective-permute-start | bytes 786440 | tf_op jit(solution)/shard_map/ppermute | solution.py:62
  83.0 11.4 %collective-permute-start.11 = (bf16[64,4096]{1,0:T(8,128)(2,1)S(1)}, bf16[64,4096]{1,0:T(8,128)(2,1)S(1)}, u32[]{:S(2)}, u32[]{:S(2)}) collective-permute-start(bf16[64,4096]{1,0:T(8,128)(2,1)S(1)} %add_convert_fusion.5), channel_id=1, source_target_pairs={{0,224},{4,228},{8,232},{12,236},{16,240},{20,244},{24,248},{28,25... | collective-permute-start | bytes 1572872 | tf_op jit(solution)/shard_map/ppermute | solution.py:62
  85.9 10.6 %collective-permute-start.14 = (bf16[64,4096]{1,0:T(8,128)(2,1)S(1)}, bf16[64,4096]{1,0:T(8,128)(2,1)S(1)}, u32[]{:S(2)}, u32[]{:S(2)}) collective-permute-start(bf16[64,4096]{1,0:T(8,128)(2,1)S(1)} %add_convert_fusion.2), channel_id=1, source_target_pairs={{0,32},{4,36},{8,40},{12,44},{16,48},{20,52},{24,56},{28,60},{32,0... | collective-permute-start | bytes 1572872 | tf_op jit(solution)/shard_map/ppermute | solution.py:62
  94.6 10.2 %collective-permute-start.12 = (bf16[64,4096]{1,0:T(8,128)(2,1)S(1)}, bf16[64,4096]{1,0:T(8,128)(2,1)S(1)}, u32[]{:S(2)}, u32[]{:S(2)}) collective-permute-start(bf16[64,4096]{1,0:T(8,128)(2,1)S(1)} %add_convert_fusion.4), channel_id=1, source_target_pairs={{0,32},{4,36},{8,40},{12,44},{16,48},{20,52},{24,56},{28,60},{32,0... | collective-permute-start | bytes 1572872 | tf_op jit(solution)/shard_map/ppermute | solution.py:62
  96.6 11.4 %collective-permute-start.15 = (bf16[64,4096]{1,0:T(8,128)(2,1)S(1)}, bf16[64,4096]{1,0:T(8,128)(2,1)S(1)}, u32[]{:S(2)}, u32[]{:S(2)}) collective-permute-start(bf16[64,4096]{1,0:T(8,128)(2,1)S(1)} %add_convert_fusion.1), channel_id=1, source_target_pairs={{0,224},{4,228},{8,232},{12,236},{16,240},{20,244},{24,248},{28,25... | collective-permute-start | bytes 1572872 | tf_op jit(solution)/shard_map/ppermute | solution.py:62
  104.9 11.1 %collective-permute-start.13 = (bf16[64,4096]{1,0:T(8,128)(2,1)S(1)}, bf16[64,4096]{1,0:T(8,128)(2,1)S(1)}, u32[]{:S(2)}, u32[]{:S(2)}) collective-permute-start(bf16[64,4096]{1,0:T(8,128)(2,1)S(1)} %add_convert_fusion.3), channel_id=1, source_target_pairs={{0,224},{4,228},{8,232},{12,236},{16,240},{20,244},{24,248},{28,25... | collective-permute-start | bytes 1572872 | tf_op jit(solution)/shard_map/ppermute | solution.py:62
  108.1 10.2 %collective-permute-start.16 = (bf16[64,4096]{1,0:T(8,128)(2,1)S(1)}, bf16[64,4096]{1,0:T(8,128)(2,1)S(1)}, u32[]{:S(2)}, u32[]{:S(2)}) collective-permute-start(bf16[64,4096]{1,0:T(8,128)(2,1)S(1)} %add_convert_fusion), channel_id=1, source_target_pairs={{0,32},{4,36},{8,40},{12,44},{16,48},{20,52},{24,56},{28,60},{32,0... | collective-permute-start | bytes 1572872 | tf_op jit(solution)/shard_map/ppermute | solution.py:62
  133.1 11.7 %collective-permute-start.17 = (bf16[8,4096]{1,0:T(8,128)(2,1)S(1)}, bf16[8,4096]{1,0:T(8,128)(2,1)S(1)}, u32[]{:S(2)}, u32[]{:S(2)}) collective-permute-start(bf16[8,4096]{1,0:T(8,128)(2,1)S(1)} %reduce_sum.72), channel_id=1, source_target_pairs={{0,256},{256,0},{1,257},{257,1},{2,258},{258,2},{3,259},{259,3},{4... | collective-permute-start | bytes 196616 | tf_op jit(solution)/shard_map/ppermute | solution.py:129

commit v4 on v3

--- a/solution.py
+++ b/solution.py
@@ -62,14 +62,13 @@
         return lax.ppermute(to_one, AXES, pairs[0]), lax.ppermute(to_two, AXES, pairs[1])
 
     one_in, two_in = [own], [own]
-    far = lax.ppermute(own, AXES, opposite)
     for step in range(1, REACH + 1):
         to_one, to_two = one_in[-1], two_in[-1]
-        if step == REACH:
-            to_one, far = lax.optimization_barrier((to_one, far))
         from_one, from_two = swap_both(to_one, to_two, step)
         one_in.append(from_one)
         two_in.append(from_two)
+
+    far = lax.ppermute(one_in[REACH], AXES, even_pairs)
 
     gate_part, up_part, down, _ = lax.optimization_barrier(
         (gate_weight[0], up_weight[0], down_weight[0], own)
@@ -94,28 +93,26 @@
         return out * column[:, None]
 
     size = SIDE * half
-    middle_column = width // 2
-    far_part = part_of(far).astype(jnp.bfloat16)
-    from_one, from_two = swap_both(
-        far_part[:, :middle_column], far_part[:, middle_column:], REACH + 1
-    )
     parts = [None]
     for step in range(1, REACH):
         parts.append(part_of(jnp.concatenate([one_in[step], two_in[step]], axis=0)))
-    last_one, last_two, from_one, from_two, parts[1], parts[2] = lax.optimization_barrier(
-        (one_in[REACH], two_in[REACH], from_one, from_two, parts[1], parts[2])
+    last_one, last_two, parts[1], parts[2] = lax.optimization_barrier(
+        (one_in[REACH], two_in[REACH], parts[1], parts[2])
     )
     parts.append(part_of(jnp.concatenate([last_one, last_two], axis=0)))
-    from_one = jnp.pad(from_one, ((0, 0), (0, width - middle_column)))
-    from_two = jnp.pad(from_two, ((0, 0), (middle_column, 0)))
+    far_part = part_of(far).astype(jnp.bfloat16)
+    from_far = lax.ppermute(far_part, AXES, opposite)
+    from_one = from_two = None
     for step in range(REACH, 0, -1):
-        one_part, two_part = lax.optimization_barrier((parts[step][:size], parts[step][size:]))
-        one_sum = one_part + from_one.astype(jnp.float32)
-        two_sum = two_part + from_two.astype(jnp.float32)
+        one_sum, two_sum = lax.optimization_barrier((parts[step][:size], parts[step][size:]))
+        if step < REACH:
+            one_sum = one_sum + from_one.astype(jnp.float32)
+            two_sum = two_sum + from_two.astype(jnp.float32)
         from_one, from_two = swap_both(
             one_sum.astype(jnp.bfloat16), two_sum.astype(jnp.bfloat16), step
         )
-    summed = part_of(own) + from_one.astype(jnp.float32) + from_two.astype(jnp.float32)
+    own_sum = part_of(own) + from_far.astype(jnp.float32)
+    summed = own_sum + from_one.astype(jnp.float32) + from_two.astype(jnp.float32)
 
     returned = lax.all_to_all(
         summed.astype(jnp.bfloat16).reshape(SIDE, half, width),

time: 146 us -> 142 us (0.973)
  waiting for transfers between devices: 46.3 us -> 41.2 us
  blocking collectives: 14.3 us -> 15.9 us
    ppermute x7 -> x6, starting transfers between devices: 18.2 us -> 13.7 us  [swap_both(): lax.ppermute(to_two, AXES, pairs[1])]
    ppermute x1 -> x2, waiting for transfers between devices: 3.83 us -> 0.01 us  [the longest x1 0.01 us: body(): far = lax.ppermute(one_in[REACH], AXES, even_pairs)]
    ppermute x1 -> x2, starting transfers between devices: 4.25 us -> 7.56 us  [the longest x1 5.42 us: body(): from_far = lax.ppermute(far_part, AXES, opposite)]
    ppermute x7 -> x6, starting transfers between devices: 23.3 us -> 26.5 us  [swap_both(): lax.ppermute(to_one, AXES, pairs[0])]
    ppermute x7 -> x6, waiting for transfers between devices: 4.99 us -> 2.51 us  [swap_both(): lax.ppermute(to_two, AXES, pairs[1])]
    ppermute x1, starting transfers between devices: 10.8 us -> 8.98 us  [body(): other = lax.ppermute(total, 'pool', SWAP)]
    all_to_all x1, blocking collectives: 14.3 us -> 15.9 us  [body(): lax.all_to_all(summed.astype(jnp.bfloat16).reshape(SIDE, half, width), AX...]
    ppermute x7 -> x6, waiting for transfers between devices: 24.2 us -> 25.5 us  [swap_both(): lax.ppermute(to_one, AXES, pairs[0])]
  transfers between devices with their start and end apart: 19 -> 18, of which waited for: 12 -> 8; matrix products, arithmetic and copies ran while one was open for 6% -> 7% of each run, Pallas kernels for 0% -> 0%
where the time goes in v4:
time: 142 us; the launch traced here: 141 us
  starting transfers between devices  68.7 us (48%)
  waiting for transfers between devices  41.2 us (29%)
  blocking collectives  15.9 us (11%)
  matrix products  8.64 us (6%)
  local copies, waits for them, and re-layouts  3.73 us (3%)
  other arithmetic  2.49 us (2%)
    ppermute x6, starting transfers between devices, swap_both(): lax.ppermute(to_one, AXES, pairs[0])  26.5 us
    ppermute x6, waiting for transfers between devices, swap_both(): lax.ppermute(to_one, AXES, pairs[0])  25.5 us
    all_to_all x1, blocking collectives, body(): lax.all_to_all(summed.astype(jnp.bfloat16).reshape(SIDE, half, width), AX...  15.9 us
    ppermute x6, starting transfers between devices, swap_both(): lax.ppermute(to_two, AXES, pairs[1])  13.7 us
    all_to_all x1, waiting for transfers between devices, body(): lax.all_to_all(spread, AXES, split_axis=0, concat_axis=0, tiled=True, axi...  12.3 us
    ppermute x1, starting transfers between devices, body(): other = lax.ppermute(total, 'pool', SWAP)  8.98 us
    all_to_all x1, starting transfers between devices, body(): lax.all_to_all(spread, AXES, split_axis=0, concat_axis=0, tiled=True, axi...  7.65 us
    ppermute x1, starting transfers between devices, body(): from_far = lax.ppermute(far_part, AXES, opposite)  5.42 us
  transfers between devices with their start and end apart: 18, of which 8 were waited for; matrix products, arithmetic and copies ran while one was open for 7% of the time, Pallas kernels for 0%

profile of v4, /device:TPU:1, one launch (start us, length us, event | category | flops | bytes accessed | tf_op | source)
XLA Modules:
  0.0 141.2 jit_solution(1714945183608298188)
XLA Ops:
  0.0 0.9 copy.12
  0.9 0.8 copy.13
  1.9 0.8 fusion.29
  2.7 0.8 broadcast_in_dim.69
  3.6 7.7 %all-to-all-start = ((bf16[8,8,4224]{2,1,0:T(8,128)(2,1)}), bf16[8,8,4224]{2,1,0:T(8,128)(2,1)S(1)}, u32[]{:S(2)}, u32[]{:S(2)}) async-start(bf16[8,8,4224]{2,1,0:T(8,128)(2,1)} %broadcast_in_dim.69), calls=%async_computation | async-start | bytes 1081344 | tf_op jit(solution)/shard_map/all_to_all | solution.py:56
  11.2 12.3 %all-to-all-done = bf16[8,8,4224]{2,1,0:T(8,128)(2,1)S(1)} async-done(((bf16[8,8,4224]{2,1,0:T(8,128)(2,1)}), bf16[8,8,4224]{2,1,0:T(8,128)(2,1)S(1)}, u32[]{:S(2)}, u32[]{:S(2)}) %all-to-all-start) | async-done | bytes 540704 | tf_op jit(solution)/shard_map/all_to_all | solution.py:56
  23.5 10.7 %collective-permute-start.2 = (bf16[64,4224]{1,0:T(8,128)(2,1)S(1)}, bf16[64,4224]{1,0:T(8,128)(2,1)S(1)}, u32[]{:S(2)}, u32[]{:S(2)}) collective-permute-start(bf16[64,4224]{1,0:T(8,128)(2,1)S(1)} %bitcast.32), channel_id=1, source_target_pairs={{0,224},{4,228},{8,232},{12,236},{16,240},{20,244},{24,248},{28,25... | collective-permute-start | bytes 1622024 | tf_op jit(solution)/shard_map/ppermute | solution.py:62
  34.2 1.9 %collective-permute-start.7 = (bf16[64,4224]{1,0:T(8,128)(2,1)S(1)}, bf16[64,4224]{1,0:T(8,128)(2,1)S(1)}, u32[]{:S(2)}, u32[]{:S(2)}) collective-permute-start(bf16[64,4224]{1,0:T(8,128)(2,1)S(1)} %bitcast.33), channel_id=1, source_target_pairs={{0,32},{4,36},{8,40},{12,44},{16,48},{20,52},{24,56},{28,60},{32,0... | collective-permute-start | bytes 1622024 | tf_op jit(solution)/shard_map/ppermute | solution.py:62
  36.6 1.9 %collective-permute-start = (bf16[4096,256]{1,0:T(8,128)(2,1)S(1)}, bf16[4096,256]{1,0:T(8,128)(2,1)S(1)}, u32[]{:S(2)}, u32[]{:S(2)}) collective-permute-start(bf16[4096,256]{1,0:T(8,128)(2,1)S(1)} %constant_dynamic-update-slice_fusion), channel_id=1, source_target_pairs={{0,256},{256,0},{1,257},{257,1},{2,258},{258,2},{3,259},{259,3},{4... | collective-permute-start | bytes 6291464 | tf_op jit(solution)/shard_map/ppermute | solution.py:77
  38.6 2.4 %collective-permute-start.1 = (bf16[128,4096]{1,0:T(8,128)(2,1)S(1)}, bf16[128,4096]{1,0:T(8,128)(2,1)S(1)}, u32[]{:S(2)}, u32[]{:S(2)}) collective-permute-start(bf16[128,4096]{1,0:T(8,128)(2,1)S(1)} %bitcast.26), channel_id=1, source_target_pairs={{0,256},{256,0},{1,257},{257,1},{2,258},{258,2},{3,259},{259,3},{4... | collective-permute-start | bytes 3145736 | tf_op jit(solution)/shard_map/ppermute | solution.py:78
  41.0 0.5 fusion.27
  41.5 3.4 %collective-permute-start.3 = (bf16[64,4224]{1,0:T(8,128)(2,1)S(1)}, bf16[64,4224]{1,0:T(8,128)(2,1)S(1)}, u32[]{:S(2)}, u32[]{:S(2)}) collective-permute-start(bf16[64,4224]{1,0:T(8,128)(2,1)S(1)} %collective-permute-done.2), channel_id=1, source_target_pairs={{0,32},{4,36},{8,40},{12,44},{16,48},{20,52},{24,56},{28,60},{32,0... | collective-permute-start | bytes 1622024 | tf_op jit(solution)/shard_map/ppermute | solution.py:62
  44.9 2.6 %collective-permute-start.8 = (bf16[64,4224]{1,0:T(8,128)(2,1)S(1)}, bf16[64,4224]{1,0:T(8,128)(2,1)S(1)}, u32[]{:S(2)}, u32[]{:S(2)}) collective-permute-start(bf16[64,4224]{1,0:T(8,128)(2,1)S(1)} %collective-permute-done.7), channel_id=1, source_target_pairs={{0,224},{4,228},{8,232},{12,236},{16,240},{20,244},{24,248},{28,25... | collective-permute-start | bytes 1622024 | tf_op jit(solution)/shard_map/ppermute | solution.py:62
  47.5 0.4 fusion.19
  48.0 0.4 fusion.36
  48.4 3.4 %collective-permute-done.3 = bf16[64,4224]{1,0:T(8,128)(2,1)S(1)} collective-permute-done((bf16[64,4224]{1,0:T(8,128)(2,1)S(1)}, bf16[64,4224]{1,0:T(8,128)(2,1)S(1)}, u32[]{:S(2)}, u32[]{:S(2)}) %collective-permute-start.3) | collective-permute-done | bytes 540704 | tf_op jit(solution)/shard_map/ppermute | solution.py:62
  51.9 4.0 %collective-permute-start.4 = (bf16[64,4224]{1,0:T(8,128)(2,1)S(1)}, bf16[64,4224]{1,0:T(8,128)(2,1)S(1)}, u32[]{:S(2)}, u32[]{:S(2)}) collective-permute-start(bf16[64,4224]{1,0:T(8,128)(2,1)S(1)} %collective-permute-done.3), channel_id=1, source_target_pairs={{0,224},{4,228},{8,232},{12,236},{16,240},{20,244},{24,248},{28,25... | collective-permute-start | bytes 1622024 | tf_op jit(solution)/shard_map/ppermute | solution.py:62
  55.9 0.6 collective-permute-done.8
  56.5 1.9 %collective-permute-start.9 = (bf16[64,4224]{1,0:T(8,128)(2,1)S(1)}, bf16[64,4224]{1,0:T(8,128)(2,1)S(1)}, u32[]{:S(2)}, u32[]{:S(2)}) collective-permute-start(bf16[64,4224]{1,0:T(8,128)(2,1)S(1)} %collective-permute-done.8), channel_id=1, source_target_pairs={{0,32},{4,36},{8,40},{12,44},{16,48},{20,52},{24,56},{28,60},{32,0... | collective-permute-start | bytes 1622024 | tf_op jit(solution)/shard_map/ppermute | solution.py:62
  58.6 0.5 fusion.15
  59.5 3.9 %collective-permute-done.4 = bf16[64,4224]{1,0:T(8,128)(2,1)S(1)} collective-permute-done((bf16[64,4224]{1,0:T(8,128)(2,1)S(1)}, bf16[64,4224]{1,0:T(8,128)(2,1)S(1)}, u32[]{:S(2)}, u32[]{:S(2)}) %collective-permute-start.4) | collective-permute-done | bytes 540704 | tf_op jit(solution)/shard_map/ppermute | solution.py:62
  63.4 2.1 %collective-permute-start.5 = (bf16[64,4224]{1,0:T(8,128)(2,1)S(1)}, bf16[64,4224]{1,0:T(8,128)(2,1)S(1)}, u32[]{:S(2)}, u32[]{:S(2)}) collective-permute-start(bf16[64,4224]{1,0:T(8,128)(2,1)S(1)} %collective-permute-done.4), channel_id=1, source_target_pairs={{0,32},{4,36},{8,40},{12,44},{16,48},{20,52},{24,56},{28,60},{32,0... | collective-permute-start | bytes 1622024 | tf_op jit(solution)/shard_map/ppermute | solution.py:71
  65.6 0.4 fusion.13
  66.1 0.4 fusion.1
  66.5 0.4 fusion.17
  67.5 0.4 fusion.11
  68.1 0.4 fusion.42
  68.5 0.4 fusion.9
  69.0 0.5 fusion
  69.5 3.6 %collective-permute-start.10 = (bf16[64,4096]{1,0:T(8,128)(2,1)S(1)}, bf16[64,4096]{1,0:T(8,128)(2,1)S(1)}, u32[]{:S(2)}, u32[]{:S(2)}) collective-permute-start(bf16[64,4096]{1,0:T(8,128)(2,1)S(1)} %get-tuple-element.27), channel_id=1, source_target_pairs={{0,224},{4,228},{8,232},{12,236},{16,240},{20,244},{24,248},{28,25... | collective-permute-start | bytes 1572872 | tf_op jit(solution)/shard_map/ppermute | solution.py:62
  73.1 0.4 fusion.84
  73.5 1.9 %collective-permute-start.13 = (bf16[64,4096]{1,0:T(8,128)(2,1)S(1)}, bf16[64,4096]{1,0:T(8,128)(2,1)S(1)}, u32[]{:S(2)}, u32[]{:S(2)}) collective-permute-start(bf16[64,4096]{1,0:T(8,128)(2,1)S(1)} %get-tuple-element.30), channel_id=1, source_target_pairs={{0,32},{4,36},{8,40},{12,44},{16,48},{20,52},{24,56},{28,60},{32,0... | collective-permute-start | bytes 1572872 | tf_op jit(solution)/shard_map/ppermute | solution.py:62
  75.6 0.5 fusion.23
  76.1 0.5 fusion.21
  77.2 5.4 %collective-permute-start.6 = (bf16[64,4096]{1,0:T(8,128)(2,1)S(1)}, bf16[64,4096]{1,0:T(8,128)(2,1)S(1)}, u32[]{:S(2)}, u32[]{:S(2)}) collective-permute-start(bf16[64,4096]{1,0:T(8,128)(2,1)S(1)} %multiply_convert_fusion), channel_id=1, source_target_pairs={{0,128},{4,132},{8,136},{12,140},{16,144},{20,148},{24,152},{28,15... | collective-permute-start | bytes 1572872 | tf_op jit(solution)/shard_map/ppermute | solution.py:104
  82.7 1.9 %collective-permute-start.11 = (bf16[64,4096]{1,0:T(8,128)(2,1)S(1)}, bf16[64,4096]{1,0:T(8,128)(2,1)S(1)}, u32[]{:S(2)}, u32[]{:S(2)}) collective-permute-start(bf16[64,4096]{1,0:T(8,128)(2,1)S(1)} %add_convert_fusion.3), channel_id=1, source_target_pairs={{0,32},{4,36},{8,40},{12,44},{16,48},{20,52},{24,56},{28,60},{32,0... | collective-permute-start | bytes 1572872 | tf_op jit(solution)/shard_map/ppermute | solution.py:62
  84.8 3.0 %collective-permute-start.14 = (bf16[64,4096]{1,0:T(8,128)(2,1)S(1)}, bf16[64,4096]{1,0:T(8,128)(2,1)S(1)}, u32[]{:S(2)}, u32[]{:S(2)}) collective-permute-start(bf16[64,4096]{1,0:T(8,128)(2,1)S(1)} %add_convert_fusion.1), channel_id=1, source_target_pairs={{0,224},{4,228},{8,232},{12,236},{16,240},{20,244},{24,248},{28,25... | collective-permute-start | bytes 1572872 | tf_op jit(solution)/shard_map/ppermute | solution.py:62
  87.8 13.0 %collective-permute-done.11 = bf16[64,4096]{1,0:T(8,128)(2,1)S(1)} collective-permute-done((bf16[64,4096]{1,0:T(8,128)(2,1)S(1)}, bf16[64,4096]{1,0:T(8,128)(2,1)S(1)}, u32[]{:S(2)}, u32[]{:S(2)}) %collective-permute-start.11) | collective-permute-done | bytes 524320 | tf_op jit(solution)/shard_map/ppermute | solution.py:62
  100.8 3.0 %collective-permute-start.12 = (bf16[64,4096]{1,0:T(8,128)(2,1)S(1)}, bf16[64,4096]{1,0:T(8,128)(2,1)S(1)}, u32[]{:S(2)}, u32[]{:S(2)}) collective-permute-start(bf16[64,4096]{1,0:T(8,128)(2,1)S(1)} %add_convert_fusion.2), channel_id=1, source_target_pairs={{0,224},{4,228},{8,232},{12,236},{16,240},{20,244},{24,248},{28,25... | collective-permute-start | bytes 1572872 | tf_op jit(solution)/shard_map/ppermute | solution.py:62
  103.9 2.4 %collective-permute-start.15 = (bf16[64,4096]{1,0:T(8,128)(2,1)S(1)}, bf16[64,4096]{1,0:T(8,128)(2,1)S(1)}, u32[]{:S(2)}, u32[]{:S(2)}) collective-permute-start(bf16[64,4096]{1,0:T(8,128)(2,1)S(1)} %add_convert_fusion), channel_id=1, source_target_pairs={{0,32},{4,36},{8,40},{12,44},{16,48},{20,52},{24,56},{28,60},{32,0... | collective-permute-start | bytes 1572872 | tf_op jit(solution)/shard_map/ppermute | solution.py:62
  106.6 0.5 fusion.25
  107.1 5.1 %collective-permute-done.12 = bf16[64,4096]{1,0:T(8,128)(2,1)S(1)} collective-permute-done((bf16[64,4096]{1,0:T(8,128)(2,1)S(1)}, bf16[64,4096]{1,0:T(8,128)(2,1)S(1)}, u32[]{:S(2)}, u32[]{:S(2)}) %collective-permute-start.12) | collective-permute-done | bytes 524320 | tf_op jit(solution)/shard_map/ppermute | solution.py:62
  112.3 1.9 %collective-permute-done.15 = bf16[64,4096]{1,0:T(8,128)(2,1)S(1)} collective-permute-done((bf16[64,4096]{1,0:T(8,128)(2,1)S(1)}, bf16[64,4096]{1,0:T(8,128)(2,1)S(1)}, u32[]{:S(2)}, u32[]{:S(2)}) %collective-permute-start.15) | collective-permute-done | bytes 524320 | tf_op jit(solution)/shard_map/ppermute | solution.py:62
  114.2 0.5 fusion.8
  114.7 15.9 %all_to_all.10 = bf16[8,8,4096]{2,1,0:T(8,128)(2,1)S(1)} all-to-all(bf16[8,8,4096]{2,1,0:T(8,128)(2,1)S(1)} %fusion.8), channel_id=1, replica_groups={{0,4,8,12,16,20,24,28},{32,36,40,44,48,52,56,60},{64,68,72,76,80,84,88,..., dimensions={0} | all-to-all | bytes 1048576 | tf_op jit(solution)/shard_map/all_to_all | solution.py:117
  130.7 9.0 %collective-permute-start.16 = (bf16[8,4096]{1,0:T(8,128)(2,1)S(1)}, bf16[8,4096]{1,0:T(8,128)(2,1)S(1)}, u32[]{:S(2)}, u32[]{:S(2)}) collective-permute-start(bf16[8,4096]{1,0:T(8,128)(2,1)S(1)} %reduce_sum.72), channel_id=1, source_target_pairs={{0,256},{256,0},{1,257},{257,1},{2,258},{258,2},{3,259},{259,3},{4... | collective-permute-start | bytes 196616 | tf_op jit(solution)/shard_map/ppermute | solution.py:126
  139.7 0.9 collective-permute-done.16
  140.6 0.7 pad_maximum_fusion
  (43 shorter events, 3.6 us)
Async XLA Ops:
  0.0 36.1 %copy-start.1 = (bf16[1,4096,128]{2,1,0:T(8,128)(2,1)S(1)}, bf16[1,4096,128]{2,1,0:T(8,128)(2,1)}, u32[]{:S(2)}) copy-start(bf16[1,4096,128]{2,1,0:T(8,128)(2,1)} %param.9) | copy-start | bytes 3145732
  0.0 36.3 %copy-start.2 = (bf16[1,4096,128]{2,1,0:T(8,128)(2,1)S(1)}, bf16[1,4096,128]{2,1,0:T(8,128)(2,1)}, u32[]{:S(2)}) copy-start(bf16[1,4096,128]{2,1,0:T(8,128)(2,1)} %param.10) | copy-start | bytes 3145732
  3.6 20.0 %all-to-all-start = ((bf16[8,8,4224]{2,1,0:T(8,128)(2,1)}), bf16[8,8,4224]{2,1,0:T(8,128)(2,1)S(1)}, u32[]{:S(2)}, u32[]{:S(2)}) async-start(bf16[8,8,4224]{2,1,0:T(8,128)(2,1)} %broadcast_in_dim.69), calls=%async_computation | async-start | bytes 1081344 | tf_op jit(solution)/shard_map/all_to_all | solution.py:56
  23.5 17.9 %collective-permute-start.2 = (bf16[64,4224]{1,0:T(8,128)(2,1)S(1)}, bf16[64,4224]{1,0:T(8,128)(2,1)S(1)}, u32[]{:S(2)}, u32[]{:S(2)}) collective-permute-start(bf16[64,4224]{1,0:T(8,128)(2,1)S(1)} %bitcast.32), channel_id=1, source_target_pairs={{0,224},{4,228},{8,232},{12,236},{16,240},{20,244},{24,248},{28,25... | collective-permute-start | bytes 1622024 | tf_op jit(solution)/shard_map/ppermute | solution.py:62
  34.2 10.7 %collective-permute-start.7 = (bf16[64,4224]{1,0:T(8,128)(2,1)S(1)}, bf16[64,4224]{1,0:T(8,128)(2,1)S(1)}, u32[]{:S(2)}, u32[]{:S(2)}) collective-permute-start(bf16[64,4224]{1,0:T(8,128)(2,1)S(1)} %bitcast.33), channel_id=1, source_target_pairs={{0,32},{4,36},{8,40},{12,44},{16,48},{20,52},{24,56},{28,60},{32,0... | collective-permute-start | bytes 1622024 | tf_op jit(solution)/shard_map/ppermute | solution.py:62
  36.1 2.4 %copy-start = (bf16[1,128,4096]{2,1,0:T(8,128)(2,1)S(1)}, bf16[1,128,4096]{2,1,0:T(8,128)(2,1)}, u32[]{:S(2)}) copy-start(bf16[1,128,4096]{2,1,0:T(8,128)(2,1)} %param.11) | copy-start | bytes 3145732
  36.6 29.0 %collective-permute-start = (bf16[4096,256]{1,0:T(8,128)(2,1)S(1)}, bf16[4096,256]{1,0:T(8,128)(2,1)S(1)}, u32[]{:S(2)}, u32[]{:S(2)}) collective-permute-start(bf16[4096,256]{1,0:T(8,128)(2,1)S(1)} %constant_dynamic-update-slice_fusion), channel_id=1, source_target_pairs={{0,256},{256,0},{1,257},{257,1},{2,258},{258,2},{3,259},{259,3},{4... | collective-permute-start | bytes 6291464 | tf_op jit(solution)/shard_map/ppermute | solution.py:77
  38.6 27.5 %collective-permute-start.1 = (bf16[128,4096]{1,0:T(8,128)(2,1)S(1)}, bf16[128,4096]{1,0:T(8,128)(2,1)S(1)}, u32[]{:S(2)}, u32[]{:S(2)}) collective-permute-start(bf16[128,4096]{1,0:T(8,128)(2,1)S(1)} %bitcast.26), channel_id=1, source_target_pairs={{0,256},{256,0},{1,257},{257,1},{2,258},{258,2},{3,259},{259,3},{4... | collective-permute-start | bytes 3145736 | tf_op jit(solution)/shard_map/ppermute | solution.py:78
  41.5 10.4 %collective-permute-start.3 = (bf16[64,4224]{1,0:T(8,128)(2,1)S(1)}, bf16[64,4224]{1,0:T(8,128)(2,1)S(1)}, u32[]{:S(2)}, u32[]{:S(2)}) collective-permute-start(bf16[64,4224]{1,0:T(8,128)(2,1)S(1)} %collective-permute-done.2), channel_id=1, source_target_pairs={{0,32},{4,36},{8,40},{12,44},{16,48},{20,52},{24,56},{28,60},{32,0... | collective-permute-start | bytes 1622024 | tf_op jit(solution)/shard_map/ppermute | solution.py:62
  44.9 11.6 %collective-permute-start.8 = (bf16[64,4224]{1,0:T(8,128)(2,1)S(1)}, bf16[64,4224]{1,0:T(8,128)(2,1)S(1)}, u32[]{:S(2)}, u32[]{:S(2)}) collective-permute-start(bf16[64,4224]{1,0:T(8,128)(2,1)S(1)} %collective-permute-done.7), channel_id=1, source_target_pairs={{0,224},{4,228},{8,232},{12,236},{16,240},{20,244},{24,248},{28,25... | collective-permute-start | bytes 1622024 | tf_op jit(solution)/shard_map/ppermute | solution.py:62
  51.9 11.6 %collective-permute-start.4 = (bf16[64,4224]{1,0:T(8,128)(2,1)S(1)}, bf16[64,4224]{1,0:T(8,128)(2,1)S(1)}, u32[]{:S(2)}, u32[]{:S(2)}) collective-permute-start(bf16[64,4224]{1,0:T(8,128)(2,1)S(1)} %collective-permute-done.3), channel_id=1, source_target_pairs={{0,224},{4,228},{8,232},{12,236},{16,240},{20,244},{24,248},{28,25... | collective-permute-start | bytes 1622024 | tf_op jit(solution)/shard_map/ppermute | solution.py:62
  56.5 10.9 %collective-permute-start.9 = (bf16[64,4224]{1,0:T(8,128)(2,1)S(1)}, bf16[64,4224]{1,0:T(8,128)(2,1)S(1)}, u32[]{:S(2)}, u32[]{:S(2)}) collective-permute-start(bf16[64,4224]{1,0:T(8,128)(2,1)S(1)} %collective-permute-done.8), channel_id=1, source_target_pairs={{0,32},{4,36},{8,40},{12,44},{16,48},{20,52},{24,56},{28,60},{32,0... | collective-permute-start | bytes 1622024 | tf_op jit(solution)/shard_map/ppermute | solution.py:62
  63.4 12.0 %collective-permute-start.5 = (bf16[64,4224]{1,0:T(8,128)(2,1)S(1)}, bf16[64,4224]{1,0:T(8,128)(2,1)S(1)}, u32[]{:S(2)}, u32[]{:S(2)}) collective-permute-start(bf16[64,4224]{1,0:T(8,128)(2,1)S(1)} %collective-permute-done.4), channel_id=1, source_target_pairs={{0,32},{4,36},{8,40},{12,44},{16,48},{20,52},{24,56},{28,60},{32,0... | collective-permute-start | bytes 1622024 | tf_op jit(solution)/shard_map/ppermute | solution.py:71
  69.5 13.1 %collective-permute-start.10 = (bf16[64,4096]{1,0:T(8,128)(2,1)S(1)}, bf16[64,4096]{1,0:T(8,128)(2,1)S(1)}, u32[]{:S(2)}, u32[]{:S(2)}) collective-permute-start(bf16[64,4096]{1,0:T(8,128)(2,1)S(1)} %get-tuple-element.27), channel_id=1, source_target_pairs={{0,224},{4,228},{8,232},{12,236},{16,240},{20,244},{24,248},{28,25... | collective-permute-start | bytes 1572872 | tf_op jit(solution)/shard_map/ppermute | solution.py:62
  73.5 11.1 %collective-permute-start.13 = (bf16[64,4096]{1,0:T(8,128)(2,1)S(1)}, bf16[64,4096]{1,0:T(8,128)(2,1)S(1)}, u32[]{:S(2)}, u32[]{:S(2)}) collective-permute-start(bf16[64,4096]{1,0:T(8,128)(2,1)S(1)} %get-tuple-element.30), channel_id=1, source_target_pairs={{0,32},{4,36},{8,40},{12,44},{16,48},{20,52},{24,56},{28,60},{32,0... | collective-permute-start | bytes 1572872 | tf_op jit(solution)/shard_map/ppermute | solution.py:62
  77.2 29.9 %collective-permute-start.6 = (bf16[64,4096]{1,0:T(8,128)(2,1)S(1)}, bf16[64,4096]{1,0:T(8,128)(2,1)S(1)}, u32[]{:S(2)}, u32[]{:S(2)}) collective-permute-start(bf16[64,4096]{1,0:T(8,128)(2,1)S(1)} %multiply_convert_fusion), channel_id=1, source_target_pairs={{0,128},{4,132},{8,136},{12,140},{16,144},{20,148},{24,152},{28,15... | collective-permute-start | bytes 1572872 | tf_op jit(solution)/shard_map/ppermute | solution.py:104
  82.7 18.0 %collective-permute-start.11 = (bf16[64,4096]{1,0:T(8,128)(2,1)S(1)}, bf16[64,4096]{1,0:T(8,128)(2,1)S(1)}, u32[]{:S(2)}, u32[]{:S(2)}) collective-permute-start(bf16[64,4096]{1,0:T(8,128)(2,1)S(1)} %add_convert_fusion.3), channel_id=1, source_target_pairs={{0,32},{4,36},{8,40},{12,44},{16,48},{20,52},{24,56},{28,60},{32,0... | collective-permute-start | bytes 1572872 | tf_op jit(solution)/shard_map/ppermute | solution.py:62
  84.8 19.1 %collective-permute-start.14 = (bf16[64,4096]{1,0:T(8,128)(2,1)S(1)}, bf16[64,4096]{1,0:T(8,128)(2,1)S(1)}, u32[]{:S(2)}, u32[]{:S(2)}) collective-permute-start(bf16[64,4096]{1,0:T(8,128)(2,1)S(1)} %add_convert_fusion.1), channel_id=1, source_target_pairs={{0,224},{4,228},{8,232},{12,236},{16,240},{20,244},{24,248},{28,25... | collective-permute-start | bytes 1572872 | tf_op jit(solution)/shard_map/ppermute | solution.py:62
  100.8 11.4 %collective-permute-start.12 = (bf16[64,4096]{1,0:T(8,128)(2,1)S(1)}, bf16[64,4096]{1,0:T(8,128)(2,1)S(1)}, u32[]{:S(2)}, u32[]{:S(2)}) collective-permute-start(bf16[64,4096]{1,0:T(8,128)(2,1)S(1)} %add_convert_fusion.2), channel_id=1, source_target_pairs={{0,224},{4,228},{8,232},{12,236},{16,240},{20,244},{24,248},{28,25... | collective-permute-start | bytes 1572872 | tf_op jit(solution)/shard_map/ppermute | solution.py:62
  103.9 10.2 %collective-permute-start.15 = (bf16[64,4096]{1,0:T(8,128)(2,1)S(1)}, bf16[64,4096]{1,0:T(8,128)(2,1)S(1)}, u32[]{:S(2)}, u32[]{:S(2)}) collective-permute-start(bf16[64,4096]{1,0:T(8,128)(2,1)S(1)} %add_convert_fusion), channel_id=1, source_target_pairs={{0,32},{4,36},{8,40},{12,44},{16,48},{20,52},{24,56},{28,60},{32,0... | collective-permute-start | bytes 1572872 | tf_op jit(solution)/shard_map/ppermute | solution.py:62
  130.7 9.9 %collective-permute-start.16 = (bf16[8,4096]{1,0:T(8,128)(2,1)S(1)}, bf16[8,4096]{1,0:T(8,128)(2,1)S(1)}, u32[]{:S(2)}, u32[]{:S(2)}) collective-permute-start(bf16[8,4096]{1,0:T(8,128)(2,1)S(1)} %reduce_sum.72), channel_id=1, source_target_pairs={{0,256},{256,0},{1,257},{257,1},{2,258},{258,2},{3,259},{259,3},{4... | collective-permute-start | bytes 196616 | tf_op jit(solution)/shard_map/ppermute | solution.py:126

commit v5 on v4

--- a/solution.py
+++ b/solution.py
@@ -1,6 +1,8 @@
 import jax
 import jax.numpy as jnp
 from jax import lax
+from jax.experimental import pallas as pl
+from jax.experimental.pallas import tpu as pltpu
 from jax.sharding import PartitionSpec as P
 
 EXPERTS = 16
@@ -29,6 +31,55 @@
     return second_axis(lambda c: (c + 1) % SIDE if c % 2 == odd else (c - 1) % SIDE)
 
 
+def pack_kernel(pool_ref, *refs):
+    sources, out_ref, targets, done = refs[:3], refs[3], refs[4:7], refs[7]
+    copies = [
+        pltpu.make_async_copy(source, target, done.at[i])
+        for i, (source, target) in enumerate(zip(sources, targets))
+    ]
+    for copy in copies:
+        copy.start()
+    for copy in copies:
+        copy.wait()
+    rows_ref, routes_ref, gates_ref = targets
+    row_count, width = rows_ref.shape
+    half = row_count // 2
+    expert_ids = lax.broadcasted_iota(jnp.int32, (EXPERTS, row_count), 0)
+    weight = jnp.zeros((EXPERTS, row_count), jnp.float32)
+    for k in range(routes_ref.shape[0]):
+        chosen = routes_ref[k : k + 1, :] == expert_ids
+        weight = weight + jnp.where(chosen, gates_ref[k : k + 1, :], 0.0)
+    high = weight.astype(jnp.bfloat16).astype(jnp.float32)
+    middle = (weight - high).astype(jnp.bfloat16).astype(jnp.float32)
+    low = weight - high - middle
+    rest = jnp.zeros((PAD - 3 * EXPERTS, row_count), jnp.float32)
+    terms = jnp.concatenate([high, middle, low, rest], axis=0).astype(jnp.bfloat16)
+    across = lax.broadcasted_iota(jnp.int32, (row_count, row_count), 0)
+    down = lax.broadcasted_iota(jnp.int32, (row_count, row_count), 1)
+    identity = (across == down).astype(jnp.float32).astype(jnp.bfloat16)
+    beside = lax.dot_general(
+        identity, terms, (((1,), (1,)), ((), ())), preferred_element_type=jnp.float32
+    )
+    packed = jnp.concatenate([rows_ref[...].astype(jnp.float32), beside], axis=1)
+    mine = jnp.where(pool_ref[0] == 0, packed[:half], packed[half:])
+    out_ref[...] = jnp.concatenate([mine] * SIDE, axis=0).astype(jnp.bfloat16)
+
+
+def pack(pool, moe_rows, routes, gate_values):
+    row_count, width = moe_rows.shape
+    hbm = pl.BlockSpec(memory_space=pltpu.HBM)
+    arrays = moe_rows, routes.T, gate_values.T
+    return pl.pallas_call(
+        pack_kernel,
+        out_shape=jax.ShapeDtypeStruct((SIDE * row_count // 2, width + PAD), jnp.bfloat16),
+        in_specs=[pl.BlockSpec(memory_space=pltpu.SMEM), hbm, hbm, hbm],
+        out_specs=pl.BlockSpec(memory_space=pltpu.VMEM),
+        scratch_shapes=[pltpu.VMEM(a.shape, a.dtype) for a in arrays]
+        + [pltpu.SemaphoreType.DMA((len(arrays),))],
+        compiler_params=pltpu.CompilerParams(vmem_limit_bytes=60 * 1024 * 1024),
+    )(pool.reshape(1), *arrays)
+
+
 def body(moe_rows, routes, gate_values, gate_weight, up_weight, down_weight):
     device_count = lax.axis_size("dev")
     groups = line_groups()
@@ -39,20 +90,8 @@
     row_count, width = moe_rows.shape
     half = row_count // 2
 
-    expert_ids = jnp.arange(EXPERTS, dtype=jnp.int32)
-    chosen = routes[:, :, None] == expert_ids[None, None, :]
-    weight = jnp.sum(jnp.where(chosen, gate_values[:, :, None], 0.0), axis=1)
-    high = lax.reduce_precision(weight, 8, 7)
-    middle = lax.reduce_precision(weight - high, 8, 7)
-    low = weight - high - middle
-    terms = jnp.concatenate([high, middle, low], axis=1).astype(jnp.bfloat16)
-    packed = jnp.concatenate(
-        [moe_rows, jnp.pad(terms, ((0, 0), (0, PAD - 3 * EXPERTS)))], axis=1
-    )
-    mine = lax.dynamic_slice_in_dim(packed, pool * half, half, 0)
-
     cut = gate_weight.shape[2]
-    spread = jnp.broadcast_to(mine[None], (SIDE,) + mine.shape)
+    spread = pack(pool, moe_rows, routes, gate_values).reshape(SIDE, half, width + PAD)
     own = lax.all_to_all(
         spread, AXES, split_axis=0, concat_axis=0, tiled=True, axis_index_groups=groups
     ).reshape(SIDE * half, width + PAD)

time: 142 us -> 140 us (0.986)
  local copies, waits for them, and re-layouts: 3.73 us -> 1.25 us
  Pallas kernels: 0 us -> 2.02 us
    pallas_call x0 -> x1, Pallas kernels: none -> 2.02 us  [pack(): pl.pallas_call(pack_kernel, out_shape=jax.ShapeDtypeStruct((SIDE * row_co...]
    unnamed x12 -> x10, local copies, waits for them, and re-layouts: 1.97 us -> 0.31 us
where the time goes in v5:
time: 140 us
  starting transfers between devices  68.7 us (49%)
  waiting for transfers between devices  41.2 us (29%)
  blocking collectives  16 us (11%)
  matrix products  8.64 us (6%)
  Pallas kernels  2.02 us (1%)
  other arithmetic  1.44 us (1%)
    ppermute x6, starting transfers between devices, swap_both(): lax.ppermute(to_one, AXES, pairs[0])  26.5 us
    ppermute x6, waiting for transfers between devices, swap_both(): lax.ppermute(to_one, AXES, pairs[0])  25.5 us
    all_to_all x1, blocking collectives, body(): lax.all_to_all(summed.astype(jnp.bfloat16).reshape(SIDE, half, width), AX...  16 us
    ppermute x6, starting transfers between devices, swap_both(): lax.ppermute(to_two, AXES, pairs[1])  13.7 us
    all_to_all x1, waiting for transfers between devices, body(): lax.all_to_all(spread, AXES, split_axis=0, concat_axis=0, tiled=True, axi...  12.3 us
    ppermute x1, starting transfers between devices, body(): other = lax.ppermute(total, 'pool', SWAP)  8.95 us
    all_to_all x1, starting transfers between devices, body(): lax.all_to_all(spread, AXES, split_axis=0, concat_axis=0, tiled=True, axi...  7.66 us
    ppermute x1, starting transfers between devices, body(): from_far = lax.ppermute(far_part, AXES, opposite)  5.44 us
  transfers between devices with their start and end apart: 18, of which 8 were waited for; matrix products, arithmetic and copies ran while one was open for 7% of the time, Pallas kernels for 0%

profile of v5, /device:TPU:1, one launch (start us, length us, event | category | flops | bytes accessed | tf_op | source)
XLA Modules:
  0.0 139.7 jit_solution(6053908864343668909)
XLA Ops:
  0.0 2.0 %shard_map.64 = bf16[64,4224]{1,0:T(8,128)(2,1)} custom-call(s32[1]{0:T(128)} %bitcast.pool_ref, bf16[16,4096]{1,0:T(8,128)(2,1)} %refs_0_.1, s32[8,16]{1,0:T(8,128)} %bitcast.44, f32[8,16]{1,0:T(8,128)} %bitcast.45), custom_call_target="tpu_custom_call" | custom-call | tf_op jit(solution)/shard_map/pallas_call | solution.py:72
  2.0 7.7 %all-to-all-start = ((bf16[8,8,4224]{2,1,0:T(8,128)(2,1)}), bf16[8,8,4224]{2,1,0:T(8,128)(2,1)S(1)}, u32[]{:S(2)}, u32[]{:S(2)}) async-start(bf16[8,8,4224]{2,1,0:T(8,128)(2,1)} %bitcast.41), calls=%async_computation | async-start | bytes 1081344 | tf_op jit(solution)/shard_map/all_to_all | solution.py:95
  9.7 12.3 %all-to-all-done = bf16[8,8,4224]{2,1,0:T(8,128)(2,1)S(1)} async-done(((bf16[8,8,4224]{2,1,0:T(8,128)(2,1)}), bf16[8,8,4224]{2,1,0:T(8,128)(2,1)S(1)}, u32[]{:S(2)}, u32[]{:S(2)}) %all-to-all-start) | async-done | bytes 540704 | tf_op jit(solution)/shard_map/all_to_all | solution.py:95
  22.0 10.7 %collective-permute-start.2 = (bf16[64,4224]{1,0:T(8,128)(2,1)S(1)}, bf16[64,4224]{1,0:T(8,128)(2,1)S(1)}, u32[]{:S(2)}, u32[]{:S(2)}) collective-permute-start(bf16[64,4224]{1,0:T(8,128)(2,1)S(1)} %bitcast.36), channel_id=1, source_target_pairs={{0,224},{4,228},{8,232},{12,236},{16,240},{20,244},{24,248},{28,25... | collective-permute-start | bytes 1622024 | tf_op jit(solution)/shard_map/ppermute | solution.py:101
  32.7 1.9 %collective-permute-start.7 = (bf16[64,4224]{1,0:T(8,128)(2,1)S(1)}, bf16[64,4224]{1,0:T(8,128)(2,1)S(1)}, u32[]{:S(2)}, u32[]{:S(2)}) collective-permute-start(bf16[64,4224]{1,0:T(8,128)(2,1)S(1)} %bitcast.37), channel_id=1, source_target_pairs={{0,32},{4,36},{8,40},{12,44},{16,48},{20,52},{24,56},{28,60},{32,0... | collective-permute-start | bytes 1622024 | tf_op jit(solution)/shard_map/ppermute | solution.py:101
  35.1 1.9 %collective-permute-start = (bf16[4096,256]{1,0:T(8,128)(2,1)S(1)}, bf16[4096,256]{1,0:T(8,128)(2,1)S(1)}, u32[]{:S(2)}, u32[]{:S(2)}) collective-permute-start(bf16[4096,256]{1,0:T(8,128)(2,1)S(1)} %constant_dynamic-update-slice_fusion), channel_id=1, source_target_pairs={{0,256},{256,0},{1,257},{257,1},{2,258},{258,2},{3,259},{259,3},{4... | collective-permute-start | bytes 6291464 | tf_op jit(solution)/shard_map/ppermute | solution.py:116
  37.0 2.4 %collective-permute-start.1 = (bf16[128,4096]{1,0:T(8,128)(2,1)S(1)}, bf16[128,4096]{1,0:T(8,128)(2,1)S(1)}, u32[]{:S(2)}, u32[]{:S(2)}) collective-permute-start(bf16[128,4096]{1,0:T(8,128)(2,1)S(1)} %bitcast.30), channel_id=1, source_target_pairs={{0,256},{256,0},{1,257},{257,1},{2,258},{258,2},{3,259},{259,3},{4... | collective-permute-start | bytes 3145736 | tf_op jit(solution)/shard_map/ppermute | solution.py:117
  39.4 0.5 fusion.27
  39.9 3.4 %collective-permute-start.3 = (bf16[64,4224]{1,0:T(8,128)(2,1)S(1)}, bf16[64,4224]{1,0:T(8,128)(2,1)S(1)}, u32[]{:S(2)}, u32[]{:S(2)}) collective-permute-start(bf16[64,4224]{1,0:T(8,128)(2,1)S(1)} %collective-permute-done.2), channel_id=1, source_target_pairs={{0,32},{4,36},{8,40},{12,44},{16,48},{20,52},{24,56},{28,60},{32,0... | collective-permute-start | bytes 1622024 | tf_op jit(solution)/shard_map/ppermute | solution.py:101
  43.4 2.6 %collective-permute-start.8 = (bf16[64,4224]{1,0:T(8,128)(2,1)S(1)}, bf16[64,4224]{1,0:T(8,128)(2,1)S(1)}, u32[]{:S(2)}, u32[]{:S(2)}) collective-permute-start(bf16[64,4224]{1,0:T(8,128)(2,1)S(1)} %collective-permute-done.7), channel_id=1, source_target_pairs={{0,224},{4,228},{8,232},{12,236},{16,240},{20,244},{24,248},{28,25... | collective-permute-start | bytes 1622024 | tf_op jit(solution)/shard_map/ppermute | solution.py:101
  46.0 0.4 fusion.19
  46.5 0.4 fusion.35
  46.9 3.4 %collective-permute-done.3 = bf16[64,4224]{1,0:T(8,128)(2,1)S(1)} collective-permute-done((bf16[64,4224]{1,0:T(8,128)(2,1)S(1)}, bf16[64,4224]{1,0:T(8,128)(2,1)S(1)}, u32[]{:S(2)}, u32[]{:S(2)}) %collective-permute-start.3) | collective-permute-done | bytes 540704 | tf_op jit(solution)/shard_map/ppermute | solution.py:101
  50.3 4.0 %collective-permute-start.4 = (bf16[64,4224]{1,0:T(8,128)(2,1)S(1)}, bf16[64,4224]{1,0:T(8,128)(2,1)S(1)}, u32[]{:S(2)}, u32[]{:S(2)}) collective-permute-start(bf16[64,4224]{1,0:T(8,128)(2,1)S(1)} %collective-permute-done.3), channel_id=1, source_target_pairs={{0,224},{4,228},{8,232},{12,236},{16,240},{20,244},{24,248},{28,25... | collective-permute-start | bytes 1622024 | tf_op jit(solution)/shard_map/ppermute | solution.py:101
  54.4 0.6 collective-permute-done.8
  55.0 1.9 %collective-permute-start.9 = (bf16[64,4224]{1,0:T(8,128)(2,1)S(1)}, bf16[64,4224]{1,0:T(8,128)(2,1)S(1)}, u32[]{:S(2)}, u32[]{:S(2)}) collective-permute-start(bf16[64,4224]{1,0:T(8,128)(2,1)S(1)} %collective-permute-done.8), channel_id=1, source_target_pairs={{0,32},{4,36},{8,40},{12,44},{16,48},{20,52},{24,56},{28,60},{32,0... | collective-permute-start | bytes 1622024 | tf_op jit(solution)/shard_map/ppermute | solution.py:101
  57.1 0.5 fusion.15
  57.6 0.4 fusion.38
  58.0 3.9 %collective-permute-done.4 = bf16[64,4224]{1,0:T(8,128)(2,1)S(1)} collective-permute-done((bf16[64,4224]{1,0:T(8,128)(2,1)S(1)}, bf16[64,4224]{1,0:T(8,128)(2,1)S(1)}, u32[]{:S(2)}, u32[]{:S(2)}) %collective-permute-start.4) | collective-permute-done | bytes 540704 | tf_op jit(solution)/shard_map/ppermute | solution.py:101
  61.9 2.1 %collective-permute-start.5 = (bf16[64,4224]{1,0:T(8,128)(2,1)S(1)}, bf16[64,4224]{1,0:T(8,128)(2,1)S(1)}, u32[]{:S(2)}, u32[]{:S(2)}) collective-permute-start(bf16[64,4224]{1,0:T(8,128)(2,1)S(1)} %collective-permute-done.4), channel_id=1, source_target_pairs={{0,32},{4,36},{8,40},{12,44},{16,48},{20,52},{24,56},{28,60},{32,0... | collective-permute-start | bytes 1622024 | tf_op jit(solution)/shard_map/ppermute | solution.py:110
  64.1 0.4 fusion.13
  64.6 0.4 fusion.1
  65.0 0.4 fusion.17
  65.4 0.4 fusion.2
  66.0 0.4 fusion.11
  66.6 0.4 fusion.41
  67.0 0.4 fusion.9
  67.5 0.5 fusion
  68.0 3.5 %collective-permute-start.10 = (bf16[64,4096]{1,0:T(8,128)(2,1)S(1)}, bf16[64,4096]{1,0:T(8,128)(2,1)S(1)}, u32[]{:S(2)}, u32[]{:S(2)}) collective-permute-start(bf16[64,4096]{1,0:T(8,128)(2,1)S(1)} %get-tuple-element.27), channel_id=1, source_target_pairs={{0,224},{4,228},{8,232},{12,236},{16,240},{20,244},{24,248},{28,25... | collective-permute-start | bytes 1572872 | tf_op jit(solution)/shard_map/ppermute | solution.py:101
  71.6 0.4 fusion.77
  72.0 1.9 %collective-permute-start.13 = (bf16[64,4096]{1,0:T(8,128)(2,1)S(1)}, bf16[64,4096]{1,0:T(8,128)(2,1)S(1)}, u32[]{:S(2)}, u32[]{:S(2)}) collective-permute-start(bf16[64,4096]{1,0:T(8,128)(2,1)S(1)} %get-tuple-element.30), channel_id=1, source_target_pairs={{0,32},{4,36},{8,40},{12,44},{16,48},{20,52},{24,56},{28,60},{32,0... | collective-permute-start | bytes 1572872 | tf_op jit(solution)/shard_map/ppermute | solution.py:101
  74.1 0.5 fusion.23
  74.6 0.5 fusion.21
  75.3 0.3 multiply_convert_fusion
  75.7 5.4 %collective-permute-start.6 = (bf16[64,4096]{1,0:T(8,128)(2,1)S(1)}, bf16[64,4096]{1,0:T(8,128)(2,1)S(1)}, u32[]{:S(2)}, u32[]{:S(2)}) collective-permute-start(bf16[64,4096]{1,0:T(8,128)(2,1)S(1)} %multiply_convert_fusion), channel_id=1, source_target_pairs={{0,128},{4,132},{8,136},{12,140},{16,144},{20,148},{24,152},{28,15... | collective-permute-start | bytes 1572872 | tf_op jit(solution)/shard_map/ppermute | solution.py:143
  81.2 1.9 %collective-permute-start.11 = (bf16[64,4096]{1,0:T(8,128)(2,1)S(1)}, bf16[64,4096]{1,0:T(8,128)(2,1)S(1)}, u32[]{:S(2)}, u32[]{:S(2)}) collective-permute-start(bf16[64,4096]{1,0:T(8,128)(2,1)S(1)} %add_convert_fusion.3), channel_id=1, source_target_pairs={{0,32},{4,36},{8,40},{12,44},{16,48},{20,52},{24,56},{28,60},{32,0... | collective-permute-start | bytes 1572872 | tf_op jit(solution)/shard_map/ppermute | solution.py:101
  83.3 3.0 %collective-permute-start.14 = (bf16[64,4096]{1,0:T(8,128)(2,1)S(1)}, bf16[64,4096]{1,0:T(8,128)(2,1)S(1)}, u32[]{:S(2)}, u32[]{:S(2)}) collective-permute-start(bf16[64,4096]{1,0:T(8,128)(2,1)S(1)} %add_convert_fusion.1), channel_id=1, source_target_pairs={{0,224},{4,228},{8,232},{12,236},{16,240},{20,244},{24,248},{28,25... | collective-permute-start | bytes 1572872 | tf_op jit(solution)/shard_map/ppermute | solution.py:101
  86.2 13.0 %collective-permute-done.11 = bf16[64,4096]{1,0:T(8,128)(2,1)S(1)} collective-permute-done((bf16[64,4096]{1,0:T(8,128)(2,1)S(1)}, bf16[64,4096]{1,0:T(8,128)(2,1)S(1)}, u32[]{:S(2)}, u32[]{:S(2)}) %collective-permute-start.11) | collective-permute-done | bytes 524320 | tf_op jit(solution)/shard_map/ppermute | solution.py:101
  99.3 3.0 %collective-permute-start.12 = (bf16[64,4096]{1,0:T(8,128)(2,1)S(1)}, bf16[64,4096]{1,0:T(8,128)(2,1)S(1)}, u32[]{:S(2)}, u32[]{:S(2)}) collective-permute-start(bf16[64,4096]{1,0:T(8,128)(2,1)S(1)} %add_convert_fusion.2), channel_id=1, source_target_pairs={{0,224},{4,228},{8,232},{12,236},{16,240},{20,244},{24,248},{28,25... | collective-permute-start | bytes 1572872 | tf_op jit(solution)/shard_map/ppermute | solution.py:101
  102.4 2.4 %collective-permute-start.15 = (bf16[64,4096]{1,0:T(8,128)(2,1)S(1)}, bf16[64,4096]{1,0:T(8,128)(2,1)S(1)}, u32[]{:S(2)}, u32[]{:S(2)}) collective-permute-start(bf16[64,4096]{1,0:T(8,128)(2,1)S(1)} %add_convert_fusion), channel_id=1, source_target_pairs={{0,32},{4,36},{8,40},{12,44},{16,48},{20,52},{24,56},{28,60},{32,0... | collective-permute-start | bytes 1572872 | tf_op jit(solution)/shard_map/ppermute | solution.py:101
  105.1 0.5 fusion.25
  105.6 5.1 %collective-permute-done.12 = bf16[64,4096]{1,0:T(8,128)(2,1)S(1)} collective-permute-done((bf16[64,4096]{1,0:T(8,128)(2,1)S(1)}, bf16[64,4096]{1,0:T(8,128)(2,1)S(1)}, u32[]{:S(2)}, u32[]{:S(2)}) %collective-permute-start.12) | collective-permute-done | bytes 524320 | tf_op jit(solution)/shard_map/ppermute | solution.py:101
  110.8 1.9 %collective-permute-done.15 = bf16[64,4096]{1,0:T(8,128)(2,1)S(1)} collective-permute-done((bf16[64,4096]{1,0:T(8,128)(2,1)S(1)}, bf16[64,4096]{1,0:T(8,128)(2,1)S(1)}, u32[]{:S(2)}, u32[]{:S(2)}) %collective-permute-start.15) | collective-permute-done | bytes 524320 | tf_op jit(solution)/shard_map/ppermute | solution.py:101
  112.7 0.5 fusion.8
  113.2 16.0 %all_to_all.10 = bf16[8,8,4096]{2,1,0:T(8,128)(2,1)S(1)} all-to-all(bf16[8,8,4096]{2,1,0:T(8,128)(2,1)S(1)} %fusion.8), channel_id=1, replica_groups={{0,4,8,12,16,20,24,28},{32,36,40,44,48,52,56,60},{64,68,72,76,80,84,88,..., dimensions={0} | all-to-all | bytes 1048576 | tf_op jit(solution)/shard_map/all_to_all | solution.py:156
  129.2 8.9 %collective-permute-start.16 = (bf16[8,4096]{1,0:T(8,128)(2,1)S(1)}, bf16[8,4096]{1,0:T(8,128)(2,1)S(1)}, u32[]{:S(2)}, u32[]{:S(2)}) collective-permute-start(bf16[8,4096]{1,0:T(8,128)(2,1)S(1)} %reduce_sum.62), channel_id=1, source_target_pairs={{0,256},{256,0},{1,257},{257,1},{2,258},{258,2},{3,259},{259,3},{4... | collective-permute-start | bytes 196616 | tf_op jit(solution)/shard_map/ppermute | solution.py:165
  138.2 0.9 collective-permute-done.16
  139.0 0.7 pad_maximum_fusion
  (37 shorter events, 2.2 us)
Async XLA Ops:
  0.0 34.6 %copy-start.1 = (bf16[1,4096,128]{2,1,0:T(8,128)(2,1)S(1)}, bf16[1,4096,128]{2,1,0:T(8,128)(2,1)}, u32[]{:S(2)}) copy-start(bf16[1,4096,128]{2,1,0:T(8,128)(2,1)} %param.9) | copy-start | bytes 3145732
  0.0 34.8 %copy-start.2 = (bf16[1,4096,128]{2,1,0:T(8,128)(2,1)S(1)}, bf16[1,4096,128]{2,1,0:T(8,128)(2,1)}, u32[]{:S(2)}) copy-start(bf16[1,4096,128]{2,1,0:T(8,128)(2,1)} %param.10) | copy-start | bytes 3145732
  2.0 20.0 %all-to-all-start = ((bf16[8,8,4224]{2,1,0:T(8,128)(2,1)}), bf16[8,8,4224]{2,1,0:T(8,128)(2,1)S(1)}, u32[]{:S(2)}, u32[]{:S(2)}) async-start(bf16[8,8,4224]{2,1,0:T(8,128)(2,1)} %bitcast.41), calls=%async_computation | async-start | bytes 1081344 | tf_op jit(solution)/shard_map/all_to_all | solution.py:95
  22.0 17.9 %collective-permute-start.2 = (bf16[64,4224]{1,0:T(8,128)(2,1)S(1)}, bf16[64,4224]{1,0:T(8,128)(2,1)S(1)}, u32[]{:S(2)}, u32[]{:S(2)}) collective-permute-start(bf16[64,4224]{1,0:T(8,128)(2,1)S(1)} %bitcast.36), channel_id=1, source_target_pairs={{0,224},{4,228},{8,232},{12,236},{16,240},{20,244},{24,248},{28,25... | collective-permute-start | bytes 1622024 | tf_op jit(solution)/shard_map/ppermute | solution.py:101
  32.7 10.7 %collective-permute-start.7 = (bf16[64,4224]{1,0:T(8,128)(2,1)S(1)}, bf16[64,4224]{1,0:T(8,128)(2,1)S(1)}, u32[]{:S(2)}, u32[]{:S(2)}) collective-permute-start(bf16[64,4224]{1,0:T(8,128)(2,1)S(1)} %bitcast.37), channel_id=1, source_target_pairs={{0,32},{4,36},{8,40},{12,44},{16,48},{20,52},{24,56},{28,60},{32,0... | collective-permute-start | bytes 1622024 | tf_op jit(solution)/shard_map/ppermute | solution.py:101
  34.6 2.4 %copy-start = (bf16[1,128,4096]{2,1,0:T(8,128)(2,1)S(1)}, bf16[1,128,4096]{2,1,0:T(8,128)(2,1)}, u32[]{:S(2)}) copy-start(bf16[1,128,4096]{2,1,0:T(8,128)(2,1)} %param.11) | copy-start | bytes 3145732
  35.1 29.0 %collective-permute-start = (bf16[4096,256]{1,0:T(8,128)(2,1)S(1)}, bf16[4096,256]{1,0:T(8,128)(2,1)S(1)}, u32[]{:S(2)}, u32[]{:S(2)}) collective-permute-start(bf16[4096,256]{1,0:T(8,128)(2,1)S(1)} %constant_dynamic-update-slice_fusion), channel_id=1, source_target_pairs={{0,256},{256,0},{1,257},{257,1},{2,258},{258,2},{3,259},{259,3},{4... | collective-permute-start | bytes 6291464 | tf_op jit(solution)/shard_map/ppermute | solution.py:116
  37.0 27.5 %collective-permute-start.1 = (bf16[128,4096]{1,0:T(8,128)(2,1)S(1)}, bf16[128,4096]{1,0:T(8,128)(2,1)S(1)}, u32[]{:S(2)}, u32[]{:S(2)}) collective-permute-start(bf16[128,4096]{1,0:T(8,128)(2,1)S(1)} %bitcast.30), channel_id=1, source_target_pairs={{0,256},{256,0},{1,257},{257,1},{2,258},{258,2},{3,259},{259,3},{4... | collective-permute-start | bytes 3145736 | tf_op jit(solution)/shard_map/ppermute | solution.py:117
  39.9 10.4 %collective-permute-start.3 = (bf16[64,4224]{1,0:T(8,128)(2,1)S(1)}, bf16[64,4224]{1,0:T(8,128)(2,1)S(1)}, u32[]{:S(2)}, u32[]{:S(2)}) collective-permute-start(bf16[64,4224]{1,0:T(8,128)(2,1)S(1)} %collective-permute-done.2), channel_id=1, source_target_pairs={{0,32},{4,36},{8,40},{12,44},{16,48},{20,52},{24,56},{28,60},{32,0... | collective-permute-start | bytes 1622024 | tf_op jit(solution)/shard_map/ppermute | solution.py:101
  43.4 11.6 %collective-permute-start.8 = (bf16[64,4224]{1,0:T(8,128)(2,1)S(1)}, bf16[64,4224]{1,0:T(8,128)(2,1)S(1)}, u32[]{:S(2)}, u32[]{:S(2)}) collective-permute-start(bf16[64,4224]{1,0:T(8,128)(2,1)S(1)} %collective-permute-done.7), channel_id=1, source_target_pairs={{0,224},{4,228},{8,232},{12,236},{16,240},{20,244},{24,248},{28,25... | collective-permute-start | bytes 1622024 | tf_op jit(solution)/shard_map/ppermute | solution.py:101
  50.3 11.6 %collective-permute-start.4 = (bf16[64,4224]{1,0:T(8,128)(2,1)S(1)}, bf16[64,4224]{1,0:T(8,128)(2,1)S(1)}, u32[]{:S(2)}, u32[]{:S(2)}) collective-permute-start(bf16[64,4224]{1,0:T(8,128)(2,1)S(1)} %collective-permute-done.3), channel_id=1, source_target_pairs={{0,224},{4,228},{8,232},{12,236},{16,240},{20,244},{24,248},{28,25... | collective-permute-start | bytes 1622024 | tf_op jit(solution)/shard_map/ppermute | solution.py:101
  55.0 10.9 %collective-permute-start.9 = (bf16[64,4224]{1,0:T(8,128)(2,1)S(1)}, bf16[64,4224]{1,0:T(8,128)(2,1)S(1)}, u32[]{:S(2)}, u32[]{:S(2)}) collective-permute-start(bf16[64,4224]{1,0:T(8,128)(2,1)S(1)} %collective-permute-done.8), channel_id=1, source_target_pairs={{0,32},{4,36},{8,40},{12,44},{16,48},{20,52},{24,56},{28,60},{32,0... | collective-permute-start | bytes 1622024 | tf_op jit(solution)/shard_map/ppermute | solution.py:101
  61.9 12.0 %collective-permute-start.5 = (bf16[64,4224]{1,0:T(8,128)(2,1)S(1)}, bf16[64,4224]{1,0:T(8,128)(2,1)S(1)}, u32[]{:S(2)}, u32[]{:S(2)}) collective-permute-start(bf16[64,4224]{1,0:T(8,128)(2,1)S(1)} %collective-permute-done.4), channel_id=1, source_target_pairs={{0,32},{4,36},{8,40},{12,44},{16,48},{20,52},{24,56},{28,60},{32,0... | collective-permute-start | bytes 1622024 | tf_op jit(solution)/shard_map/ppermute | solution.py:110
  68.0 13.1 %collective-permute-start.10 = (bf16[64,4096]{1,0:T(8,128)(2,1)S(1)}, bf16[64,4096]{1,0:T(8,128)(2,1)S(1)}, u32[]{:S(2)}, u32[]{:S(2)}) collective-permute-start(bf16[64,4096]{1,0:T(8,128)(2,1)S(1)} %get-tuple-element.27), channel_id=1, source_target_pairs={{0,224},{4,228},{8,232},{12,236},{16,240},{20,244},{24,248},{28,25... | collective-permute-start | bytes 1572872 | tf_op jit(solution)/shard_map/ppermute | solution.py:101
  72.0 11.1 %collective-permute-start.13 = (bf16[64,4096]{1,0:T(8,128)(2,1)S(1)}, bf16[64,4096]{1,0:T(8,128)(2,1)S(1)}, u32[]{:S(2)}, u32[]{:S(2)}) collective-permute-start(bf16[64,4096]{1,0:T(8,128)(2,1)S(1)} %get-tuple-element.30), channel_id=1, source_target_pairs={{0,32},{4,36},{8,40},{12,44},{16,48},{20,52},{24,56},{28,60},{32,0... | collective-permute-start | bytes 1572872 | tf_op jit(solution)/shard_map/ppermute | solution.py:101
  75.7 30.0 %collective-permute-start.6 = (bf16[64,4096]{1,0:T(8,128)(2,1)S(1)}, bf16[64,4096]{1,0:T(8,128)(2,1)S(1)}, u32[]{:S(2)}, u32[]{:S(2)}) collective-permute-start(bf16[64,4096]{1,0:T(8,128)(2,1)S(1)} %multiply_convert_fusion), channel_id=1, source_target_pairs={{0,128},{4,132},{8,136},{12,140},{16,144},{20,148},{24,152},{28,15... | collective-permute-start | bytes 1572872 | tf_op jit(solution)/shard_map/ppermute | solution.py:143
  81.2 18.0 %collective-permute-start.11 = (bf16[64,4096]{1,0:T(8,128)(2,1)S(1)}, bf16[64,4096]{1,0:T(8,128)(2,1)S(1)}, u32[]{:S(2)}, u32[]{:S(2)}) collective-permute-start(bf16[64,4096]{1,0:T(8,128)(2,1)S(1)} %add_convert_fusion.3), channel_id=1, source_target_pairs={{0,32},{4,36},{8,40},{12,44},{16,48},{20,52},{24,56},{28,60},{32,0... | collective-permute-start | bytes 1572872 | tf_op jit(solution)/shard_map/ppermute | solution.py:101
  83.3 19.1 %collective-permute-start.14 = (bf16[64,4096]{1,0:T(8,128)(2,1)S(1)}, bf16[64,4096]{1,0:T(8,128)(2,1)S(1)}, u32[]{:S(2)}, u32[]{:S(2)}) collective-permute-start(bf16[64,4096]{1,0:T(8,128)(2,1)S(1)} %add_convert_fusion.1), channel_id=1, source_target_pairs={{0,224},{4,228},{8,232},{12,236},{16,240},{20,244},{24,248},{28,25... | collective-permute-start | bytes 1572872 | tf_op jit(solution)/shard_map/ppermute | solution.py:101
  99.3 11.4 %collective-permute-start.12 = (bf16[64,4096]{1,0:T(8,128)(2,1)S(1)}, bf16[64,4096]{1,0:T(8,128)(2,1)S(1)}, u32[]{:S(2)}, u32[]{:S(2)}) collective-permute-start(bf16[64,4096]{1,0:T(8,128)(2,1)S(1)} %add_convert_fusion.2), channel_id=1, source_target_pairs={{0,224},{4,228},{8,232},{12,236},{16,240},{20,244},{24,248},{28,25... | collective-permute-start | bytes 1572872 | tf_op jit(solution)/shard_map/ppermute | solution.py:101
  102.4 10.2 %collective-permute-start.15 = (bf16[64,4096]{1,0:T(8,128)(2,1)S(1)}, bf16[64,4096]{1,0:T(8,128)(2,1)S(1)}, u32[]{:S(2)}, u32[]{:S(2)}) collective-permute-start(bf16[64,4096]{1,0:T(8,128)(2,1)S(1)} %add_convert_fusion), channel_id=1, source_target_pairs={{0,32},{4,36},{8,40},{12,44},{16,48},{20,52},{24,56},{28,60},{32,0... | collective-permute-start | bytes 1572872 | tf_op jit(solution)/shard_map/ppermute | solution.py:101
  129.2 9.8 %collective-permute-start.16 = (bf16[8,4096]{1,0:T(8,128)(2,1)S(1)}, bf16[8,4096]{1,0:T(8,128)(2,1)S(1)}, u32[]{:S(2)}, u32[]{:S(2)}) collective-permute-start(bf16[8,4096]{1,0:T(8,128)(2,1)S(1)} %reduce_sum.62), channel_id=1, source_target_pairs={{0,256},{256,0},{1,257},{257,1},{2,258},{258,2},{3,259},{259,3},{4... | collective-permute-start | bytes 196616 | tf_op jit(solution)/shard_map/ppermute | solution.py:165

commit v6 on v5

--- a/solution.py
+++ b/solution.py
@@ -17,14 +17,14 @@
     along_z = [[y * SIDE + z for z in range(SIDE)] for y in range(SIDE)]
     along_y = [[y * SIDE + z for y in range(SIDE)] for z in range(SIDE)]
     shift = SIDE * SIDE
-    return along_z + [[shift + i for i in group] for group in along_y]
+    return along_y + [[shift + i for i in group] for group in along_z]
 
 
 def second_axis(other):
     places = [(y, z) for y in range(SIDE) for z in range(SIDE)]
     shift = SIDE * SIDE
-    pairs = [(y * SIDE + z, other(y) * SIDE + z) for y, z in places]
-    return pairs + [(shift + y * SIDE + z, shift + y * SIDE + other(z)) for y, z in places]
+    pairs = [(y * SIDE + z, y * SIDE + other(z)) for y, z in places]
+    return pairs + [(shift + y * SIDE + z, shift + other(y) * SIDE + z) for y, z in places]
 
 
 def neighbour_swap(odd):

time: 140 us -> 140 us (level)
  waiting for transfers between devices: 41.2 us -> 44.5 us
  starting transfers between devices: 68.7 us -> 65.5 us
    ppermute x6, starting transfers between devices: 26.5 us -> 17.6 us  [swap_both(): lax.ppermute(to_one, AXES, pairs[0])]
    ppermute x1, starting transfers between devices: 1.94 us -> 6.72 us  [body(): gate_up_other = lax.ppermute(gate_up, 'pool', SWAP)]
    all_to_all x1, starting transfers between devices: 7.66 us -> 10.9 us  [body(): lax.all_to_all(spread, AXES, split_axis=0, concat_axis=0, tiled=True, axi...]
    ppermute x6, waiting for transfers between devices: 2.5 us -> 5.14 us  [swap_both(): lax.ppermute(to_two, AXES, pairs[1])]
    ppermute x6, starting transfers between devices: 13.7 us -> 15.4 us  [swap_both(): lax.ppermute(to_two, AXES, pairs[1])]
    ppermute x1, starting transfers between devices: 8.95 us -> 7.28 us  [body(): other = lax.ppermute(total, 'pool', SWAP)]
    ppermute x1, starting transfers between devices: 5.44 us -> 3.82 us  [body(): from_far = lax.ppermute(far_part, AXES, opposite)]
  transfers between devices with their start and end apart: 18 -> 18, of which waited for: 8 -> 9; matrix products, arithmetic and copies ran while one was open for 7% -> 7% of each run, Pallas kernels for 0% -> 0%
where the time goes in v6:
time: 140 us
  starting transfers between devices  65.5 us (47%)
  waiting for transfers between devices  44.5 us (32%)
  blocking collectives  15.8 us (11%)
  matrix products  8.63 us (6%)
  Pallas kernels  2.02 us (1%)
  other arithmetic  1.44 us (1%)
    ppermute x6, waiting for transfers between devices, swap_both(): lax.ppermute(to_one, AXES, pairs[0])  25.9 us
    ppermute x6, starting transfers between devices, swap_both(): lax.ppermute(to_one, AXES, pairs[0])  17.6 us
    all_to_all x1, blocking collectives, body(): lax.all_to_all(summed.astype(jnp.bfloat16).reshape(SIDE, half, width), AX...  15.8 us
    ppermute x6, starting transfers between devices, swap_both(): lax.ppermute(to_two, AXES, pairs[1])  15.4 us
    all_to_all x1, waiting for transfers between devices, body(): lax.all_to_all(spread, AXES, split_axis=0, concat_axis=0, tiled=True, axi...  12.5 us
    all_to_all x1, starting transfers between devices, body(): lax.all_to_all(spread, AXES, split_axis=0, concat_axis=0, tiled=True, axi...  10.9 us
    ppermute x1, starting transfers between devices, body(): other = lax.ppermute(total, 'pool', SWAP)  7.28 us
    ppermute x1, starting transfers between devices, body(): gate_up_other = lax.ppermute(gate_up, 'pool', SWAP)  6.72 us
  transfers between devices with their start and end apart: 18, of which 9 were waited for; matrix products, arithmetic and copies ran while one was open for 7% of the time, Pallas kernels for 0%

profile of v6, /device:TPU:1, one launch (start us, length us, event | category | flops | bytes accessed | tf_op | source)
XLA Modules:
  0.0 139.7 jit_solution(15270882687882929061)
XLA Ops:
  0.0 2.0 %shard_map.64 = bf16[64,4224]{1,0:T(8,128)(2,1)} custom-call(s32[1]{0:T(128)} %bitcast.pool_ref, bf16[16,4096]{1,0:T(8,128)(2,1)} %refs_0_.1, s32[8,16]{1,0:T(8,128)} %bitcast.44, f32[8,16]{1,0:T(8,128)} %bitcast.45), custom_call_target="tpu_custom_call" | custom-call | tf_op jit(solution)/shard_map/pallas_call | solution.py:72
  2.0 10.9 %all-to-all-start = ((bf16[8,8,4224]{2,1,0:T(8,128)(2,1)}), bf16[8,8,4224]{2,1,0:T(8,128)(2,1)S(1)}, u32[]{:S(2)}, u32[]{:S(2)}) async-start(bf16[8,8,4224]{2,1,0:T(8,128)(2,1)} %bitcast.41), calls=%async_computation | async-start | bytes 1081344 | tf_op jit(solution)/shard_map/all_to_all | solution.py:95
  12.9 12.5 %all-to-all-done = bf16[8,8,4224]{2,1,0:T(8,128)(2,1)S(1)} async-done(((bf16[8,8,4224]{2,1,0:T(8,128)(2,1)}), bf16[8,8,4224]{2,1,0:T(8,128)(2,1)S(1)}, u32[]{:S(2)}, u32[]{:S(2)}) %all-to-all-start) | async-done | bytes 540704 | tf_op jit(solution)/shard_map/all_to_all | solution.py:95
  25.5 4.9 %collective-permute-start.2 = (bf16[64,4224]{1,0:T(8,128)(2,1)S(1)}, bf16[64,4224]{1,0:T(8,128)(2,1)S(1)}, u32[]{:S(2)}, u32[]{:S(2)}) collective-permute-start(bf16[64,4224]{1,0:T(8,128)(2,1)S(1)} %bitcast.36), channel_id=1, source_target_pairs={{0,28},{4,8},{8,4},{12,16},{16,12},{20,24},{24,20},{28,0},{32,60},... | collective-permute-start | bytes 1622024 | tf_op jit(solution)/shard_map/ppermute | solution.py:101
  30.3 1.9 %collective-permute-start.7 = (bf16[64,4224]{1,0:T(8,128)(2,1)S(1)}, bf16[64,4224]{1,0:T(8,128)(2,1)S(1)}, u32[]{:S(2)}, u32[]{:S(2)}) collective-permute-start(bf16[64,4224]{1,0:T(8,128)(2,1)S(1)} %bitcast.37), channel_id=1, source_target_pairs={{0,4},{4,0},{8,12},{12,8},{16,20},{20,16},{24,28},{28,24},{32,36},... | collective-permute-start | bytes 1622024 | tf_op jit(solution)/shard_map/ppermute | solution.py:101
  32.7 6.7 %collective-permute-start = (bf16[4096,256]{1,0:T(8,128)(2,1)S(1)}, bf16[4096,256]{1,0:T(8,128)(2,1)S(1)}, u32[]{:S(2)}, u32[]{:S(2)}) collective-permute-start(bf16[4096,256]{1,0:T(8,128)(2,1)S(1)} %constant_dynamic-update-slice_fusion), channel_id=1, source_target_pairs={{0,256},{256,0},{1,257},{257,1},{2,258},{258,2},{3,259},{259,3},{4... | collective-permute-start | bytes 6291464 | tf_op jit(solution)/shard_map/ppermute | solution.py:116
  39.5 1.9 %collective-permute-start.1 = (bf16[128,4096]{1,0:T(8,128)(2,1)S(1)}, bf16[128,4096]{1,0:T(8,128)(2,1)S(1)}, u32[]{:S(2)}, u32[]{:S(2)}) collective-permute-start(bf16[128,4096]{1,0:T(8,128)(2,1)S(1)} %bitcast.30), channel_id=1, source_target_pairs={{0,256},{256,0},{1,257},{257,1},{2,258},{258,2},{3,259},{259,3},{4... | collective-permute-start | bytes 3145736 | tf_op jit(solution)/shard_map/ppermute | solution.py:117
  41.4 0.5 fusion.27
  41.9 2.2 %collective-permute-start.3 = (bf16[64,4224]{1,0:T(8,128)(2,1)S(1)}, bf16[64,4224]{1,0:T(8,128)(2,1)S(1)}, u32[]{:S(2)}, u32[]{:S(2)}) collective-permute-start(bf16[64,4224]{1,0:T(8,128)(2,1)S(1)} %collective-permute-done.2), channel_id=1, source_target_pairs={{0,4},{4,0},{8,12},{12,8},{16,20},{20,16},{24,28},{28,24},{32,36},... | collective-permute-start | bytes 1622024 | tf_op jit(solution)/shard_map/ppermute | solution.py:101
  44.2 1.9 %collective-permute-start.8 = (bf16[64,4224]{1,0:T(8,128)(2,1)S(1)}, bf16[64,4224]{1,0:T(8,128)(2,1)S(1)}, u32[]{:S(2)}, u32[]{:S(2)}) collective-permute-start(bf16[64,4224]{1,0:T(8,128)(2,1)S(1)} %collective-permute-done.7), channel_id=1, source_target_pairs={{0,28},{4,8},{8,4},{12,16},{16,12},{20,24},{24,20},{28,0},{32,60},... | collective-permute-start | bytes 1622024 | tf_op jit(solution)/shard_map/ppermute | solution.py:101
  46.2 0.4 fusion.19
  46.6 0.4 fusion.35
  47.1 5.2 %collective-permute-done.3 = bf16[64,4224]{1,0:T(8,128)(2,1)S(1)} collective-permute-done((bf16[64,4224]{1,0:T(8,128)(2,1)S(1)}, bf16[64,4224]{1,0:T(8,128)(2,1)S(1)}, u32[]{:S(2)}, u32[]{:S(2)}) %collective-permute-start.3) | collective-permute-done | bytes 540704 | tf_op jit(solution)/shard_map/ppermute | solution.py:101
  52.3 1.9 %collective-permute-start.4 = (bf16[64,4224]{1,0:T(8,128)(2,1)S(1)}, bf16[64,4224]{1,0:T(8,128)(2,1)S(1)}, u32[]{:S(2)}, u32[]{:S(2)}) collective-permute-start(bf16[64,4224]{1,0:T(8,128)(2,1)S(1)} %collective-permute-done.3), channel_id=1, source_target_pairs={{0,28},{4,8},{8,4},{12,16},{16,12},{20,24},{24,20},{28,0},{32,60},... | collective-permute-start | bytes 1622024 | tf_op jit(solution)/shard_map/ppermute | solution.py:101
  54.2 1.6 %collective-permute-done.8 = bf16[64,4224]{1,0:T(8,128)(2,1)S(1)} collective-permute-done((bf16[64,4224]{1,0:T(8,128)(2,1)S(1)}, bf16[64,4224]{1,0:T(8,128)(2,1)S(1)}, u32[]{:S(2)}, u32[]{:S(2)}) %collective-permute-start.8) | collective-permute-done | bytes 540704 | tf_op jit(solution)/shard_map/ppermute | solution.py:101
  55.8 1.9 %collective-permute-start.9 = (bf16[64,4224]{1,0:T(8,128)(2,1)S(1)}, bf16[64,4224]{1,0:T(8,128)(2,1)S(1)}, u32[]{:S(2)}, u32[]{:S(2)}) collective-permute-start(bf16[64,4224]{1,0:T(8,128)(2,1)S(1)} %collective-permute-done.8), channel_id=1, source_target_pairs={{0,4},{4,0},{8,12},{12,8},{16,20},{20,16},{24,28},{28,24},{32,36},... | collective-permute-start | bytes 1622024 | tf_op jit(solution)/shard_map/ppermute | solution.py:101
  57.9 0.4 fusion.15
  58.4 0.4 fusion.38
  58.8 5.1 %collective-permute-done.4 = bf16[64,4224]{1,0:T(8,128)(2,1)S(1)} collective-permute-done((bf16[64,4224]{1,0:T(8,128)(2,1)S(1)}, bf16[64,4224]{1,0:T(8,128)(2,1)S(1)}, u32[]{:S(2)}, u32[]{:S(2)}) %collective-permute-start.4) | collective-permute-done | bytes 540704 | tf_op jit(solution)/shard_map/ppermute | solution.py:101
  63.9 1.9 %collective-permute-start.5 = (bf16[64,4224]{1,0:T(8,128)(2,1)S(1)}, bf16[64,4224]{1,0:T(8,128)(2,1)S(1)}, u32[]{:S(2)}, u32[]{:S(2)}) collective-permute-start(bf16[64,4224]{1,0:T(8,128)(2,1)S(1)} %collective-permute-done.4), channel_id=1, source_target_pairs={{0,4},{4,0},{8,12},{12,8},{16,20},{20,16},{24,28},{28,24},{32,36},... | collective-permute-start | bytes 1622024 | tf_op jit(solution)/shard_map/ppermute | solution.py:110
  65.8 0.4 fusion.13
  66.3 0.4 fusion.1
  66.7 0.4 fusion.17
  67.2 0.4 fusion.2
  67.7 0.4 fusion.11
  68.3 0.4 fusion.41
  68.7 0.4 fusion.9
  69.2 0.4 fusion
  69.7 1.9 %collective-permute-start.10 = (bf16[64,4096]{1,0:T(8,128)(2,1)S(1)}, bf16[64,4096]{1,0:T(8,128)(2,1)S(1)}, u32[]{:S(2)}, u32[]{:S(2)}) collective-permute-start(bf16[64,4096]{1,0:T(8,128)(2,1)S(1)} %get-tuple-element.27), channel_id=1, source_target_pairs={{0,28},{4,8},{8,4},{12,16},{16,12},{20,24},{24,20},{28,0},{32,60},... | collective-permute-start | bytes 1572872 | tf_op jit(solution)/shard_map/ppermute | solution.py:101
  71.7 0.4 fusion.77
  72.1 3.4 %collective-permute-start.13 = (bf16[64,4096]{1,0:T(8,128)(2,1)S(1)}, bf16[64,4096]{1,0:T(8,128)(2,1)S(1)}, u32[]{:S(2)}, u32[]{:S(2)}) collective-permute-start(bf16[64,4096]{1,0:T(8,128)(2,1)S(1)} %get-tuple-element.30), channel_id=1, source_target_pairs={{0,4},{4,0},{8,12},{12,8},{16,20},{20,16},{24,28},{28,24},{32,36},... | collective-permute-start | bytes 1572872 | tf_op jit(solution)/shard_map/ppermute | solution.py:101
  75.6 0.5 fusion.23
  76.1 0.5 fusion.21
  76.9 0.3 multiply_convert_fusion
  77.2 3.8 %collective-permute-start.6 = (bf16[64,4096]{1,0:T(8,128)(2,1)S(1)}, bf16[64,4096]{1,0:T(8,128)(2,1)S(1)}, u32[]{:S(2)}, u32[]{:S(2)}) collective-permute-start(bf16[64,4096]{1,0:T(8,128)(2,1)S(1)} %multiply_convert_fusion), channel_id=1, source_target_pairs={{0,16},{4,20},{8,24},{12,28},{16,0},{20,4},{24,8},{28,12},{32,48},... | collective-permute-start | bytes 1572872 | tf_op jit(solution)/shard_map/ppermute | solution.py:143
  81.3 2.3 %collective-permute-start.11 = (bf16[64,4096]{1,0:T(8,128)(2,1)S(1)}, bf16[64,4096]{1,0:T(8,128)(2,1)S(1)}, u32[]{:S(2)}, u32[]{:S(2)}) collective-permute-start(bf16[64,4096]{1,0:T(8,128)(2,1)S(1)} %add_convert_fusion.3), channel_id=1, source_target_pairs={{0,4},{4,0},{8,12},{12,8},{16,20},{20,16},{24,28},{28,24},{32,36},... | collective-permute-start | bytes 1572872 | tf_op jit(solution)/shard_map/ppermute | solution.py:101
  83.7 4.3 %collective-permute-start.14 = (bf16[64,4096]{1,0:T(8,128)(2,1)S(1)}, bf16[64,4096]{1,0:T(8,128)(2,1)S(1)}, u32[]{:S(2)}, u32[]{:S(2)}) collective-permute-start(bf16[64,4096]{1,0:T(8,128)(2,1)S(1)} %add_convert_fusion.1), channel_id=1, source_target_pairs={{0,28},{4,8},{8,4},{12,16},{16,12},{20,24},{24,20},{28,0},{32,60},... | collective-permute-start | bytes 1572872 | tf_op jit(solution)/shard_map/ppermute | solution.py:101
  87.9 11.7 %collective-permute-done.11 = bf16[64,4096]{1,0:T(8,128)(2,1)S(1)} collective-permute-done((bf16[64,4096]{1,0:T(8,128)(2,1)S(1)}, bf16[64,4096]{1,0:T(8,128)(2,1)S(1)}, u32[]{:S(2)}, u32[]{:S(2)}) %collective-permute-start.11) | collective-permute-done | bytes 524320 | tf_op jit(solution)/shard_map/ppermute | solution.py:101
  99.7 4.3 %collective-permute-start.12 = (bf16[64,4096]{1,0:T(8,128)(2,1)S(1)}, bf16[64,4096]{1,0:T(8,128)(2,1)S(1)}, u32[]{:S(2)}, u32[]{:S(2)}) collective-permute-start(bf16[64,4096]{1,0:T(8,128)(2,1)S(1)} %add_convert_fusion.2), channel_id=1, source_target_pairs={{0,28},{4,8},{8,4},{12,16},{16,12},{20,24},{24,20},{28,0},{32,60},... | collective-permute-start | bytes 1572872 | tf_op jit(solution)/shard_map/ppermute | solution.py:101
  104.2 2.0 %collective-permute-start.15 = (bf16[64,4096]{1,0:T(8,128)(2,1)S(1)}, bf16[64,4096]{1,0:T(8,128)(2,1)S(1)}, u32[]{:S(2)}, u32[]{:S(2)}) collective-permute-start(bf16[64,4096]{1,0:T(8,128)(2,1)S(1)} %add_convert_fusion), channel_id=1, source_target_pairs={{0,4},{4,0},{8,12},{12,8},{16,20},{20,16},{24,28},{28,24},{32,36},... | collective-permute-start | bytes 1572872 | tf_op jit(solution)/shard_map/ppermute | solution.py:101
  106.5 0.5 fusion.25
  107.0 3.8 %collective-permute-done.12 = bf16[64,4096]{1,0:T(8,128)(2,1)S(1)} collective-permute-done((bf16[64,4096]{1,0:T(8,128)(2,1)S(1)}, bf16[64,4096]{1,0:T(8,128)(2,1)S(1)}, u32[]{:S(2)}, u32[]{:S(2)}) %collective-permute-start.12) | collective-permute-done | bytes 524320 | tf_op jit(solution)/shard_map/ppermute | solution.py:101
  110.8 3.5 %collective-permute-done.15 = bf16[64,4096]{1,0:T(8,128)(2,1)S(1)} collective-permute-done((bf16[64,4096]{1,0:T(8,128)(2,1)S(1)}, bf16[64,4096]{1,0:T(8,128)(2,1)S(1)}, u32[]{:S(2)}, u32[]{:S(2)}) %collective-permute-start.15) | collective-permute-done | bytes 524320 | tf_op jit(solution)/shard_map/ppermute | solution.py:101
  114.4 0.5 fusion.8
  114.9 15.8 %all_to_all.10 = bf16[8,8,4096]{2,1,0:T(8,128)(2,1)S(1)} all-to-all(bf16[8,8,4096]{2,1,0:T(8,128)(2,1)S(1)} %fusion.8), channel_id=1, replica_groups={{0,32,64,96,128,160,192,224},{4,36,68,100,132,164,196,228},{8,40,72,104..., dimensions={0} | all-to-all | bytes 1048576 | tf_op jit(solution)/shard_map/all_to_all | solution.py:156
  130.8 7.3 %collective-permute-start.16 = (bf16[8,4096]{1,0:T(8,128)(2,1)S(1)}, bf16[8,4096]{1,0:T(8,128)(2,1)S(1)}, u32[]{:S(2)}, u32[]{:S(2)}) collective-permute-start(bf16[8,4096]{1,0:T(8,128)(2,1)S(1)} %reduce_sum.62), channel_id=1, source_target_pairs={{0,256},{256,0},{1,257},{257,1},{2,258},{258,2},{3,259},{259,3},{4... | collective-permute-start | bytes 196616 | tf_op jit(solution)/shard_map/ppermute | solution.py:165
  138.1 0.9 collective-permute-done.16
  139.0 0.7 pad_maximum_fusion
  (37 shorter events, 2.3 us)
Async XLA Ops:
  0.0 32.3 %copy-start.1 = (bf16[1,4096,128]{2,1,0:T(8,128)(2,1)S(1)}, bf16[1,4096,128]{2,1,0:T(8,128)(2,1)}, u32[]{:S(2)}) copy-start(bf16[1,4096,128]{2,1,0:T(8,128)(2,1)} %param.9) | copy-start | bytes 3145732
  0.0 32.5 %copy-start.2 = (bf16[1,4096,128]{2,1,0:T(8,128)(2,1)S(1)}, bf16[1,4096,128]{2,1,0:T(8,128)(2,1)}, u32[]{:S(2)}) copy-start(bf16[1,4096,128]{2,1,0:T(8,128)(2,1)} %param.10) | copy-start | bytes 3145732
  2.0 23.4 %all-to-all-start = ((bf16[8,8,4224]{2,1,0:T(8,128)(2,1)}), bf16[8,8,4224]{2,1,0:T(8,128)(2,1)S(1)}, u32[]{:S(2)}, u32[]{:S(2)}) async-start(bf16[8,8,4224]{2,1,0:T(8,128)(2,1)} %bitcast.41), calls=%async_computation | async-start | bytes 1081344 | tf_op jit(solution)/shard_map/all_to_all | solution.py:95
  25.5 16.4 %collective-permute-start.2 = (bf16[64,4224]{1,0:T(8,128)(2,1)S(1)}, bf16[64,4224]{1,0:T(8,128)(2,1)S(1)}, u32[]{:S(2)}, u32[]{:S(2)}) collective-permute-start(bf16[64,4224]{1,0:T(8,128)(2,1)S(1)} %bitcast.36), channel_id=1, source_target_pairs={{0,28},{4,8},{8,4},{12,16},{16,12},{20,24},{24,20},{28,0},{32,60},... | collective-permute-start | bytes 1622024 | tf_op jit(solution)/shard_map/ppermute | solution.py:101
  30.3 13.9 %collective-permute-start.7 = (bf16[64,4224]{1,0:T(8,128)(2,1)S(1)}, bf16[64,4224]{1,0:T(8,128)(2,1)S(1)}, u32[]{:S(2)}, u32[]{:S(2)}) collective-permute-start(bf16[64,4224]{1,0:T(8,128)(2,1)S(1)} %bitcast.37), channel_id=1, source_target_pairs={{0,4},{4,0},{8,12},{12,8},{16,20},{20,16},{24,28},{28,24},{32,36},... | collective-permute-start | bytes 1622024 | tf_op jit(solution)/shard_map/ppermute | solution.py:101
  32.3 7.2 %copy-start = (bf16[1,128,4096]{2,1,0:T(8,128)(2,1)S(1)}, bf16[1,128,4096]{2,1,0:T(8,128)(2,1)}, u32[]{:S(2)}) copy-start(bf16[1,128,4096]{2,1,0:T(8,128)(2,1)} %param.11) | copy-start | bytes 3145732
  32.7 33.1 %collective-permute-start = (bf16[4096,256]{1,0:T(8,128)(2,1)S(1)}, bf16[4096,256]{1,0:T(8,128)(2,1)S(1)}, u32[]{:S(2)}, u32[]{:S(2)}) collective-permute-start(bf16[4096,256]{1,0:T(8,128)(2,1)S(1)} %constant_dynamic-update-slice_fusion), channel_id=1, source_target_pairs={{0,256},{256,0},{1,257},{257,1},{2,258},{258,2},{3,259},{259,3},{4... | collective-permute-start | bytes 6291464 | tf_op jit(solution)/shard_map/ppermute | solution.py:116
  39.5 26.8 %collective-permute-start.1 = (bf16[128,4096]{1,0:T(8,128)(2,1)S(1)}, bf16[128,4096]{1,0:T(8,128)(2,1)S(1)}, u32[]{:S(2)}, u32[]{:S(2)}) collective-permute-start(bf16[128,4096]{1,0:T(8,128)(2,1)S(1)} %bitcast.30), channel_id=1, source_target_pairs={{0,256},{256,0},{1,257},{257,1},{2,258},{258,2},{3,259},{259,3},{4... | collective-permute-start | bytes 3145736 | tf_op jit(solution)/shard_map/ppermute | solution.py:117
  41.9 10.4 %collective-permute-start.3 = (bf16[64,4224]{1,0:T(8,128)(2,1)S(1)}, bf16[64,4224]{1,0:T(8,128)(2,1)S(1)}, u32[]{:S(2)}, u32[]{:S(2)}) collective-permute-start(bf16[64,4224]{1,0:T(8,128)(2,1)S(1)} %collective-permute-done.2), channel_id=1, source_target_pairs={{0,4},{4,0},{8,12},{12,8},{16,20},{20,16},{24,28},{28,24},{32,36},... | collective-permute-start | bytes 1622024 | tf_op jit(solution)/shard_map/ppermute | solution.py:101
  44.2 11.6 %collective-permute-start.8 = (bf16[64,4224]{1,0:T(8,128)(2,1)S(1)}, bf16[64,4224]{1,0:T(8,128)(2,1)S(1)}, u32[]{:S(2)}, u32[]{:S(2)}) collective-permute-start(bf16[64,4224]{1,0:T(8,128)(2,1)S(1)} %collective-permute-done.7), channel_id=1, source_target_pairs={{0,28},{4,8},{8,4},{12,16},{16,12},{20,24},{24,20},{28,0},{32,60},... | collective-permute-start | bytes 1622024 | tf_op jit(solution)/shard_map/ppermute | solution.py:101
  52.3 11.6 %collective-permute-start.4 = (bf16[64,4224]{1,0:T(8,128)(2,1)S(1)}, bf16[64,4224]{1,0:T(8,128)(2,1)S(1)}, u32[]{:S(2)}, u32[]{:S(2)}) collective-permute-start(bf16[64,4224]{1,0:T(8,128)(2,1)S(1)} %collective-permute-done.3), channel_id=1, source_target_pairs={{0,28},{4,8},{8,4},{12,16},{16,12},{20,24},{24,20},{28,0},{32,60},... | collective-permute-start | bytes 1622024 | tf_op jit(solution)/shard_map/ppermute | solution.py:101
  55.8 11.8 %collective-permute-start.9 = (bf16[64,4224]{1,0:T(8,128)(2,1)S(1)}, bf16[64,4224]{1,0:T(8,128)(2,1)S(1)}, u32[]{:S(2)}, u32[]{:S(2)}) collective-permute-start(bf16[64,4224]{1,0:T(8,128)(2,1)S(1)} %collective-permute-done.8), channel_id=1, source_target_pairs={{0,4},{4,0},{8,12},{12,8},{16,20},{20,16},{24,28},{28,24},{32,36},... | collective-permute-start | bytes 1622024 | tf_op jit(solution)/shard_map/ppermute | solution.py:101
  63.9 11.6 %collective-permute-start.5 = (bf16[64,4224]{1,0:T(8,128)(2,1)S(1)}, bf16[64,4224]{1,0:T(8,128)(2,1)S(1)}, u32[]{:S(2)}, u32[]{:S(2)}) collective-permute-start(bf16[64,4224]{1,0:T(8,128)(2,1)S(1)} %collective-permute-done.4), channel_id=1, source_target_pairs={{0,4},{4,0},{8,12},{12,8},{16,20},{20,16},{24,28},{28,24},{32,36},... | collective-permute-start | bytes 1622024 | tf_op jit(solution)/shard_map/ppermute | solution.py:110
  69.7 11.4 %collective-permute-start.10 = (bf16[64,4096]{1,0:T(8,128)(2,1)S(1)}, bf16[64,4096]{1,0:T(8,128)(2,1)S(1)}, u32[]{:S(2)}, u32[]{:S(2)}) collective-permute-start(bf16[64,4096]{1,0:T(8,128)(2,1)S(1)} %get-tuple-element.27), channel_id=1, source_target_pairs={{0,28},{4,8},{8,4},{12,16},{16,12},{20,24},{24,20},{28,0},{32,60},... | collective-permute-start | bytes 1572872 | tf_op jit(solution)/shard_map/ppermute | solution.py:101
  72.1 11.4 %collective-permute-start.13 = (bf16[64,4096]{1,0:T(8,128)(2,1)S(1)}, bf16[64,4096]{1,0:T(8,128)(2,1)S(1)}, u32[]{:S(2)}, u32[]{:S(2)}) collective-permute-start(bf16[64,4096]{1,0:T(8,128)(2,1)S(1)} %get-tuple-element.30), channel_id=1, source_target_pairs={{0,4},{4,0},{8,12},{12,8},{16,20},{20,16},{24,28},{28,24},{32,36},... | collective-permute-start | bytes 1572872 | tf_op jit(solution)/shard_map/ppermute | solution.py:101
  77.2 29.8 %collective-permute-start.6 = (bf16[64,4096]{1,0:T(8,128)(2,1)S(1)}, bf16[64,4096]{1,0:T(8,128)(2,1)S(1)}, u32[]{:S(2)}, u32[]{:S(2)}) collective-permute-start(bf16[64,4096]{1,0:T(8,128)(2,1)S(1)} %multiply_convert_fusion), channel_id=1, source_target_pairs={{0,16},{4,20},{8,24},{12,28},{16,0},{20,4},{24,8},{28,12},{32,48},... | collective-permute-start | bytes 1572872 | tf_op jit(solution)/shard_map/ppermute | solution.py:143
  81.3 18.3 %collective-permute-start.11 = (bf16[64,4096]{1,0:T(8,128)(2,1)S(1)}, bf16[64,4096]{1,0:T(8,128)(2,1)S(1)}, u32[]{:S(2)}, u32[]{:S(2)}) collective-permute-start(bf16[64,4096]{1,0:T(8,128)(2,1)S(1)} %add_convert_fusion.3), channel_id=1, source_target_pairs={{0,4},{4,0},{8,12},{12,8},{16,20},{20,16},{24,28},{28,24},{32,36},... | collective-permute-start | bytes 1572872 | tf_op jit(solution)/shard_map/ppermute | solution.py:101
  83.7 20.4 %collective-permute-start.14 = (bf16[64,4096]{1,0:T(8,128)(2,1)S(1)}, bf16[64,4096]{1,0:T(8,128)(2,1)S(1)}, u32[]{:S(2)}, u32[]{:S(2)}) collective-permute-start(bf16[64,4096]{1,0:T(8,128)(2,1)S(1)} %add_convert_fusion.1), channel_id=1, source_target_pairs={{0,28},{4,8},{8,4},{12,16},{16,12},{20,24},{24,20},{28,0},{32,60},... | collective-permute-start | bytes 1572872 | tf_op jit(solution)/shard_map/ppermute | solution.py:101
  99.7 11.1 %collective-permute-start.12 = (bf16[64,4096]{1,0:T(8,128)(2,1)S(1)}, bf16[64,4096]{1,0:T(8,128)(2,1)S(1)}, u32[]{:S(2)}, u32[]{:S(2)}) collective-permute-start(bf16[64,4096]{1,0:T(8,128)(2,1)S(1)} %add_convert_fusion.2), channel_id=1, source_target_pairs={{0,28},{4,8},{8,4},{12,16},{16,12},{20,24},{24,20},{28,0},{32,60},... | collective-permute-start | bytes 1572872 | tf_op jit(solution)/shard_map/ppermute | solution.py:101
  104.2 10.2 %collective-permute-start.15 = (bf16[64,4096]{1,0:T(8,128)(2,1)S(1)}, bf16[64,4096]{1,0:T(8,128)(2,1)S(1)}, u32[]{:S(2)}, u32[]{:S(2)}) collective-permute-start(bf16[64,4096]{1,0:T(8,128)(2,1)S(1)} %add_convert_fusion), channel_id=1, source_target_pairs={{0,4},{4,0},{8,12},{12,8},{16,20},{20,16},{24,28},{28,24},{32,36},... | collective-permute-start | bytes 1572872 | tf_op jit(solution)/shard_map/ppermute | solution.py:101
  130.8 8.2 %collective-permute-start.16 = (bf16[8,4096]{1,0:T(8,128)(2,1)S(1)}, bf16[8,4096]{1,0:T(8,128)(2,1)S(1)}, u32[]{:S(2)}, u32[]{:S(2)}) collective-permute-start(bf16[8,4096]{1,0:T(8,128)(2,1)S(1)} %reduce_sum.62), channel_id=1, source_target_pairs={{0,256},{256,0},{1,257},{257,1},{2,258},{258,2},{3,259},{259,3},{4... | collective-permute-start | bytes 196616 | tf_op jit(solution)/shard_map/ppermute | solution.py:165

commit v7 on v6

--- a/solution.py
+++ b/solution.py
@@ -97,7 +97,7 @@
     ).reshape(SIDE * half, width + PAD)
 
     def swap_both(to_one, to_two, step):
-        pairs = (odd_pairs, even_pairs) if step % 2 else (even_pairs, odd_pairs)
+        pairs = (even_pairs, odd_pairs) if step % 2 else (odd_pairs, even_pairs)
         return lax.ppermute(to_one, AXES, pairs[0]), lax.ppermute(to_two, AXES, pairs[1])
 
     one_in, two_in = [own], [own]
@@ -107,7 +107,7 @@
         one_in.append(from_one)
         two_in.append(from_two)
 
-    far = lax.ppermute(one_in[REACH], AXES, even_pairs)
+    far = lax.ppermute(one_in[REACH], AXES, odd_pairs)
 
     gate_part, up_part, down, _ = lax.optimization_barrier(
         (gate_weight[0], up_weight[0], down_weight[0], own)

time: 140 us -> 142 us (1.014)
  starting transfers between devices: 65.5 us -> 69.1 us
    ppermute x6, starting transfers between devices: 15.4 us -> 22.6 us  [swap_both(): lax.ppermute(to_two, AXES, pairs[1])]
    ppermute x6, starting transfers between devices: 17.6 us -> 12.8 us  [swap_both(): lax.ppermute(to_one, AXES, pairs[0])]
    ppermute x6, waiting for transfers between devices: 5.14 us -> 3.27 us  [swap_both(): lax.ppermute(to_two, AXES, pairs[1])]
    ppermute x1, starting transfers between devices: 7.28 us -> 8.86 us  [body(): other = lax.ppermute(total, 'pool', SWAP)]
  transfers between devices with their start and end apart: 18 -> 18, of which waited for: 9 -> 7; matrix products, arithmetic and copies ran while one was open for 7% -> 7% of each run, Pallas kernels for 0% -> 0%
where the time goes in v7:
time: 142 us
  starting transfers between devices  69.1 us (49%)
  waiting for transfers between devices  43.5 us (31%)
  blocking collectives  15.1 us (11%)
  matrix products  8.63 us (6%)
  Pallas kernels  2.02 us (1%)
  other arithmetic  1.44 us (1%)
    ppermute x6, waiting for transfers between devices, swap_both(): lax.ppermute(to_one, AXES, pairs[0])  26.9 us
    ppermute x6, starting transfers between devices, swap_both(): lax.ppermute(to_two, AXES, pairs[1])  22.6 us
    all_to_all x1, blocking collectives, body(): lax.all_to_all(summed.astype(jnp.bfloat16).reshape(SIDE, half, width), AX...  15.1 us
    ppermute x6, starting transfers between devices, swap_both(): lax.ppermute(to_one, AXES, pairs[0])  12.8 us
    all_to_all x1, waiting for transfers between devices, body(): lax.all_to_all(spread, AXES, split_axis=0, concat_axis=0, tiled=True, axi...  12.5 us
    all_to_all x1, starting transfers between devices, body(): lax.all_to_all(spread, AXES, split_axis=0, concat_axis=0, tiled=True, axi...  10.9 us
    ppermute x1, starting transfers between devices, body(): other = lax.ppermute(total, 'pool', SWAP)  8.86 us
    ppermute x1, starting transfers between devices, body(): gate_up_other = lax.ppermute(gate_up, 'pool', SWAP)  6.13 us
  transfers between devices with their start and end apart: 18, of which 7 were waited for; matrix products, arithmetic and copies ran while one was open for 7% of the time, Pallas kernels for 0%

profile of v7, /device:TPU:1, one launch (start us, length us, event | category | flops | bytes accessed | tf_op | source)
XLA Modules:
  0.0 141.6 jit_solution(15580358562133111844)
XLA Ops:
  0.0 2.0 %shard_map.64 = bf16[64,4224]{1,0:T(8,128)(2,1)} custom-call(s32[1]{0:T(128)} %bitcast.pool_ref, bf16[16,4096]{1,0:T(8,128)(2,1)} %refs_0_.1, s32[8,16]{1,0:T(8,128)} %bitcast.44, f32[8,16]{1,0:T(8,128)} %bitcast.45), custom_call_target="tpu_custom_call" | custom-call | tf_op jit(solution)/shard_map/pallas_call | solution.py:72
  2.0 10.9 %all-to-all-start = ((bf16[8,8,4224]{2,1,0:T(8,128)(2,1)}), bf16[8,8,4224]{2,1,0:T(8,128)(2,1)S(1)}, u32[]{:S(2)}, u32[]{:S(2)}) async-start(bf16[8,8,4224]{2,1,0:T(8,128)(2,1)} %bitcast.41), calls=%async_computation | async-start | bytes 1081344 | tf_op jit(solution)/shard_map/all_to_all | solution.py:95
  12.9 12.5 %all-to-all-done = bf16[8,8,4224]{2,1,0:T(8,128)(2,1)S(1)} async-done(((bf16[8,8,4224]{2,1,0:T(8,128)(2,1)}), bf16[8,8,4224]{2,1,0:T(8,128)(2,1)S(1)}, u32[]{:S(2)}, u32[]{:S(2)}) %all-to-all-start) | async-done | bytes 540704 | tf_op jit(solution)/shard_map/all_to_all | solution.py:95
  25.5 3.0 %collective-permute-start.2 = (bf16[64,4224]{1,0:T(8,128)(2,1)S(1)}, bf16[64,4224]{1,0:T(8,128)(2,1)S(1)}, u32[]{:S(2)}, u32[]{:S(2)}) collective-permute-start(bf16[64,4224]{1,0:T(8,128)(2,1)S(1)} %bitcast.36), channel_id=1, source_target_pairs={{0,4},{4,0},{8,12},{12,8},{16,20},{20,16},{24,28},{28,24},{32,36},... | collective-permute-start | bytes 1622024 | tf_op jit(solution)/shard_map/ppermute | solution.py:101
  28.4 4.9 %collective-permute-start.7 = (bf16[64,4224]{1,0:T(8,128)(2,1)S(1)}, bf16[64,4224]{1,0:T(8,128)(2,1)S(1)}, u32[]{:S(2)}, u32[]{:S(2)}) collective-permute-start(bf16[64,4224]{1,0:T(8,128)(2,1)S(1)} %bitcast.37), channel_id=1, source_target_pairs={{0,28},{4,8},{8,4},{12,16},{16,12},{20,24},{24,20},{28,0},{32,60},... | collective-permute-start | bytes 1622024 | tf_op jit(solution)/shard_map/ppermute | solution.py:101
  33.8 6.1 %collective-permute-start = (bf16[4096,256]{1,0:T(8,128)(2,1)S(1)}, bf16[4096,256]{1,0:T(8,128)(2,1)S(1)}, u32[]{:S(2)}, u32[]{:S(2)}) collective-permute-start(bf16[4096,256]{1,0:T(8,128)(2,1)S(1)} %constant_dynamic-update-slice_fusion), channel_id=1, source_target_pairs={{0,256},{256,0},{1,257},{257,1},{2,258},{258,2},{3,259},{259,3},{4... | collective-permute-start | bytes 6291464 | tf_op jit(solution)/shard_map/ppermute | solution.py:116
  39.9 1.9 %collective-permute-start.1 = (bf16[128,4096]{1,0:T(8,128)(2,1)S(1)}, bf16[128,4096]{1,0:T(8,128)(2,1)S(1)}, u32[]{:S(2)}, u32[]{:S(2)}) collective-permute-start(bf16[128,4096]{1,0:T(8,128)(2,1)S(1)} %bitcast.30), channel_id=1, source_target_pairs={{0,256},{256,0},{1,257},{257,1},{2,258},{258,2},{3,259},{259,3},{4... | collective-permute-start | bytes 3145736 | tf_op jit(solution)/shard_map/ppermute | solution.py:117
  41.9 0.5 fusion.27
  42.4 1.9 %collective-permute-start.3 = (bf16[64,4224]{1,0:T(8,128)(2,1)S(1)}, bf16[64,4224]{1,0:T(8,128)(2,1)S(1)}, u32[]{:S(2)}, u32[]{:S(2)}) collective-permute-start(bf16[64,4224]{1,0:T(8,128)(2,1)S(1)} %collective-permute-done.2), channel_id=1, source_target_pairs={{0,28},{4,8},{8,4},{12,16},{16,12},{20,24},{24,20},{28,0},{32,60},... | collective-permute-start | bytes 1622024 | tf_op jit(solution)/shard_map/ppermute | solution.py:101
  44.4 2.3 %collective-permute-start.8 = (bf16[64,4224]{1,0:T(8,128)(2,1)S(1)}, bf16[64,4224]{1,0:T(8,128)(2,1)S(1)}, u32[]{:S(2)}, u32[]{:S(2)}) collective-permute-start(bf16[64,4224]{1,0:T(8,128)(2,1)S(1)} %collective-permute-done.7), channel_id=1, source_target_pairs={{0,4},{4,0},{8,12},{12,8},{16,20},{20,16},{24,28},{28,24},{32,36},... | collective-permute-start | bytes 1622024 | tf_op jit(solution)/shard_map/ppermute | solution.py:101
  46.7 0.4 fusion.19
  47.2 0.4 fusion.35
  47.6 6.4 %collective-permute-done.3 = bf16[64,4224]{1,0:T(8,128)(2,1)S(1)} collective-permute-done((bf16[64,4224]{1,0:T(8,128)(2,1)S(1)}, bf16[64,4224]{1,0:T(8,128)(2,1)S(1)}, u32[]{:S(2)}, u32[]{:S(2)}) %collective-permute-start.3) | collective-permute-done | bytes 540704 | tf_op jit(solution)/shard_map/ppermute | solution.py:101
  54.0 1.9 %collective-permute-start.4 = (bf16[64,4224]{1,0:T(8,128)(2,1)S(1)}, bf16[64,4224]{1,0:T(8,128)(2,1)S(1)}, u32[]{:S(2)}, u32[]{:S(2)}) collective-permute-start(bf16[64,4224]{1,0:T(8,128)(2,1)S(1)} %collective-permute-done.3), channel_id=1, source_target_pairs={{0,4},{4,0},{8,12},{12,8},{16,20},{20,16},{24,28},{28,24},{32,36},... | collective-permute-start | bytes 1622024 | tf_op jit(solution)/shard_map/ppermute | solution.py:101
  55.9 3.1 %collective-permute-start.9 = (bf16[64,4224]{1,0:T(8,128)(2,1)S(1)}, bf16[64,4224]{1,0:T(8,128)(2,1)S(1)}, u32[]{:S(2)}, u32[]{:S(2)}) collective-permute-start(bf16[64,4224]{1,0:T(8,128)(2,1)S(1)} %collective-permute-done.8), channel_id=1, source_target_pairs={{0,28},{4,8},{8,4},{12,16},{16,12},{20,24},{24,20},{28,0},{32,60},... | collective-permute-start | bytes 1622024 | tf_op jit(solution)/shard_map/ppermute | solution.py:101
  59.2 0.5 fusion.15
  59.7 0.4 fusion.38
  60.1 4.2 %collective-permute-done.4 = bf16[64,4224]{1,0:T(8,128)(2,1)S(1)} collective-permute-done((bf16[64,4224]{1,0:T(8,128)(2,1)S(1)}, bf16[64,4224]{1,0:T(8,128)(2,1)S(1)}, u32[]{:S(2)}, u32[]{:S(2)}) %collective-permute-start.4) | collective-permute-done | bytes 540704 | tf_op jit(solution)/shard_map/ppermute | solution.py:101
  64.4 1.9 %collective-permute-start.5 = (bf16[64,4224]{1,0:T(8,128)(2,1)S(1)}, bf16[64,4224]{1,0:T(8,128)(2,1)S(1)}, u32[]{:S(2)}, u32[]{:S(2)}) collective-permute-start(bf16[64,4224]{1,0:T(8,128)(2,1)S(1)} %collective-permute-done.4), channel_id=1, source_target_pairs={{0,28},{4,8},{8,4},{12,16},{16,12},{20,24},{24,20},{28,0},{32,60},... | collective-permute-start | bytes 1622024 | tf_op jit(solution)/shard_map/ppermute | solution.py:110
  66.3 0.4 fusion.13
  66.7 0.4 fusion.1
  67.2 0.4 fusion.17
  67.6 0.4 fusion.2
  68.2 0.4 fusion.11
  68.8 0.4 fusion.41
  69.2 0.4 fusion.9
  69.6 0.5 fusion
  70.2 1.9 %collective-permute-start.10 = (bf16[64,4096]{1,0:T(8,128)(2,1)S(1)}, bf16[64,4096]{1,0:T(8,128)(2,1)S(1)}, u32[]{:S(2)}, u32[]{:S(2)}) collective-permute-start(bf16[64,4096]{1,0:T(8,128)(2,1)S(1)} %get-tuple-element.27), channel_id=1, source_target_pairs={{0,4},{4,0},{8,12},{12,8},{16,20},{20,16},{24,28},{28,24},{32,36},... | collective-permute-start | bytes 1572872 | tf_op jit(solution)/shard_map/ppermute | solution.py:101
  72.1 0.4 fusion.77
  72.6 4.6 %collective-permute-start.13 = (bf16[64,4096]{1,0:T(8,128)(2,1)S(1)}, bf16[64,4096]{1,0:T(8,128)(2,1)S(1)}, u32[]{:S(2)}, u32[]{:S(2)}) collective-permute-start(bf16[64,4096]{1,0:T(8,128)(2,1)S(1)} %get-tuple-element.30), channel_id=1, source_target_pairs={{0,28},{4,8},{8,4},{12,16},{16,12},{20,24},{24,20},{28,0},{32,60},... | collective-permute-start | bytes 1572872 | tf_op jit(solution)/shard_map/ppermute | solution.py:101
  77.3 0.5 fusion.23
  77.8 0.5 fusion.21
  78.3 0.3 fusion.57
  78.6 0.3 multiply_convert_fusion
  78.9 4.0 %collective-permute-start.6 = (bf16[64,4096]{1,0:T(8,128)(2,1)S(1)}, bf16[64,4096]{1,0:T(8,128)(2,1)S(1)}, u32[]{:S(2)}, u32[]{:S(2)}) collective-permute-start(bf16[64,4096]{1,0:T(8,128)(2,1)S(1)} %multiply_convert_fusion), channel_id=1, source_target_pairs={{0,16},{4,20},{8,24},{12,28},{16,0},{20,4},{24,8},{28,12},{32,48},... | collective-permute-start | bytes 1572872 | tf_op jit(solution)/shard_map/ppermute | solution.py:143
  83.0 2.1 %collective-permute-start.11 = (bf16[64,4096]{1,0:T(8,128)(2,1)S(1)}, bf16[64,4096]{1,0:T(8,128)(2,1)S(1)}, u32[]{:S(2)}, u32[]{:S(2)}) collective-permute-start(bf16[64,4096]{1,0:T(8,128)(2,1)S(1)} %add_convert_fusion.3), channel_id=1, source_target_pairs={{0,28},{4,8},{8,4},{12,16},{16,12},{20,24},{24,20},{28,0},{32,60},... | collective-permute-start | bytes 1572872 | tf_op jit(solution)/shard_map/ppermute | solution.py:101
  85.2 3.2 %collective-permute-start.14 = (bf16[64,4096]{1,0:T(8,128)(2,1)S(1)}, bf16[64,4096]{1,0:T(8,128)(2,1)S(1)}, u32[]{:S(2)}, u32[]{:S(2)}) collective-permute-start(bf16[64,4096]{1,0:T(8,128)(2,1)S(1)} %add_convert_fusion.1), channel_id=1, source_target_pairs={{0,4},{4,0},{8,12},{12,8},{16,20},{20,16},{24,28},{28,24},{32,36},... | collective-permute-start | bytes 1572872 | tf_op jit(solution)/shard_map/ppermute | solution.py:101
  88.4 13.8 %collective-permute-done.11 = bf16[64,4096]{1,0:T(8,128)(2,1)S(1)} collective-permute-done((bf16[64,4096]{1,0:T(8,128)(2,1)S(1)}, bf16[64,4096]{1,0:T(8,128)(2,1)S(1)}, u32[]{:S(2)}, u32[]{:S(2)}) %collective-permute-start.11) | collective-permute-done | bytes 524320 | tf_op jit(solution)/shard_map/ppermute | solution.py:101
  102.3 1.9 %collective-permute-start.12 = (bf16[64,4096]{1,0:T(8,128)(2,1)S(1)}, bf16[64,4096]{1,0:T(8,128)(2,1)S(1)}, u32[]{:S(2)}, u32[]{:S(2)}) collective-permute-start(bf16[64,4096]{1,0:T(8,128)(2,1)S(1)} %add_convert_fusion.2), channel_id=1, source_target_pairs={{0,4},{4,0},{8,12},{12,8},{16,20},{20,16},{24,28},{28,24},{32,36},... | collective-permute-start | bytes 1572872 | tf_op jit(solution)/shard_map/ppermute | solution.py:101
  104.3 4.6 %collective-permute-start.15 = (bf16[64,4096]{1,0:T(8,128)(2,1)S(1)}, bf16[64,4096]{1,0:T(8,128)(2,1)S(1)}, u32[]{:S(2)}, u32[]{:S(2)}) collective-permute-start(bf16[64,4096]{1,0:T(8,128)(2,1)S(1)} %add_convert_fusion), channel_id=1, source_target_pairs={{0,28},{4,8},{8,4},{12,16},{16,12},{20,24},{24,20},{28,0},{32,60},... | collective-permute-start | bytes 1572872 | tf_op jit(solution)/shard_map/ppermute | solution.py:101
  109.2 0.5 fusion.25
  109.7 2.5 %collective-permute-done.12 = bf16[64,4096]{1,0:T(8,128)(2,1)S(1)} collective-permute-done((bf16[64,4096]{1,0:T(8,128)(2,1)S(1)}, bf16[64,4096]{1,0:T(8,128)(2,1)S(1)}, u32[]{:S(2)}, u32[]{:S(2)}) %collective-permute-start.12) | collective-permute-done | bytes 524320 | tf_op jit(solution)/shard_map/ppermute | solution.py:101
  112.2 3.3 %collective-permute-done.15 = bf16[64,4096]{1,0:T(8,128)(2,1)S(1)} collective-permute-done((bf16[64,4096]{1,0:T(8,128)(2,1)S(1)}, bf16[64,4096]{1,0:T(8,128)(2,1)S(1)}, u32[]{:S(2)}, u32[]{:S(2)}) %collective-permute-start.15) | collective-permute-done | bytes 524320 | tf_op jit(solution)/shard_map/ppermute | solution.py:101
  115.5 0.5 fusion.8
  116.0 15.1 %all_to_all.10 = bf16[8,8,4096]{2,1,0:T(8,128)(2,1)S(1)} all-to-all(bf16[8,8,4096]{2,1,0:T(8,128)(2,1)S(1)} %fusion.8), channel_id=1, replica_groups={{0,32,64,96,128,160,192,224},{4,36,68,100,132,164,196,228},{8,40,72,104..., dimensions={0} | all-to-all | bytes 1048576 | tf_op jit(solution)/shard_map/all_to_all | solution.py:156
  131.1 8.9 %collective-permute-start.16 = (bf16[8,4096]{1,0:T(8,128)(2,1)S(1)}, bf16[8,4096]{1,0:T(8,128)(2,1)S(1)}, u32[]{:S(2)}, u32[]{:S(2)}) collective-permute-start(bf16[8,4096]{1,0:T(8,128)(2,1)S(1)} %reduce_sum.62), channel_id=1, source_target_pairs={{0,256},{256,0},{1,257},{257,1},{2,258},{258,2},{3,259},{259,3},{4... | collective-permute-start | bytes 196616 | tf_op jit(solution)/shard_map/ppermute | solution.py:165
  140.0 0.9 collective-permute-done.16
  140.9 0.7 pad_maximum_fusion
  (37 shorter events, 1.9 us)
Async XLA Ops:
  0.0 33.3 %copy-start.1 = (bf16[1,4096,128]{2,1,0:T(8,128)(2,1)S(1)}, bf16[1,4096,128]{2,1,0:T(8,128)(2,1)}, u32[]{:S(2)}) copy-start(bf16[1,4096,128]{2,1,0:T(8,128)(2,1)} %param.9) | copy-start | bytes 3145732
  0.0 33.5 %copy-start.2 = (bf16[1,4096,128]{2,1,0:T(8,128)(2,1)S(1)}, bf16[1,4096,128]{2,1,0:T(8,128)(2,1)}, u32[]{:S(2)}) copy-start(bf16[1,4096,128]{2,1,0:T(8,128)(2,1)} %param.10) | copy-start | bytes 3145732
  2.0 23.4 %all-to-all-start = ((bf16[8,8,4224]{2,1,0:T(8,128)(2,1)}), bf16[8,8,4224]{2,1,0:T(8,128)(2,1)S(1)}, u32[]{:S(2)}, u32[]{:S(2)}) async-start(bf16[8,8,4224]{2,1,0:T(8,128)(2,1)} %bitcast.41), calls=%async_computation | async-start | bytes 1081344 | tf_op jit(solution)/shard_map/all_to_all | solution.py:95
  25.5 16.9 %collective-permute-start.2 = (bf16[64,4224]{1,0:T(8,128)(2,1)S(1)}, bf16[64,4224]{1,0:T(8,128)(2,1)S(1)}, u32[]{:S(2)}, u32[]{:S(2)}) collective-permute-start(bf16[64,4224]{1,0:T(8,128)(2,1)S(1)} %bitcast.36), channel_id=1, source_target_pairs={{0,4},{4,0},{8,12},{12,8},{16,20},{20,16},{24,28},{28,24},{32,36},... | collective-permute-start | bytes 1622024 | tf_op jit(solution)/shard_map/ppermute | solution.py:101
  28.4 15.9 %collective-permute-start.7 = (bf16[64,4224]{1,0:T(8,128)(2,1)S(1)}, bf16[64,4224]{1,0:T(8,128)(2,1)S(1)}, u32[]{:S(2)}, u32[]{:S(2)}) collective-permute-start(bf16[64,4224]{1,0:T(8,128)(2,1)S(1)} %bitcast.37), channel_id=1, source_target_pairs={{0,28},{4,8},{8,4},{12,16},{16,12},{20,24},{24,20},{28,0},{32,60},... | collective-permute-start | bytes 1622024 | tf_op jit(solution)/shard_map/ppermute | solution.py:101
  33.3 6.6 %copy-start = (bf16[1,128,4096]{2,1,0:T(8,128)(2,1)S(1)}, bf16[1,128,4096]{2,1,0:T(8,128)(2,1)}, u32[]{:S(2)}) copy-start(bf16[1,128,4096]{2,1,0:T(8,128)(2,1)} %param.11) | copy-start | bytes 3145732
  33.8 32.5 %collective-permute-start = (bf16[4096,256]{1,0:T(8,128)(2,1)S(1)}, bf16[4096,256]{1,0:T(8,128)(2,1)S(1)}, u32[]{:S(2)}, u32[]{:S(2)}) collective-permute-start(bf16[4096,256]{1,0:T(8,128)(2,1)S(1)} %constant_dynamic-update-slice_fusion), channel_id=1, source_target_pairs={{0,256},{256,0},{1,257},{257,1},{2,258},{258,2},{3,259},{259,3},{4... | collective-permute-start | bytes 6291464 | tf_op jit(solution)/shard_map/ppermute | solution.py:116
  39.9 26.8 %collective-permute-start.1 = (bf16[128,4096]{1,0:T(8,128)(2,1)S(1)}, bf16[128,4096]{1,0:T(8,128)(2,1)S(1)}, u32[]{:S(2)}, u32[]{:S(2)}) collective-permute-start(bf16[128,4096]{1,0:T(8,128)(2,1)S(1)} %bitcast.30), channel_id=1, source_target_pairs={{0,256},{256,0},{1,257},{257,1},{2,258},{258,2},{3,259},{259,3},{4... | collective-permute-start | bytes 3145736 | tf_op jit(solution)/shard_map/ppermute | solution.py:117
  42.4 11.6 %collective-permute-start.3 = (bf16[64,4224]{1,0:T(8,128)(2,1)S(1)}, bf16[64,4224]{1,0:T(8,128)(2,1)S(1)}, u32[]{:S(2)}, u32[]{:S(2)}) collective-permute-start(bf16[64,4224]{1,0:T(8,128)(2,1)S(1)} %collective-permute-done.2), channel_id=1, source_target_pairs={{0,28},{4,8},{8,4},{12,16},{16,12},{20,24},{24,20},{28,0},{32,60},... | collective-permute-start | bytes 1622024 | tf_op jit(solution)/shard_map/ppermute | solution.py:101
  44.4 11.5 %collective-permute-start.8 = (bf16[64,4224]{1,0:T(8,128)(2,1)S(1)}, bf16[64,4224]{1,0:T(8,128)(2,1)S(1)}, u32[]{:S(2)}, u32[]{:S(2)}) collective-permute-start(bf16[64,4224]{1,0:T(8,128)(2,1)S(1)} %collective-permute-done.7), channel_id=1, source_target_pairs={{0,4},{4,0},{8,12},{12,8},{16,20},{20,16},{24,28},{28,24},{32,36},... | collective-permute-start | bytes 1622024 | tf_op jit(solution)/shard_map/ppermute | solution.py:101
  54.0 10.4 %collective-permute-start.4 = (bf16[64,4224]{1,0:T(8,128)(2,1)S(1)}, bf16[64,4224]{1,0:T(8,128)(2,1)S(1)}, u32[]{:S(2)}, u32[]{:S(2)}) collective-permute-start(bf16[64,4224]{1,0:T(8,128)(2,1)S(1)} %collective-permute-done.3), channel_id=1, source_target_pairs={{0,4},{4,0},{8,12},{12,8},{16,20},{20,16},{24,28},{28,24},{32,36},... | collective-permute-start | bytes 1622024 | tf_op jit(solution)/shard_map/ppermute | solution.py:101
  55.9 12.2 %collective-permute-start.9 = (bf16[64,4224]{1,0:T(8,128)(2,1)S(1)}, bf16[64,4224]{1,0:T(8,128)(2,1)S(1)}, u32[]{:S(2)}, u32[]{:S(2)}) collective-permute-start(bf16[64,4224]{1,0:T(8,128)(2,1)S(1)} %collective-permute-done.8), channel_id=1, source_target_pairs={{0,28},{4,8},{8,4},{12,16},{16,12},{20,24},{24,20},{28,0},{32,60},... | collective-permute-start | bytes 1622024 | tf_op jit(solution)/shard_map/ppermute | solution.py:101
  64.4 12.8 %collective-permute-start.5 = (bf16[64,4224]{1,0:T(8,128)(2,1)S(1)}, bf16[64,4224]{1,0:T(8,128)(2,1)S(1)}, u32[]{:S(2)}, u32[]{:S(2)}) collective-permute-start(bf16[64,4224]{1,0:T(8,128)(2,1)S(1)} %collective-permute-done.4), channel_id=1, source_target_pairs={{0,28},{4,8},{8,4},{12,16},{16,12},{20,24},{24,20},{28,0},{32,60},... | collective-permute-start | bytes 1622024 | tf_op jit(solution)/shard_map/ppermute | solution.py:110
  70.2 12.7 %collective-permute-start.10 = (bf16[64,4096]{1,0:T(8,128)(2,1)S(1)}, bf16[64,4096]{1,0:T(8,128)(2,1)S(1)}, u32[]{:S(2)}, u32[]{:S(2)}) collective-permute-start(bf16[64,4096]{1,0:T(8,128)(2,1)S(1)} %get-tuple-element.27), channel_id=1, source_target_pairs={{0,4},{4,0},{8,12},{12,8},{16,20},{20,16},{24,28},{28,24},{32,36},... | collective-permute-start | bytes 1572872 | tf_op jit(solution)/shard_map/ppermute | solution.py:101
  72.6 12.5 %collective-permute-start.13 = (bf16[64,4096]{1,0:T(8,128)(2,1)S(1)}, bf16[64,4096]{1,0:T(8,128)(2,1)S(1)}, u32[]{:S(2)}, u32[]{:S(2)}) collective-permute-start(bf16[64,4096]{1,0:T(8,128)(2,1)S(1)} %get-tuple-element.30), channel_id=1, source_target_pairs={{0,28},{4,8},{8,4},{12,16},{16,12},{20,24},{24,20},{28,0},{32,60},... | collective-permute-start | bytes 1572872 | tf_op jit(solution)/shard_map/ppermute | solution.py:101
  78.9 30.8 %collective-permute-start.6 = (bf16[64,4096]{1,0:T(8,128)(2,1)S(1)}, bf16[64,4096]{1,0:T(8,128)(2,1)S(1)}, u32[]{:S(2)}, u32[]{:S(2)}) collective-permute-start(bf16[64,4096]{1,0:T(8,128)(2,1)S(1)} %multiply_convert_fusion), channel_id=1, source_target_pairs={{0,16},{4,20},{8,24},{12,28},{16,0},{20,4},{24,8},{28,12},{32,48},... | collective-permute-start | bytes 1572872 | tf_op jit(solution)/shard_map/ppermute | solution.py:143
  83.0 19.2 %collective-permute-start.11 = (bf16[64,4096]{1,0:T(8,128)(2,1)S(1)}, bf16[64,4096]{1,0:T(8,128)(2,1)S(1)}, u32[]{:S(2)}, u32[]{:S(2)}) collective-permute-start(bf16[64,4096]{1,0:T(8,128)(2,1)S(1)} %add_convert_fusion.3), channel_id=1, source_target_pairs={{0,28},{4,8},{8,4},{12,16},{16,12},{20,24},{24,20},{28,0},{32,60},... | collective-permute-start | bytes 1572872 | tf_op jit(solution)/shard_map/ppermute | solution.py:101
  85.2 19.0 %collective-permute-start.14 = (bf16[64,4096]{1,0:T(8,128)(2,1)S(1)}, bf16[64,4096]{1,0:T(8,128)(2,1)S(1)}, u32[]{:S(2)}, u32[]{:S(2)}) collective-permute-start(bf16[64,4096]{1,0:T(8,128)(2,1)S(1)} %add_convert_fusion.1), channel_id=1, source_target_pairs={{0,4},{4,0},{8,12},{12,8},{16,20},{20,16},{24,28},{28,24},{32,36},... | collective-permute-start | bytes 1572872 | tf_op jit(solution)/shard_map/ppermute | solution.py:101
  102.3 9.9 %collective-permute-start.12 = (bf16[64,4096]{1,0:T(8,128)(2,1)S(1)}, bf16[64,4096]{1,0:T(8,128)(2,1)S(1)}, u32[]{:S(2)}, u32[]{:S(2)}) collective-permute-start(bf16[64,4096]{1,0:T(8,128)(2,1)S(1)} %add_convert_fusion.2), channel_id=1, source_target_pairs={{0,4},{4,0},{8,12},{12,8},{16,20},{20,16},{24,28},{28,24},{32,36},... | collective-permute-start | bytes 1572872 | tf_op jit(solution)/shard_map/ppermute | solution.py:101
  104.3 11.1 %collective-permute-start.15 = (bf16[64,4096]{1,0:T(8,128)(2,1)S(1)}, bf16[64,4096]{1,0:T(8,128)(2,1)S(1)}, u32[]{:S(2)}, u32[]{:S(2)}) collective-permute-start(bf16[64,4096]{1,0:T(8,128)(2,1)S(1)} %add_convert_fusion), channel_id=1, source_target_pairs={{0,28},{4,8},{8,4},{12,16},{16,12},{20,24},{24,20},{28,0},{32,60},... | collective-permute-start | bytes 1572872 | tf_op jit(solution)/shard_map/ppermute | solution.py:101
  131.1 9.8 %collective-permute-start.16 = (bf16[8,4096]{1,0:T(8,128)(2,1)S(1)}, bf16[8,4096]{1,0:T(8,128)(2,1)S(1)}, u32[]{:S(2)}, u32[]{:S(2)}) collective-permute-start(bf16[8,4096]{1,0:T(8,128)(2,1)S(1)} %reduce_sum.62), channel_id=1, source_target_pairs={{0,256},{256,0},{1,257},{257,1},{2,258},{258,2},{3,259},{259,3},{4... | collective-permute-start | bytes 196616 | tf_op jit(solution)/shard_map/ppermute | solution.py:165
